TPU v7x, 128 devices: a whole 4x4x4 slice. The times are simulated.
128 devices in a mesh: tile: 8 (over x, core), bulk: 16 (over y, z).
Axes of the slice: x: 4, y: 4, z: 4, core: 2. Of those that a mesh axis runs over, the one named last changes fastest.
Arguments:
- coarse_now: float32 [512, 1024, 128], P('tile', 'bulk'), may hold values from -6 to 6
- coarse_before: float32 [512, 1024, 128], P('tile', 'bulk'), may hold values from -6 to 6
- coarse_courant: float32 [512, 1024, 128], P('tile', 'bulk'), may hold values from 0.05 to 0.3
- coarse_absorb: float32 [512, 1024, 128], P('tile', 'bulk'), may hold values from 0.02 to 0.3
- fine_now: float32 [256, 48, 2304], P(('tile', 'bulk')), may hold values from -6 to 6
- fine_before: float32 [256, 48, 2304], P(('tile', 'bulk')), may hold values from -6 to 6
- fine_courant: float32 [256, 48, 2304], P(('tile', 'bulk')), may hold values from 0.05 to 0.3
- fine_absorb: float32 [256, 48, 2304], P(('tile', 'bulk')), may hold values from 0.02 to 0.3
- box_anchor: int32 [256, 3], P(('tile', 'bulk')), may hold values from 0 to 1008, as said below
- intersection: int32 [128, 4, 4], P(('tile', 'bulk')), may hold values from -1 to 255, as said below
Outputs:
- coarse_next: float32 [512, 1024, 128], P('tile', 'bulk')
- coarse_last: float32 [512, 1024, 128], P('tile', 'bulk')
- fine_next: float32 [256, 48, 2304], P(('tile', 'bulk'))
- fine_last: float32 [256, 48, 2304], P(('tile', 'bulk'))
Inputs may be any that keep to these rules, and one draw needn't show every extreme that they name: `box_anchor`: box b is held in the box order of the fine arrays, by device d = b // 2; its region of 16 coarse cells along each dimension from its anchor lies inside the coarse block of device d, d XOR 1, d XOR h or d XOR h XOR 1, where h is half the number of devices; anchors are multiples of 16, and no two regions share a cell. `intersection`: row 0 lists each box exactly once, in the block of the device whose coarse cells hold its region, -1 in unused entries; rows 1 to 3 give that region's first cell relative to the block (0 in unused entries), matching box_anchor. Some block holds exactly 4 boxes.
All inputs are finite; a program needn't handle non-finite values.
Results may differ from a plain program's by a relative error of at most 0.0001.
Values sent between devices are 32-bit elements; how exact they have to be, the bound alone decides.
No kernel may reach another device: no remote copies, remote signals or barrier semaphores. Data moves between devices by JAX's collectives and lax.ppermute only.
A program may use at most 512 MiB of HBM per device.

v0:
```python
import jax
import jax.numpy as jnp
from jax import lax
from jax.sharding import PartitionSpec as P

STEPS = 2


exact = lax.Precision.HIGHEST


def extended(array, sides, width):
    for axis, dim in sides:
        size, length = (lax.axis_size(axis), array.shape[dim])
        up = [(i, (i + 1) % size) for i in range(size - 1)]
        down = [(j, i) for i, j in up]
        last = lax.slice_in_dim(array, length - width, length, axis=dim)
        first = lax.slice_in_dim(array, 0, width, axis=dim)
        before = lax.ppermute(last, axis, up)
        after = lax.ppermute(first, axis, down)
        array = jnp.concatenate([before, array, after], axis=dim)
    return array


def fine_update(field, before, courant, absorb, ghosts):
    xm = jnp.concatenate([ghosts[0][None], field[:-1]], 0)
    xp = jnp.concatenate([field[1:], ghosts[1][None]], 0)
    ym = jnp.concatenate([ghosts[2][:, None, :], field[:, :-1]], 1)
    yp = jnp.concatenate([field[:, 1:], ghosts[3][:, None, :]], 1)
    zm = jnp.concatenate([ghosts[4][:, :, None], field[:, :, :-1]], 2)
    zp = jnp.concatenate([field[:, :, 1:], ghosts[5][:, :, None]], 2)
    lap = xm + xp + ym + yp + zm + zp - 6.0 * field
    return (2.0 * field - (1.0 - absorb) * before + courant * lap) / (1.0 + absorb)


def upsample(faces):
    return jnp.repeat(jnp.repeat(faces, 3, axis=-2), 3, axis=-1)


def coarse_update(padded, now, before, courant, absorb):
    centre = padded[1:-1, 1:-1, 1:-1]
    beside = padded[2:, 1:-1, 1:-1] + padded[:-2, 1:-1, 1:-1]
    beside = beside + padded[1:-1, 2:, 1:-1] + padded[1:-1, :-2, 1:-1]
    beside = beside + padded[1:-1, 1:-1, 2:] + padded[1:-1, 1:-1, :-2]
    lap = beside - 6.0 * centre
    return (2.0 * now - (1.0 - absorb) * before + courant * lap) / (1.0 + absorb)


def box_faces(padded, start, edge):
    cube = lax.dynamic_slice(padded, (start[0], start[1], start[2]), (edge + 2, edge + 2, edge + 2))
    inner = slice(1, edge + 1)
    return jnp.stack(
        [
            cube[0, inner, inner],
            cube[edge + 1, inner, inner],
            cube[inner, 0, inner],
            cube[inner, edge + 1, inner],
            cube[inner, inner, 0],
            cube[inner, inner, edge + 1],
        ]
    )


def old_rim(field):
    grown = extended(field, (("tile", 0), ("bulk", 1)), 1)
    return jnp.pad(grown, ((0, 0), (0, 0), (1, 1)))


def new_rim(field):
    grown = extended(field, (("tile", 0), ("bulk", 1)), 1)
    return jnp.pad(grown, ((0, 0), (0, 0), (1, 1)))


def on_device(
    coarse_now,
    coarse_before,
    coarse_courant,
    coarse_absorb,
    fine_now,
    fine_before,
    fine_courant,
    fine_absorb,
    box_anchor,
    intersection,
):
    cells_x, cells_y, depth = coarse_now.shape
    boxes_here, side, plane = fine_now.shape
    edge = side // 3
    n_bulk = lax.axis_size("bulk")
    devices = lax.axis_size("tile") * n_bulk
    slots = devices * boxes_here
    idents = intersection[0, 0]
    valid = idents >= 0
    starts = intersection[0, 1:]
    most = idents.shape[0]
    picker = (idents[:, None] == jnp.arange(slots, dtype=jnp.int32)[None, :]).astype(jnp.float32)
    source = box_anchor[:, 0] // cells_x * n_bulk + box_anchor[:, 1] // cells_y
    chooser = (source[:, None] == jnp.arange(devices, dtype=jnp.int32)[None, :]).astype(jnp.float32)
    shape = (boxes_here, side, side, side)
    fine = fine_now.reshape(shape)
    fine_prev = fine_before.reshape(shape)
    fine_c = fine_courant.reshape(shape)
    fine_a = fine_absorb.reshape(shape)
    faces_all = jax.vmap(box_faces, (None, 0, None))
    now = coarse_now
    before = coarse_before
    for step in range(STEPS):
        padded = old_rim(now)
        new = coarse_update(padded, now, before, coarse_courant, coarse_absorb)
        padded_new = new_rim(new)
        stacked = jnp.stack(
            [faces_all(padded, starts.T, edge), faces_all(padded_new, starts.T, edge)], axis=1
        )
        payload = stacked.reshape(most, 12, edge * edge)
        outgoing = jnp.einsum("ks,kpq->spq", picker, payload, precision=exact).reshape(
            devices, boxes_here, 12, edge * edge
        )
        arrived = lax.all_to_all(
            outgoing, ("tile", "bulk"), split_axis=0, concat_axis=0, tiled=True
        )
        taken = jnp.einsum("jd,djpq->jpq", chooser, arrived, precision=exact)
        taken = taken.reshape(boxes_here, 2, 6, edge, edge)
        for sub in range(3):
            weight = sub / 3.0
            ghosts = upsample(taken[:, 0] + weight * (taken[:, 1] - taken[:, 0]))
            ahead = jax.vmap(fine_update)(fine, fine_prev, fine_c, fine_a, ghosts)
            fine_prev = fine
            fine = ahead
        restricted = (
            fine.reshape(boxes_here, edge, 3, edge, 3, edge, 3)
            .mean(axis=(2, 4, 6))
            .reshape(boxes_here, edge * edge * edge)
        )
        outgoing_back = jnp.einsum("jd,jr->djr", chooser, restricted, precision=exact)
        returned = lax.all_to_all(
            outgoing_back, ("tile", "bulk"), split_axis=0, concat_axis=0, tiled=True
        )
        blocks = jnp.einsum(
            "ks,sr->kr", picker, returned.reshape(slots, edge * edge * edge), precision=exact
        )
        blocks = blocks.reshape(most, edge, edge, edge)
        for entry in range(most):
            corner = (starts[0, entry], starts[1, entry], starts[2, entry])
            current = lax.dynamic_slice(new, corner, (edge, edge, edge))
            new = lax.dynamic_update_slice(
                new, jnp.where(valid[entry], blocks[entry], current), corner
            )
        before = now
        now = new
    flat = (boxes_here, side, plane)
    return (now, before, fine.reshape(flat), fine_prev.reshape(flat))


def solution(mesh):
    in_specs = (
        P("tile", "bulk", None),
        P("tile", "bulk", None),
        P("tile", "bulk", None),
        P("tile", "bulk", None),
        P(("tile", "bulk"), None, None),
        P(("tile", "bulk"), None, None),
        P(("tile", "bulk"), None, None),
        P(("tile", "bulk"), None, None),
        P(("tile", "bulk"), None),
        P(("tile", "bulk"), None, None),
    )
    out_specs = (
        P("tile", "bulk", None),
        P("tile", "bulk", None),
        P(("tile", "bulk"), None, None),
        P(("tile", "bulk"), None, None),
    )
    return jax.shard_map(
        on_device, mesh=mesh, in_specs=in_specs, out_specs=out_specs, check_vma=False
    )
```

profile of v0, /device:TPU:0, one launch (start us, length us, event | category | flops | bytes accessed | tf_op | source)
XLA Modules:
  0.0 1465.6 jit_solution(17474779126408650114)
XLA Ops:
  23.4 15.5 %while.4 = (s32[]{:T(128)}, f32[66,66,130]{2,1,0:T(8,128)}, s32[4,3]{1,0:T(4,128)S(1)}, f32[4,18,18,18]{3,2,1,0:T(8,128)S(1)}, s32[]{:T(128)}) while((s32[]{:T(128)}, f32[66,66,130]{2,1,0:T(8,128)}, s32[4,3]{1,0:T(4,128)S(1)}, f32[4,18,18,18]{3,2,1,0:T(8,128)S(1)}, s32[]{:T(128)}) %tuple.212), condition=%wide.while_cond, body=%wide.while_body.sunk | while | flops 2 | bytes 244649 | solution.py:50
  41.0 8.5 fusion.40
  71.1 15.1 %while.5 = (s32[]{:T(128)}, f32[66,66,130]{2,1,0:T(8,128)}, s32[4,3]{1,0:T(4,128)S(1)}, f32[4,18,18,18]{3,2,1,0:T(8,128)S(1)}, s32[]{:T(128)}) while((s32[]{:T(128)}, f32[66,66,130]{2,1,0:T(8,128)}, s32[4,3]{1,0:T(4,128)S(1)}, f32[4,18,18,18]{3,2,1,0:T(8,128)S(1)}, s32[]{:T(128)}) %tuple.221), condition=%wide.while_cond.1, body=%wide.while_body.1.sunk | while | flops 2 | bytes 244649 | solution.py:50
  93.8 13.5 all-to-all-start
  110.4 38.6 %add.565 = f32[2,16,3,16,3,16,3]{6,5,4,3,2,1,0:T(8,128)} reshape(f32[2,48,2304]{2,1,0:T(8,128)S(1)} %get-tuple-element.276) | data formatting | bytes 1769472 | tf_op jit(solution)/shard_map/vmap()/add | solution.py:33
  151.9 38.7 %sub.175 = f32[2,16,3,16,3,16,3]{6,5,4,3,2,1,0:T(8,128)} reshape(f32[2,48,2304]{2,1,0:T(8,128)S(1)} %get-tuple-element.275) | data formatting | bytes 1769472 | tf_op jit(solution)/shard_map/vmap()/sub | solution.py:33
  192.1 38.7 %reshape.313 = f32[2,16,3,16,3,16,3]{6,5,4,3,2,1,0:T(8,128)} reshape(f32[2,48,2304]{2,1,0:T(8,128)S(1)} %copy-done.31) | data formatting | bytes 1769472 | tf_op jit(solution)/shard_map/reshape | solution.py:100
  234.3 39.8 %reshape.314 = f32[2,16,3,16,3,16,3]{6,5,4,3,2,1,0:T(8,128)} reshape(f32[2,48,2304]{2,1,0:T(8,128)} %param.15) | data formatting | bytes 1769472 | tf_op jit(solution)/shard_map/reshape | solution.py:101
  276.9 38.7 %reshape.315 = f32[2,16,3,16,3,16,3]{6,5,4,3,2,1,0:T(8,128)} reshape(f32[2,48,2304]{2,1,0:T(8,128)S(1)} %copy-done.29) | data formatting | bytes 1769472 | tf_op jit(solution)/shard_map/reshape | solution.py:102
  316.6 33.0 %copy.518 = f32[2,16,3,16,3,16,3]{5,3,6,4,2,1,0:T(8,128)} copy(f32[2,16,3,16,3,16,3]{6,5,4,3,2,1,0:T(8,128)} %add.565) | data formatting | bytes 1769472 | tf_op jit(solution)/shard_map/vmap()/add | solution.py:33
  349.5 32.9 %copy.489 = f32[2,16,3,16,3,16,3]{5,3,6,4,2,1,0:T(8,128)} copy(f32[2,16,3,16,3,16,3]{6,5,4,3,2,1,0:T(8,128)} %sub.175) | data formatting | bytes 1769472 | tf_op jit(solution)/shard_map/vmap()/sub | solution.py:33
  382.4 32.9 %copy.488 = f32[2,16,3,16,3,16,3]{5,3,6,4,2,1,0:T(8,128)} copy(f32[2,16,3,16,3,16,3]{6,5,4,3,2,1,0:T(8,128)} %reshape.313) | data formatting | bytes 1769472 | tf_op jit(solution)/shard_map/reshape | solution.py:100
  415.3 32.9 %copy.490 = f32[2,16,3,16,3,16,3]{5,3,6,4,2,1,0:T(8,128)} copy(f32[2,16,3,16,3,16,3]{6,5,4,3,2,1,0:T(8,128)} %reshape.314) | data formatting | bytes 1769472 | tf_op jit(solution)/shard_map/reshape | solution.py:101
  448.3 33.1 %copy.517 = f32[2,16,3,16,3,16,3]{5,3,6,4,2,1,0:T(8,128)} copy(f32[2,16,3,16,3,16,3]{6,5,4,3,2,1,0:T(8,128)} %reshape.315) | data formatting | bytes 1769472 | tf_op jit(solution)/shard_map/reshape | solution.py:102
  498.7 15.7 %add_divide_fusion.8 = (f32[2,48,48,48]{3,2,1,0:T(8,128)S(1)}, f32[2,48,48,48]{3,2,1,0:T(8,128)}, f32[2,48,48,48]{3,2,1,0:T(8,128)}, f32[2,48,48,48]{3,2,1,0:T(8...) fusion(f32[2,48,48,48]{3,2,1,0:T(8,128)} %add.569, f32[2,48,48,48]{3,2,1,0:T(8,128)} %reshape.324, ...), kind=kLoop, calls=%fused_computation.94 | loop fusion | flops 4202496 | bytes 15040512 | tf_op jit(solution)/shard_map/vmap()/div | solution.py:33
  527.9 15.4 %add_divide_fusion.7 = (f32[2,48,48,48]{3,2,1,0:T(8,128)S(1)}, f32[2,48,48,48]{3,2,1,0:T(8,128)}, f32[2,48,48,48]{3,2,1,0:T(8,128)}, f32[2,48,48,48]{3,2,1,0:T(8...) fusion(f32[2,48,48,48]{3,2,1,0:T(8,128)} %add.569, f32[2,48,48,48]{3,2,1,0:T(8,128)} %reshape.324, ...), kind=kLoop, calls=%fused_computation.93 | loop fusion | flops 4202496 | bytes 15040512 | tf_op jit(solution)/shard_map/vmap()/div | solution.py:33
  557.0 15.6 %add_divide_fusion.6 = (f32[2,48,48,48]{3,2,1,0:T(8,128)S(1)}, f32[2,48,48,48]{3,2,1,0:T(8,128)}, f32[2,48,48,48]{3,2,1,0:T(8,128)}, f32[2,48,48,48]{3,2,1,0:T(8...) fusion(f32[2,48,48,48]{3,2,1,0:T(8,128)} %add.569, f32[2,48,48,48]{3,2,1,0:T(8,128)} %reshape.324, ...), kind=kLoop, calls=%fused_computation.92 | loop fusion | flops 4202496 | bytes 15040512 | tf_op jit(solution)/shard_map/vmap()/div | solution.py:33
  572.6 24.5 %reshape.431 = f32[2,16,3,16,3,16,3]{6,5,4,3,2,1,0:T(8,128)} reshape(f32[2,48,48,48]{3,2,1,0:T(8,128)} %get-tuple-element.192) | data formatting | bytes 1769472 | tf_op jit(solution)/shard_map/vmap()/add | solution.py:32
  597.1 32.9 %copy.542 = f32[2,16,3,16,3,16,3]{5,3,6,4,2,1,0:T(8,128)} copy(f32[2,16,3,16,3,16,3]{6,5,4,3,2,1,0:T(8,128)} %reshape.431) | data formatting | bytes 1769472 | tf_op jit(solution)/shard_map/vmap()/add | solution.py:32
  630.0 24.5 %reshape.430 = f32[2,16,3,16,3,16,3]{6,5,4,3,2,1,0:T(8,128)} reshape(f32[2,48,48,48]{3,2,1,0:T(8,128)} %get-tuple-element.200) | data formatting | bytes 1769472 | tf_op jit(solution)/shard_map/vmap()/add | solution.py:32
  654.5 32.9 %copy.529 = f32[2,16,3,16,3,16,3]{5,3,6,4,2,1,0:T(8,128)} copy(f32[2,16,3,16,3,16,3]{6,5,4,3,2,1,0:T(8,128)} %reshape.430) | data formatting | bytes 1769472 | tf_op jit(solution)/shard_map/vmap()/add | solution.py:32
  687.4 24.5 %reshape.429 = f32[2,16,3,16,3,16,3]{6,5,4,3,2,1,0:T(8,128)} reshape(f32[2,48,48,48]{3,2,1,0:T(8,128)} %get-tuple-element.206) | data formatting | bytes 1769472 | tf_op jit(solution)/shard_map/vmap()/add | solution.py:32
  711.9 32.9 %copy.516 = f32[2,16,3,16,3,16,3]{5,3,6,4,2,1,0:T(8,128)} copy(f32[2,16,3,16,3,16,3]{6,5,4,3,2,1,0:T(8,128)} %reshape.429) | data formatting | bytes 1769472 | tf_op jit(solution)/shard_map/vmap()/add | solution.py:32
  744.8 22.8 %fusion.114 = (f32[2,16,16,16]{3,2,1,0:T(8,128)S(1)}, f32[2,16,3,16,3,16,3]{5,3,6,4,2,1,0:T(8,128)}) fusion(f32[2,16,3,16,3,16,3]{5,3,6,4,2,1,0:T(8,128)} %copy.518, f32[2,16,3,16,3,16,3]{5,3,6,4,2,1,0:T(8,128)} %copy.517, f32[2,16,3,16,3,16,3]{5,3,6,4,2,1,0:T(8,128)} %copy.542, f32[2,16,3,16,3,16,3]{5,3,6,4,2,1,0:T(8,128)} %copy.489, ...), kind=kLoop, calls=%fused_computation.335 | loop fusion | flops 5521408 | bytes 7995392 | tf_op jit(solution)/shard_map/reduce_sum | solution.py:131
  771.9 10.4 all-to-all-start.1
  807.5 26.9 %all-to-all-done.1 = f32[128,2,4096]{2,1,0:T(2,128)} async-done(((f32[128,2,4096]{2,1,0:T(2,128)}), f32[128,2,4096]{2,1,0:T(2,128)}, u32[]{:S(2)}, u32[]{:S(2)}) %all-to-all-start.1) | async-done | bytes 4194336 | tf_op jit(solution)/shard_map/all_to_all | solution.py:135
  834.4 6.0 reshape.327
  846.3 5.9 dynamic_update_slice.24
  853.9 5.9 dynamic_update_slice.25
  865.7 5.9 dynamic_update_slice.27
  888.4 6.6 select_maximum_fusion.4
  895.1 15.0 %while.6 = (s32[]{:T(128)}, f32[66,66,130]{2,1,0:T(8,128)}, s32[4,3]{1,0:T(4,128)S(1)}, f32[4,18,18,18]{3,2,1,0:T(8,128)S(1)}, s32[]{:T(128)}) while((s32[]{:T(128)}, f32[66,66,130]{2,1,0:T(8,128)}, s32[4,3]{1,0:T(4,128)S(1)}, f32[4,18,18,18]{3,2,1,0:T(8,128)S(1)}, s32[]{:T(128)}) %tuple.222), condition=%wide.while_cond.2, body=%wide.while_body.2.sunk | while | flops 2 | bytes 244649 | solution.py:50
  912.4 11.6 fusion.33
  945.7 15.1 %while.7 = (s32[]{:T(128)}, f32[66,66,130]{2,1,0:T(8,128)}, s32[4,3]{1,0:T(4,128)S(1)}, f32[4,18,18,18]{3,2,1,0:T(8,128)S(1)}, s32[]{:T(128)}) while((s32[]{:T(128)}, f32[66,66,130]{2,1,0:T(8,128)}, s32[4,3]{1,0:T(4,128)S(1)}, f32[4,18,18,18]{3,2,1,0:T(8,128)S(1)}, s32[]{:T(128)}) %tuple.223), condition=%wide.while_cond.3, body=%wide.while_body.3.sunk | while | flops 2 | bytes 244649 | solution.py:50
  975.4 11.3 all-to-all-start.2
  994.7 32.6 %all-to-all-done.2 = f32[128,2,12,256]{3,1,2,0:T(2,128)} async-done(((f32[128,2,12,256]{3,1,2,0:T(2,128)}), f32[128,2,12,256]{3,1,2,0:T(2,128)}, u32[]{:S(2)}, u32[]{:S(2)}) %all-to-all-start.2) | async-done | bytes 3145760 | tf_op jit(solution)/shard_map/all_to_all | solution.py:118
  1036.6 15.0 %add_divide_fusion.5 = (f32[2,48,48,48]{3,2,1,0:T(8,128)S(1)}, f32[2,48,48,48]{3,2,1,0:T(8,128)}, f32[2,48,48,48]{3,2,1,0:T(8,128)}, f32[2,48,48,48]{3,2,1,0:T(8...) fusion(f32[2,48,48,48]{3,2,1,0:T(8,128)} %add.569, f32[2,48,48,48]{3,2,1,0:T(8,128)} %reshape.324, ...), kind=kLoop, calls=%fused_computation.91 | loop fusion | flops 4202496 | bytes 15040512 | tf_op jit(solution)/shard_map/vmap()/div | solution.py:33
  1065.2 15.2 %add_divide_fusion.4 = (f32[2,48,48,48]{3,2,1,0:T(8,128)S(1)}, f32[2,48,48,48]{3,2,1,0:T(8,128)}, f32[2,48,48,48]{3,2,1,0:T(8,128)}, f32[2,48,48,48]{3,2,1,0:T(8...) fusion(f32[2,48,48,48]{3,2,1,0:T(8,128)} %add.569, f32[2,48,48,48]{3,2,1,0:T(8,128)} %reshape.324, ...), kind=kLoop, calls=%fused_computation.90 | loop fusion | flops 4202496 | bytes 15040512 | tf_op jit(solution)/shard_map/vmap()/div | solution.py:33
  1093.0 10.3 fusion.29
  1103.3 24.5 %reshape.434 = f32[2,16,3,16,3,16,3]{6,5,4,3,2,1,0:T(8,128)} reshape(f32[2,48,48,48]{3,2,1,0:T(8,128)} %get-tuple-element.174) | data formatting | bytes 1769472 | tf_op jit(solution)/shard_map/vmap()/add | solution.py:32
  1127.8 33.1 %copy.596 = f32[2,16,3,16,3,16,3]{5,3,6,4,2,1,0:T(8,128)} copy(f32[2,16,3,16,3,16,3]{6,5,4,3,2,1,0:T(8,128)} %reshape.434) | data formatting | bytes 1769472 | tf_op jit(solution)/shard_map/vmap()/add | solution.py:32
  1160.9 23.5 %reshape.433 = f32[2,16,3,16,3,16,3]{6,5,4,3,2,1,0:T(8,128)} reshape(f32[2,48,48,48]{3,2,1,0:T(8,128)S(1)} %copy-done.15) | data formatting | bytes 1769472 | tf_op jit(solution)/shard_map/vmap()/add | solution.py:32
  1184.4 33.1 %copy.583 = f32[2,16,3,16,3,16,3]{5,3,6,4,2,1,0:T(8,128)} copy(f32[2,16,3,16,3,16,3]{6,5,4,3,2,1,0:T(8,128)} %reshape.433) | data formatting | bytes 1769472 | tf_op jit(solution)/shard_map/vmap()/add | solution.py:32
  1217.5 23.5 %reshape.432 = f32[2,16,3,16,3,16,3]{6,5,4,3,2,1,0:T(8,128)} reshape(f32[2,48,48,48]{3,2,1,0:T(8,128)S(1)} %copy-done.14) | data formatting | bytes 1769472 | tf_op jit(solution)/shard_map/vmap()/add | solution.py:32
  1241.1 32.9 %copy.570 = f32[2,16,3,16,3,16,3]{5,3,6,4,2,1,0:T(8,128)} copy(f32[2,16,3,16,3,16,3]{6,5,4,3,2,1,0:T(8,128)} %reshape.432) | data formatting | bytes 1769472 | tf_op jit(solution)/shard_map/vmap()/add | solution.py:32
  1274.0 26.4 %fusion = f32[2,16,16,16]{3,2,1,0:T(8,128)S(1)} fusion(f32[2,16,3,16,3,16,3]{5,3,6,4,2,1,0:T(8,128)} %copy.518, f32[2,16,3,16,3,16,3]{5,3,6,4,2,1,0:T(8,128)} %copy.517, f32[2,16,3,16,3,16,3]{5,3,6,4,2,1,0:T(8,128)} %copy.596, f32[2,16,3,16,3,16,3]{5,3,6,4,2,1,0:T(8,128)} %copy.489, f32[2,16,3,16,3,16,3]{5,3,6,4,2,1,0:T(8,128)} %copy.583, ...), kind=kLoop, calls=%fused_computation.14 | loop fusion | flops 9060352 | bytes 9764864 | tf_op jit(solution)/shard_map/reduce_sum | solution.py:131
  1413.9 14.0 fusion.91
  1427.9 6.2 reshape.336
  (468 shorter events, 435.7 us)
Async XLA Ops:
  1.4 8.1 collective-permute-start
  2.7 5.0 collective-permute-start.1
  6.4 81.7 %copy-start.55 = (s32[4]{0:T(128)}, s32[4]{0:T(128)S(1)}, u32[]{:S(2)}) copy-start(s32[4]{0:T(128)S(1)} %slice_bitcast_fusion.54) | copy-start | bytes 52
  9.5 13.8 copy-start.28
  9.6 5.6 collective-permute-start.3
  13.5 6.1 collective-permute-start.2
  14.8 73.4 %copy-start.58 = (s32[128,2]{0,1:T(2,128)}, s32[128,2]{0,1:T(2,128)S(1)}, u32[]{:S(2)}) copy-start(s32[128,2]{0,1:T(2,128)S(1)} %multiply_add_fusion.6) | copy-start | bytes 3076
  49.5 21.5 %copy-start.4 = (f32[64,64,128]{2,1,0:T(8,128)}, f32[64,64,128]{2,1,0:T(8,128)S(1)}, u32[]{:S(2)}) copy-start(f32[64,64,128]{2,1,0:T(8,128)S(1)} %fusion.40) | copy-start | bytes 6291460
  49.5 4.4 collective-permute-start.4
  51.5 4.6 collective-permute-start.5
  56.2 6.3 collective-permute-start.6
  60.0 5.8 collective-permute-start.7
  93.8 13.5 copy-start.32
  93.8 395.5 %all-to-all-start = ((f32[128,2,12,256]{3,1,2,0:T(2,128)}), f32[128,2,12,256]{3,1,2,0:T(2,128)}, u32[]{:S(2)}, u32[]{:S(2)}) async-start(f32[128,2,12,256]{3,1,2,0:T(2,128)} %copy.505), calls=%async_computation | async-start | bytes 6291456 | tf_op jit(solution)/shard_map/all_to_all | solution.py:118
  151.9 38.7 %copy-start.31 = (f32[2,48,2304]{2,1,0:T(8,128)S(1)}, f32[2,48,2304]{2,1,0:T(8,128)}, u32[]{:S(2)}) copy-start(f32[2,48,2304]{2,1,0:T(8,128)} %param.14) | copy-start | bytes 2654212
  192.1 294.2 %copy-start.2 = (f32[2,48,48,48]{3,2,1,0:T(8,128)}, f32[2,48,48,48]{3,2,1,0:T(8,128)S(1)}, u32[]{:S(2)}) copy-start(f32[2,48,48,48]{3,2,1,0:T(8,128)S(1)} %reshape.320) | copy-start | bytes 2654212
  234.3 39.8 %copy-start.29 = (f32[2,48,2304]{2,1,0:T(8,128)S(1)}, f32[2,48,2304]{2,1,0:T(8,128)}, u32[]{:S(2)}) copy-start(f32[2,48,2304]{2,1,0:T(8,128)} %param.16) | copy-start | bytes 2654212
  276.9 38.7 %copy-start.60 = (s32[2,3]{1,0:T(2,128)S(1)}, s32[2,3]{1,0:T(2,128)}, u32[]{:S(2)}) copy-start(s32[2,3]{1,0:T(2,128)} %param.18) | copy-start | bytes 76
  316.6 172.7 %copy-start.53 = (pred[2,128,1,1]{1,2,3,0:T(4,128)(4,1)}, pred[2,128,1,1]{1,2,3,0:T(4,128)(4,1)S(1)}, u32[]{:S(2)}) copy-start(pred[2,128,1,1]{1,2,3,0:T(4,128)(4,1)S(1)} %copy.624) | copy-start | bytes 772
  493.6 5.1 copy-start.35
  493.6 5.1 copy-start.37
  514.3 13.6 copy-start.1
  543.3 5.3 copy-start
  744.8 23.0 %copy-start.33 = (f32[2,128]{0,1:T(8,128)S(1)}, f32[2,128]{0,1:T(8,128)}, u32[]{:S(2)}) copy-start(f32[2,128]{0,1:T(8,128)} %get-tuple-element.341) | copy-start | bytes 3076
  771.9 10.4 copy-start.52
  771.9 62.5 %all-to-all-start.1 = ((f32[128,2,4096]{2,1,0:T(2,128)}), f32[128,2,4096]{2,1,0:T(2,128)}, u32[]{:S(2)}, u32[]{:S(2)}) async-start(f32[128,2,4096]{2,1,0:T(2,128)} %multiply_bitcast_fusion.1), calls=%async_computation.1 | async-start | bytes 8388608 | tf_op jit(solution)/shard_map/all_to_all | solution.py:135
  807.5 32.9 %copy-start.56 = (s32[4]{0:T(128)S(1)}, s32[4]{0:T(128)}, u32[]{:S(2)}) copy-start(s32[4]{0:T(128)} %copy-done.55) | copy-start | bytes 52
  872.4 2.6 collective-permute-start.9
  873.7 3.1 collective-permute-start.8
  877.9 6.3 collective-permute-start.11
  882.6 5.8 collective-permute-start.10
  883.9 11.2 copy-start.62
  888.4 6.6 copy-start.51
  924.0 16.3 %copy-start.5 = (f32[64,64,128]{2,1,0:T(8,128)}, f32[64,64,128]{2,1,0:T(8,128)S(1)}, u32[]{:S(2)}) copy-start(f32[64,64,128]{2,1,0:T(8,128)S(1)} %fusion.33) | copy-start | bytes 6291460
  924.0 4.9 collective-permute-start.12
  926.8 4.0 collective-permute-start.13
  930.8 5.9 collective-permute-start.14
  934.5 5.8 collective-permute-start.15
  961.5 8.3 copy-start.59
  975.4 51.9 %all-to-all-start.2 = ((f32[128,2,12,256]{3,1,2,0:T(2,128)}), f32[128,2,12,256]{3,1,2,0:T(2,128)}, u32[]{:S(2)}, u32[]{:S(2)}) async-start(f32[128,2,12,256]{3,1,2,0:T(2,128)} %copy.560), calls=%async_computation.2 | async-start | bytes 6291456 | tf_op jit(solution)/shard_map/all_to_all | solution.py:118
  991.8 35.5 %copy-start.54 = (pred[2,128,1,1]{1,2,3,0:T(4,128)(4,1)S(1)}, pred[2,128,1,1]{1,2,3,0:T(4,128)(4,1)}, u32[]{:S(2)}) copy-start(pred[2,128,1,1]{1,2,3,0:T(4,128)(4,1)} %copy-done.53) | copy-start | bytes 772
  1051.6 5.3 copy-start.3
  1082.2 10.9 copy-start.11
  1127.8 33.1 %copy-start.15 = (f32[2,48,48,48]{3,2,1,0:T(8,128)S(1)}, f32[2,48,48,48]{3,2,1,0:T(8,128)}, u32[]{:S(2)}) copy-start(f32[2,48,48,48]{3,2,1,0:T(8,128)} %get-tuple-element.180) | copy-start | bytes 2654212
  1184.4 33.1 %copy-start.14 = (f32[2,48,48,48]{3,2,1,0:T(8,128)S(1)}, f32[2,48,48,48]{3,2,1,0:T(8,128)}, u32[]{:S(2)}) copy-start(f32[2,48,48,48]{3,2,1,0:T(8,128)} %get-tuple-element.186) | copy-start | bytes 2654212
  1274.0 26.7 %copy-start.34 = (f32[2,128]{0,1:T(8,128)S(1)}, f32[2,128]{0,1:T(8,128)}, u32[]{:S(2)}) copy-start(f32[2,128]{0,1:T(8,128)} %get-tuple-element.341) | copy-start | bytes 3076
  1304.7 123.2 %all-to-all-start.3 = ((f32[128,2,4096]{2,1,0:T(2,128)}), f32[128,2,4096]{2,1,0:T(2,128)}, u32[]{:S(2)}, u32[]{:S(2)}) async-start(f32[128,2,4096]{2,1,0:T(2,128)} %multiply_bitcast_fusion), calls=%async_computation.3 | async-start | bytes 8388608 | tf_op jit(solution)/shard_map/all_to_all | solution.py:135
  1427.9 6.2 copy-start.57
  (35 other events, 121.4 us)
where the time goes:
time: 1480 us; the launch traced here: 1470 us
  local copies, waits for them, and re-layouts  1050 us (71%)
  other arithmetic  217 us (15%)
  waiting for transfers between devices  81.5 us (6%)
  starting transfers between devices  76.9 us (5%)
  between operations  25.5 us (2%)
  matrix products  17.7 us (1%)
    add x12, local copies, waits for them, and re-layouts, fine_update(): lap = xm + xp + ym + yp + zm + zp - 6.0 * field  343 us
    div x6, other arithmetic, fine_update(): (2.0 * field - (1.0 - absorb) * before + courant * lap) / (1.0 + absorb)  90.9 us
    reshape x3, local copies, waits for them, and re-layouts, on_device(): fine_prev = fine_before.reshape(shape)  76.2 us
    reshape x3, local copies, waits for them, and re-layouts, on_device(): fine_c = fine_courant.reshape(shape)  74.6 us
    add x3, local copies, waits for them, and re-layouts, fine_update(): 1.0 + absorb  74.6 us
    sub x3, local copies, waits for them, and re-layouts, fine_update(): 1.0 - absorb  74.5 us
    reshape x3, local copies, waits for them, and re-layouts, on_device(): fine = fine_now.reshape(shape)  73 us
    gather x48, local copies, waits for them, and re-layouts  60.2 us
  transfers between devices with their start and end apart: 20, of which 11 were waited for; matrix products, arithmetic and copies ran while one was open for 35% of the time, Pallas kernels for 0%

commit v1 on v0

v1 whole, which is shorter than its diff:
```python
import functools

import jax
import jax.numpy as jnp
import numpy as np
from jax import lax
from jax.experimental import pallas as pl
from jax.experimental.pallas import tpu as pltpu
from jax.sharding import PartitionSpec as P

CX = 64
CY = 64
NZ = 128
BC = 16
FINE = 48
PLANE = FINE * FINE
MOST = 4
F32 = jnp.float32
BF16 = jnp.bfloat16
ANY = pl.BlockSpec(memory_space=pl.ANY)
VMEM = pl.BlockSpec(memory_space=pltpu.VMEM)
SMEM = pl.BlockSpec(memory_space=pltpu.SMEM)
LIMIT = 56 * 1024 * 1024


def tables():
    flat = np.arange(PLANE)
    y, z = flat // FINE, flat % FINE
    masks = np.stack([y > 0, y < FINE - 1, z > 0, z < FINE - 1]).astype(np.float32)
    masks = np.repeat(masks[:, None, :], 8, axis=1)
    r = np.arange(BC)[:, None]
    spread = np.zeros((128, PLANE), np.float32)
    spread[0:16] = (y == 0) & (z // 3 == r)
    spread[16:32] = (y == FINE - 1) & (z // 3 == r)
    spread[32:48] = (z == 0) & (y // 3 == r)
    spread[48:64] = (z == FINE - 1) & (y // 3 == r)
    spread[64:80] = z // 3 == r
    spread[80:96] = z // 3 == r
    spread = np.concatenate([spread, spread], axis=0)
    pick = (y // 3 == r).astype(np.float32)
    pool = ((y // 3 * BC + z // 3)[:, None] == np.arange(BC * BC)[None, :]).astype(np.float32)
    return jnp.asarray(masks), jnp.asarray(spread, BF16), jnp.asarray(pick), jnp.asarray(pool, BF16)


def partner_of(meta, device):
    away = (meta[22] * 16 + meta[23]) ^ device
    return (away & 1) + 2 * ((away >> 6) & 1)


def split(value):
    high = value.astype(BF16)
    low = (value - high.astype(F32)).astype(BF16)
    return high, low


def dot(left, right):
    return jnp.dot(left, right, preferred_element_type=F32)


def edges_kernel(p, q, c, a, xup, xdn, yup, ydn, tiles, sem):
    copies = []
    for n, ref in enumerate((p, q, c, a)):
        if n == 0:
            copies.append((ref.at[CX - 2 : CX], xup.at[0:2]))
            copies.append((ref.at[0:2], xdn.at[0:2]))
        else:
            copies.append((ref.at[CX - 1], xup.at[n + 1]))
            copies.append((ref.at[0], xdn.at[n + 1]))
        copies.append((ref.at[:, CY - 8 : CY, :], tiles.at[0, n]))
        copies.append((ref.at[:, 0:8, :], tiles.at[1, n]))
    copies = [pltpu.make_async_copy(*ends, sem.at[n]) for n, ends in enumerate(copies)]
    for copy in copies:
        copy.start()
    for copy in copies:
        copy.wait()
    yup[0:64, :] = tiles[0, 0, :, 6, :]
    yup[64:128, :] = tiles[0, 0, :, 7, :]
    ydn[0:64, :] = tiles[1, 0, :, 0, :]
    ydn[64:128, :] = tiles[1, 0, :, 1, :]
    for n in range(1, 4):
        yup[64 * (n + 1) : 64 * (n + 2), :] = tiles[0, n, :, 7, :]
        ydn[64 * (n + 1) : 64 * (n + 2), :] = tiles[1, n, :, 0, :]
    yup[320:328, :] = jnp.zeros((8, 128), F32)
    ydn[320:328, :] = jnp.zeros((8, 128), F32)


def edges(p, q, c, a):
    x = jax.ShapeDtypeStruct((5, CY, NZ), F32)
    y = jax.ShapeDtypeStruct((5 * CX + 8, NZ), F32)
    return pl.pallas_call(
        edges_kernel,
        out_shape=(x, x, y, y),
        in_specs=[ANY] * 4,
        out_specs=[VMEM] * 4,
        scratch_shapes=[pltpu.VMEM((2, 4, CX, 8, NZ), F32), pltpu.SemaphoreType.DMA((16,))],
        compiler_params=pltpu.CompilerParams(vmem_limit_bytes=LIMIT),
        name="edges",
    )(p, q, c, a)


def corners_kernel(base, meta, yup, ydn, xlo, xhi, yup_out, ydn_out, rows, sem):
    lo = meta[22] > 0
    hi = meta[22] < 7
    for n, y in ((0, CY - 1), (1, 0)):
        rows[n, 0:1, :] = jnp.where(lo, xlo[1, y : y + 1, :], 0.0)
        rows[n, 1:2, :] = jnp.where(hi, xhi[0, y : y + 1, :], 0.0)
    copies = [
        pltpu.make_async_copy(rows.at[0], yup_out.at[base : base + 8, :], sem.at[0]),
        pltpu.make_async_copy(rows.at[1], ydn_out.at[base : base + 8, :], sem.at[1]),
    ]
    for copy in copies:
        copy.start()
    for copy in copies:
        copy.wait()


def corners(meta, yup, ydn, xlo, xhi):
    base = yup.shape[0] - 8
    y = jax.ShapeDtypeStruct(yup.shape, F32)
    return pl.pallas_call(
        functools.partial(corners_kernel, base),
        out_shape=(y, y),
        in_specs=[SMEM, ANY, ANY, VMEM, VMEM],
        out_specs=[ANY, ANY],
        input_output_aliases={1: 0, 2: 1},
        scratch_shapes=[pltpu.VMEM((2, 8, NZ), F32), pltpu.SemaphoreType.DMA((2,))],
        compiler_params=pltpu.CompilerParams(vmem_limit_bytes=LIMIT),
        name="corners",
    )(meta, yup, ydn, xlo, xhi)


def coarse_kernel(
    first,
    meta,
    p,
    q,
    c,
    a,
    pxlo,
    pxhi,
    pylo,
    pyhi,
    exlo,
    exhi,
    eylo,
    eyhi,
    new_out,
    face0,
    face1,
    face2,
    face3,
    pe,
    ne,
    ring,
    faces,
    sem,
):
    load = pltpu.make_async_copy(p, pe.at[2 : CX + 2, 8 : CY + 8, :], sem.at[0])
    load.start()
    tile, bulk = meta[22], meta[23]
    has = {"xl": tile > 0, "xh": tile < 7, "yl": bulk > 0, "yh": bulk < 15}
    base = pylo.shape[0] - 8
    qlo, qhi = (2, 2) if first else (1, 0)

    def keep(side, value):
        return jnp.where(has[side], value, 0.0)

    pe[0, 8 : CY + 8, :] = keep("xl", pxlo[0])
    pe[1, 8 : CY + 8, :] = keep("xl", pxlo[1])
    pe[CX + 2, 8 : CY + 8, :] = keep("xh", pxhi[0])
    pe[CX + 3, 8 : CY + 8, :] = keep("xh", pxhi[1])
    lo_edge = keep("yl", pylo[64:128, :])
    hi_edge = keep("yh", pyhi[0:64, :])
    pe[2 : CX + 2, 7:8, :] = lo_edge[:, None, :]
    pe[2 : CX + 2, CY + 8 : CY + 9, :] = hi_edge[:, None, :]
    pe[1, 7:8, :] = keep("yl", pylo[base : base + 1, :])
    pe[CX + 2, 7:8, :] = keep("yl", pylo[base + 1 : base + 2, :])
    pe[1, CY + 8 : CY + 9, :] = keep("yh", pyhi[base : base + 1, :])
    pe[CX + 2, CY + 8 : CY + 9, :] = keep("yh", pyhi[base + 1 : base + 2, :])
    load.wait()

    lane = lax.broadcasted_iota(jnp.int32, (64, NZ), 1)
    inner_lo, inner_hi = lane > 0, lane < NZ - 1

    def along_z(here):
        return jnp.where(inner_lo, pltpu.roll(here, 1, 1), 0.0) + jnp.where(
            inner_hi, pltpu.roll(here, NZ - 1, 1), 0.0
        )

    def step(here, beside, before, courant, absorb):
        inv = 1.0 / (1.0 + absorb)
        return before + (2.0 * inv) * (here - before) + (courant * inv) * (beside - 6.0 * here)

    def row(i, before, courant, absorb):
        here = pe[i, 8 : CY + 8, :]
        beside = pe[i - 1, 8 : CY + 8, :] + pe[i + 1, 8 : CY + 8, :]
        beside = beside + pe[i, 7 : CY + 7, :] + pe[i, 9 : CY + 9, :] + along_z(here)
        return step(here, beside, before, courant, absorb)

    def body(x, carry):
        ne[x + 1, 8 : CY + 8, :] = row(x + 2, q[x], c[x], a[x])
        return carry

    lax.fori_loop(0, CX, body, 0, unroll=2)
    store = pltpu.make_async_copy(ne.at[1 : CX + 1, 8 : CY + 8, :], new_out, sem.at[1])
    store.start()

    ne[0, 8 : CY + 8, :] = row(1, keep("xl", exlo[qlo]), keep("xl", exlo[3]), keep("xl", exlo[4]))
    ne[CX + 1, 8 : CY + 8, :] = row(
        CX + 2, keep("xh", exhi[qhi]), keep("xh", exhi[3]), keep("xh", exhi[4])
    )

    def side(name, here, out, inside, first_corner, last_corner, extra, at_q):
        ring[7:8, :] = keep(name, first_corner)
        ring[8:72, :] = here
        ring[72:73, :] = keep(name, last_corner)
        beside = ring[7:71, :] + ring[9:73, :] + out + inside + along_z(here)
        part = [keep(name, extra[64 * n : 64 * n + 64, :]) for n in (at_q, 3, 4)]
        return step(here, beside, *part)

    inside = pe[2 : CX + 2, 8, :]
    out = keep("yl", pylo[0:64, :])
    value = side(
        "yl", lo_edge, out, inside, pylo[base : base + 1, :], pylo[base + 1 : base + 2, :], eylo, qlo
    )
    ne[1 : CX + 1, 7:8, :] = value[:, None, :]
    inside = pe[2 : CX + 2, CY + 7, :]
    out = keep("yh", pyhi[64:128, :])
    value = side(
        "yh", hi_edge, out, inside, pyhi[base : base + 1, :], pyhi[base + 1 : base + 2, :], eyhi, qhi
    )
    ne[1 : CX + 1, CY + 8 : CY + 9, :] = value[:, None, :]

    from_z = lax.broadcasted_iota(jnp.int32, (NZ, NZ), 0)
    to_lane = lax.broadcasted_iota(jnp.int32, (NZ, NZ), 1)
    out_lane = lax.broadcasted_iota(jnp.int32, (BC, NZ), 1)
    deep_lane = lax.broadcasted_iota(jnp.int32, (BC, BC, NZ), 2)
    deep_y = lax.broadcasted_iota(jnp.int32, (BC, BC, NZ), 1)
    diagonal = (deep_lane & 15) == deep_y

    def entry(k, carry):
        ident = meta[k]

        @pl.when(ident >= 0)
        def _():
            ox = meta[4 + k]
            oy = pl.multiple_of(meta[8 + k], 16)
            oz = meta[12 + k]
            where_to = partner_of(meta, ident >> 1) * 2 + (ident & 1)
            low_face = (to_lane >= 32) & (to_lane < 48)
            high_face = (to_lane >= 48) & (to_lane < 64)
            source = jnp.where(
                low_face, oz - 1, jnp.where(high_face, oz + BC, oz + (to_lane & 15))
            )
            mover = jnp.where(from_z == source, 1.0, 0.0).astype(BF16)
            mover = jnp.concatenate([mover, mover], axis=0)
            for t, (ref, off) in enumerate(((pe, 2), (ne, 1))):
                cube = ref[pl.ds(ox + off, BC), pl.ds(oy + 8, BC), :].reshape(BC * BC, NZ)
                ym = ref[pl.ds(ox + off, BC), pl.ds(oy, 8), :][:, 7, :]
                yp = ref[pl.ds(ox + off, BC), pl.ds(oy + 8 + BC, 8), :][:, 0, :]
                xm = ref[ox + off - 1, pl.ds(oy + 8, BC), :]
                xp = ref[ox + off + BC, pl.ds(oy + 8, BC), :]
                high, low = split(jnp.concatenate([cube, ym, yp, xm, xp], axis=0))
                moved = dot(jnp.concatenate([high, low], axis=1), mover)
                z_face = jnp.where(diagonal, moved[0:256].reshape(BC, BC, NZ), 0.0).sum(axis=1)
                tile_ = jnp.where(out_lane < 80, moved[288:304], moved[304:320])
                tile_ = jnp.where(out_lane < 64, z_face, tile_)
                tile_ = jnp.where(out_lane < 32, moved[272:288], tile_)
                tile_ = jnp.where(out_lane < 16, moved[256:272], tile_)
                faces[where_to, t] = tile_

        return carry

    lax.fori_loop(0, MOST, entry, 0)
    for n, ref in enumerate((face0, face1, face2, face3)):
        ref[...] = faces[2 * n : 2 * n + 2]
    store.wait()


def coarse(first, meta, p, q, c, a, halos, extras):
    face = jax.ShapeDtypeStruct((2, 2, BC, NZ), F32)
    return pl.pallas_call(
        functools.partial(coarse_kernel, first),
        out_shape=(jax.ShapeDtypeStruct((CX, CY, NZ), F32), face, face, face, face),
        in_specs=[SMEM, ANY] + [VMEM] * 11,
        out_specs=[ANY] + [VMEM] * 4,
        scratch_shapes=[
            pltpu.VMEM((CX + 4, CY + 16, NZ), F32),
            pltpu.VMEM((CX + 2, CY + 16, NZ), F32),
            pltpu.VMEM((80, NZ), F32),
            pltpu.VMEM((8, 2, BC, NZ), F32),
            pltpu.SemaphoreType.DMA((2,)),
        ],
        compiler_params=pltpu.CompilerParams(vmem_limit_bytes=LIMIT),
        name="coarse",
    )(meta, p, q, c, a, *halos, *extras)


def fine_kernel(
    meta,
    f,
    g,
    c,
    a,
    r0,
    r1,
    r2,
    r3,
    masks,
    spread,
    pick,
    pool,
    f_out,
    g_out,
    res,
    buf,
    two,
    cour,
    ghost,
    delta,
    xrow,
    faces,
    sem,
):
    copies = [
        pltpu.make_async_copy(f, buf.at[0, :, 8:56, :], sem.at[0]),
        pltpu.make_async_copy(g, buf.at[1, :, 8:56, :], sem.at[1]),
    ]
    for copy in copies:
        copy.start()
    for n, ref in enumerate((r0, r1, r2, r3)):
        faces[2 * n : 2 * n + 2] = ref[...]

    lane = lax.broadcasted_iota(jnp.int32, (BC, NZ), 1)
    tall = lax.broadcasted_iota(jnp.int32, (FINE, BC), 0)
    wide = lax.broadcasted_iota(jnp.int32, (FINE, BC), 1)
    thrice = jnp.where((tall >= 3 * wide) & (tall < 3 * wide + 3), 1.0, 0.0).astype(BF16)
    for j in range(2):
        source = (meta[16 + 3 * j] >> 6) * 16 + (meta[17 + 3 * j] >> 6)
        at = partner_of(meta, source) * 2 + j
        sides, rows = [], []
        for t in range(2):
            got = faces[at, t]
            high, low = split(jnp.where(lane < 96, got, 0.0))
            both = jnp.concatenate([high, low], axis=1)
            wide_lane = jnp.concatenate([lane, lane], axis=1)
            zero = jnp.zeros_like(both)
            sides.append(dot(thrice, jnp.where(wide_lane < 64, both, zero)).astype(BF16))
            rows.append(jnp.where((wide_lane >= 64) & (wide_lane < 80), both, zero))
            rows.append(jnp.where(wide_lane >= 80, both, zero))
        spreaded = dot(jnp.concatenate(sides + rows, axis=0), spread[...])
        ghost[j] = spreaded[0:48]
        delta[j] = spreaded[48:96] - spreaded[0:48]
        for n in range(4):
            part = spreaded[96 + 16 * n : 112 + 16 * n] * pick[...]
            xrow[j, n : n + 1, :] = part.sum(axis=0, keepdims=True)
        for i in range(6):
            s = slice(8 * i, 8 * i + 8)
            inv = 1.0 / (1.0 + a[j, s, :])
            two[j, s, :] = 2.0 * inv
            cour[j, s, :] = c[j, s, :] * inv
    for copy in copies:
        copy.wait()

    tiles = PLANE // 128
    small = lax.broadcasted_iota(jnp.int32, (8, 128), 1)
    from_before = {1: small < 1, 48: small < 48}
    from_after = {1: small >= 127, 48: small >= 80}

    def substep(m, j):
        now, old = m % 2, 1 - m % 2
        weight = m / 3.0
        for n, at in ((0, 7), (1, 56)):
            first = xrow[j, n : n + 1, :]
            last = xrow[j, n + 2 : n + 3, :]
            buf[now, j, at : at + 1, :] = first + weight * (last - first)
        for i in range(6):
            s = slice(8 * i, 8 * i + 8)

            def here(k):
                return buf[now, j, 8 + 8 * i : 16 + 8 * i, 128 * k : 128 * k + 128]

            def turned(v):
                return {d: (pltpu.roll(v, d, 1), pltpu.roll(v, 128 - d, 1)) for d in (1, 48)}

            cur = here(0)
            cur_t = turned(cur)
            before_t = cur_t
            for k in range(tiles):
                ls = slice(128 * k, 128 * k + 128)
                nxt = here(k + 1) if k + 1 < tiles else cur
                nxt_t = turned(nxt) if k + 1 < tiles else cur_t
                total = (
                    buf[now, j, 7 + 8 * i : 15 + 8 * i, ls] + buf[now, j, 9 + 8 * i : 17 + 8 * i, ls]
                )
                for d, n in ((48, 0), (1, 2)):
                    down = jnp.where(from_before[d], before_t[d][0], cur_t[d][0])
                    up = jnp.where(from_after[d], nxt_t[d][1], cur_t[d][1])
                    total = total + down * masks[n, :, ls] + up * masks[n + 1, :, ls]
                edge = ghost[j, s, ls]
                if m > 0:
                    edge = edge + weight * delta[j, s, ls]
                total = total + edge - 6.0 * cur
                prev = buf[old, j, 8 + 8 * i : 16 + 8 * i, ls]
                buf[old, j, 8 + 8 * i : 16 + 8 * i, ls] = (
                    prev + two[j, s, ls] * (cur - prev) + cour[j, s, ls] * total
                )
                before_t, cur, cur_t = cur_t, nxt, nxt_t

    def box(j, carry):
        for m in range(3):
            substep(m, j)
        return carry

    lax.fori_loop(0, 2, box, 0)
    stores = [
        pltpu.make_async_copy(buf.at[1, :, 8:56, :], f_out, sem.at[0]),
        pltpu.make_async_copy(buf.at[0, :, 8:56, :], g_out, sem.at[1]),
    ]
    for copy in stores:
        copy.start()
    tall = lax.broadcasted_iota(jnp.int32, (BC, FINE), 1)
    wide = lax.broadcasted_iota(jnp.int32, (BC, FINE), 0)
    gather = jnp.where((tall >= 3 * wide) & (tall < 3 * wide + 3), 1.0, 0.0).astype(BF16)
    for j in range(2):
        high, low = split(buf[1, j, 8:56, :])
        pooled = dot(high, pool[...]) + dot(low, pool[...])
        high, low = split(pooled)
        res[j] = (dot(gather, high) + dot(gather, low)) * (1.0 / 27.0)
    for copy in stores:
        copy.wait()


def fine(meta, f, g, c, a, received, consts):
    box = jax.ShapeDtypeStruct((2, FINE, PLANE), F32)
    return pl.pallas_call(
        fine_kernel,
        out_shape=(box, box, jax.ShapeDtypeStruct((2, BC, BC * BC), F32)),
        in_specs=[SMEM, ANY, ANY] + [VMEM] * 10,
        out_specs=[ANY, ANY, VMEM],
        scratch_shapes=[
            pltpu.VMEM((2, 2, 64, PLANE), F32),
            pltpu.VMEM((2, FINE, PLANE), F32),
            pltpu.VMEM((2, FINE, PLANE), F32),
            pltpu.VMEM((2, FINE, PLANE), F32),
            pltpu.VMEM((2, FINE, PLANE), F32),
            pltpu.VMEM((2, 8, PLANE), F32),
            pltpu.VMEM((8, 2, BC, NZ), F32),
            pltpu.SemaphoreType.DMA((2,)),
        ],
        compiler_params=pltpu.CompilerParams(vmem_limit_bytes=LIMIT),
        name="fine",
    )(meta, f, g, c, a, *received, *consts)


def insert_kernel(pack, meta, new, r0, r1, r2, r3, out, *rest):
    if pack:
        xup, xdn, yup, ydn, got, sem = rest
    else:
        got, sem = rest
    load = pltpu.make_async_copy(new, out, sem)
    load.start()
    for n, ref in enumerate((r0, r1, r2, r3)):
        got[2 * n : 2 * n + 2] = ref[...]
    load.wait()
    y_of = lax.broadcasted_iota(jnp.int32, (BC, BC, BC * BC), 1)
    lane_of = lax.broadcasted_iota(jnp.int32, (BC, BC, BC * BC), 2)
    mine = (lane_of >> 4) == y_of
    from_yz = lax.broadcasted_iota(jnp.int32, (BC * BC, NZ), 0)
    to_lane = lax.broadcasted_iota(jnp.int32, (BC * BC, NZ), 1)
    lane = lax.broadcasted_iota(jnp.int32, (BC, BC, NZ), 2)

    def entry(k, carry):
        ident = meta[k]

        @pl.when(ident >= 0)
        def _():
            ox = meta[4 + k]
            oy = pl.multiple_of(meta[8 + k], 16)
            oz = meta[12 + k]
            value = got[partner_of(meta, ident >> 1) * 2 + (ident & 1)]
            full = jnp.where(mine, value[:, None, :], 0.0).reshape(BC * BC, BC * BC)
            high, low = split(full)
            mover = jnp.where(to_lane == oz + (from_yz & 15), 1.0, 0.0).astype(BF16)
            moved = (dot(high, mover) + dot(low, mover)).reshape(BC, BC, NZ)
            current = out[pl.ds(ox, BC), pl.ds(oy, BC), :]
            out[pl.ds(ox, BC), pl.ds(oy, BC), :] = jnp.where(
                (lane >= oz) & (lane < oz + BC), moved, current
            )

        return carry

    lax.fori_loop(0, MOST, entry, 0)
    if pack:
        xup[...] = out[CX - 2 : CX]
        xdn[...] = out[0:2]
        yup[0:64, :] = out[:, CY - 2, :]
        yup[64:128, :] = out[:, CY - 1, :]
        ydn[0:64, :] = out[:, 0, :]
        ydn[64:128, :] = out[:, 1, :]
        yup[128:136, :] = jnp.zeros((8, NZ), F32)
        ydn[128:136, :] = jnp.zeros((8, NZ), F32)


def insert(pack, meta, new, received):
    shapes = [jax.ShapeDtypeStruct((CX, CY, NZ), F32)]
    if pack:
        x = jax.ShapeDtypeStruct((2, CY, NZ), F32)
        y = jax.ShapeDtypeStruct((2 * CX + 8, NZ), F32)
        shapes += [x, x, y, y]
    return pl.pallas_call(
        functools.partial(insert_kernel, pack),
        out_shape=tuple(shapes),
        in_specs=[SMEM, ANY] + [VMEM] * 4,
        out_specs=[VMEM] * len(shapes),
        scratch_shapes=[pltpu.VMEM((8, BC, BC * BC), F32), pltpu.SemaphoreType.DMA],
        compiler_params=pltpu.CompilerParams(vmem_limit_bytes=LIMIT),
        name="insert",
    )(meta, new, *received)


def ring(size, by):
    return [(i, (i + by) % size) for i in range(size)]


def halo(meta, xup, xdn, yup, ydn):
    xlo = lax.ppermute(xup, "tile", ring(8, 1))
    xhi = lax.ppermute(xdn, "tile", ring(8, -1))
    yup, ydn = corners(meta, yup, ydn, xlo, xhi)
    ylo = lax.ppermute(yup, "bulk", ring(16, 1))
    yhi = lax.ppermute(ydn, "bulk", ring(16, -1))
    return xlo, xhi, ylo, yhi


def trade(values):
    done = [values[0]]
    for value, away in zip(values[1:], (1, 64, 65)):
        done.append(lax.ppermute(value, ("tile", "bulk"), [(d, d ^ away) for d in range(128)]))
    return done


def on_device(
    coarse_now,
    coarse_before,
    coarse_courant,
    coarse_absorb,
    fine_now,
    fine_before,
    fine_courant,
    fine_absorb,
    box_anchor,
    intersection,
):
    place = jnp.stack([lax.axis_index("tile"), lax.axis_index("bulk")]).astype(jnp.int32)
    meta = jnp.concatenate([intersection.reshape(16), box_anchor.reshape(6), place])
    consts = tables()
    extras = halo(meta, *edges(coarse_now, coarse_before, coarse_courant, coarse_absorb))
    halos = extras
    p, q = coarse_now, coarse_before
    f, g = fine_now, fine_before
    for step in range(2):
        new, *faces = coarse(
            step == 0, meta, p, q, coarse_courant, coarse_absorb, halos, extras
        )
        f, g, res = fine(meta, f, g, fine_courant, fine_absorb, trade(faces), consts)
        back = trade([res] * 4)
        if step == 0:
            new, *packed = insert(True, meta, new, back)
            halos = halo(meta, *packed)
        else:
            (new,) = insert(False, meta, new, back)
        p, q = new, p
    return p, q, f, g


def solution(mesh):
    grid = P("tile", "bulk", None)
    boxes = P(("tile", "bulk"), None, None)
    in_specs = (grid,) * 4 + (boxes,) * 4 + (P(("tile", "bulk"), None), boxes)
    return jax.shard_map(
        on_device, mesh=mesh, in_specs=in_specs, out_specs=(grid, grid, boxes, boxes), check_vma=False
    )
```

time: 1480 us -> 128 us (0.09)
  local copies, waits for them, and re-layouts: 1050 us -> 5.92 us
  other arithmetic: 217 us -> 0.67 us
  waiting for transfers between devices: 81.5 us -> 26.5 us
  Pallas kernels: 0 us -> 54.4 us
  starting transfers between devices: 76.9 us -> 38.3 us
  between operations: 25.5 us -> 0.96 us
  matrix products: 17.7 us -> 0 us
    add x21 -> x0, local copies, waits for them, and re-layouts: 418 us -> none  [the longest x12 343 us: fine_update(): lap = xm + xp + ym + yp + zm + zp - 6.0 * field]
    reshape x21 -> x2, local copies, waits for them, and re-layouts: 237 us -> 0.16 us  [the longest x1 0.08 us: on_device(): intersection.reshape(16)]
    div x10 -> x0, other arithmetic: 111 us -> none  [the longest x6 90.9 us: fine_update(): (2.0 * field - (1.0 - absorb) * before + courant * lap) / (1.0 + absorb)]
    concatenate x49 -> x0, local copies, waits for them, and re-layouts: 102 us -> none  [the longest x12 23 us: fine_update(): xm = jnp.concatenate([ghosts[0][None], field[:-1]], 0)]
    sub x3 -> x0, local copies, waits for them, and re-layouts: 74.5 us -> none  [fine_update(): 1.0 - absorb]
    gather x56 -> x0, local copies, waits for them, and re-layouts: 67.5 us -> none
    all_to_all x4 -> x0, waiting for transfers between devices: 59.4 us -> none  [the longest x2 32.6 us: on_device(): lax.all_to_all(outgoing, ('tile', 'bulk'), split_axis=0, concat_axis=0, t...]
    pallas_call x0 -> x9, Pallas kernels: none -> 54.4 us  [the longest x2 20.5 us: coarse(): pl.pallas_call(functools.partial(coarse_kernel, first), out_shape=(jax.Sh...]
  transfers between devices with their start and end apart: 20 -> 20, of which waited for: 11 -> 14; matrix products, arithmetic and copies ran while one was open for 35% -> 1% of each run, Pallas kernels for 0% -> 0%
where the time goes in v1:
time: 128 us; the launch traced here: 127 us
  Pallas kernels  54.4 us (42%)
  starting transfers between devices  38.3 us (30%)
  waiting for transfers between devices  26.5 us (21%)
  local copies, waits for them, and re-layouts  5.92 us (5%)
    pallas_call x2, Pallas kernels, coarse(): pl.pallas_call(functools.partial(coarse_kernel, first), out_shape=(jax.Sh...  20.5 us
    ppermute x12, starting transfers between devices, trade(): lax.ppermute(value, ('tile', 'bulk'), [(d, d ^ away) for d in range(128)])  20.3 us
    pallas_call x2, Pallas kernels, fine(): pl.pallas_call(fine_kernel, out_shape=(box, box, jax.ShapeDtypeStruct((2,...  19.5 us
    ppermute x12, waiting for transfers between devices, trade(): lax.ppermute(value, ('tile', 'bulk'), [(d, d ^ away) for d in range(128)])  14.4 us
    ppermute x2, starting transfers between devices, halo(): yhi = lax.ppermute(ydn, 'bulk', ring(16, -1))  9.98 us
    pallas_call x2, Pallas kernels, insert(): pl.pallas_call(functools.partial(insert_kernel, pack), out_shape=tuple(sh...  8.5 us
    ppermute x2, waiting for transfers between devices, halo(): ylo = lax.ppermute(yup, 'bulk', ring(16, 1))  7.42 us
    ppermute x2, starting transfers between devices, halo(): xhi = lax.ppermute(xdn, 'tile', ring(8, -1))  5.89 us
  transfers between devices with their start and end apart: 20, of which 14 were waited for; matrix products, arithmetic and copies ran while one was open for 1% of the time, Pallas kernels for 0%

profile of v1, /device:TPU:0, one launch (start us, length us, event | category | flops | bytes accessed | tf_op | source)
XLA Modules:
  0.0 126.7 jit_solution(15980660606739554003)
XLA Ops:
  0.7 2.7 %edges.1 = (f32[5,64,128]{2,1,0:T(8,128)}, f32[5,64,128]{2,1,0:T(8,128)}, f32[328,128]{1,0:T(8,128)}, f32[328,128]{1,0:T(8,128)}) custom-call(f32[64,64,128]{2,1,0:T(8,128)} %q.5, f32[64,64,128]{2,1,0:T(8,128)} %q.4, f32[64,64,128]{2,1,0:T(8,128)} %c.8, f32[64,64,128]{2,1,0:T(8,128)} %a.8), custom_call_target="tpu_custom_call" | custom-call | tf_op jit(solution)/shard_map/edges/pallas_call | solution.py:90
  3.4 2.9 %collective-permute-start.1 = (f32[5,64,128]{2,1,0:T(8,128)}, f32[5,64,128]{2,1,0:T(8,128)S(1)}, u32[]{:S(2)}, u32[]{:S(2)}) collective-permute-start(f32[5,64,128]{2,1,0:T(8,128)} %get-tuple-element.34), channel_id=1, source_target_pairs={{0,112},{16,0},{32,16},{48,32},{64,48},{80,64},{96,80},{112,96},{1... | collective-permute-start | bytes 491528 | tf_op jit(solution)/shard_map/ppermute | solution.py:528
  6.5 0.7 pad_add_fusion.meta
  7.2 2.4 %collective-permute-done.xlo.pxlo.exlo = f32[5,64,128]{2,1,0:T(8,128)S(1)} collective-permute-done((f32[5,64,128]{2,1,0:T(8,128)}, f32[5,64,128]{2,1,0:T(8,128)S(1)}, u32[]{:S(2)}, u32[]{:S(2)}) %collective-permute-start) | collective-permute-done | bytes 163872 | tf_op jit(solution)/shard_map/ppermute | solution.py:527
  9.6 0.7 copy-done
  10.3 1.6 %corners.2 = (f32[328,128]{1,0:T(8,128)}, f32[328,128]{1,0:T(8,128)}) custom-call(s32[24]{0:T(128)} %pad_add_fusion.meta, f32[328,128]{1,0:T(8,128)} %get-tuple-element.35.yup, f32[328,128]{1,0:T(8,128)} %get-tuple-element.36.ydn, f32[5,64,128]{2,1,0:T(8,128)} %copy-done, f32[5,64,128]{2,1,0:T(8,128)} %copy-done.1), custom_call_target="tpu_custom_call", output_to_operand_aliasing={{0}: (1, {}), {1}: (2, {})} | custom-call | tf_op jit(solution)/shard_map/corners/pallas_call | solution.py:120
  11.9 2.1 %collective-permute-start.2 = (f32[328,128]{1,0:T(8,128)}, f32[328,128]{1,0:T(8,128)S(1)}, u32[]{:S(2)}, u32[]{:S(2)}) collective-permute-start(f32[328,128]{1,0:T(8,128)} %get-tuple-element.37), channel_id=1, source_target_pairs={{0,1},{1,2},{2,3},{3,4},{4,5},{5,6},{6,7},{7,8},{8,9},{9,10},{10,1... | collective-permute-start | bytes 503816 | tf_op jit(solution)/shard_map/ppermute | solution.py:530
  14.0 4.7 %collective-permute-start.3 = (f32[328,128]{1,0:T(8,128)}, f32[328,128]{1,0:T(8,128)S(1)}, u32[]{:S(2)}, u32[]{:S(2)}) collective-permute-start(f32[328,128]{1,0:T(8,128)} %get-tuple-element.38), channel_id=1, source_target_pairs={{0,15},{1,0},{2,1},{3,2},{4,3},{5,4},{6,5},{7,6},{8,7},{9,8},{10,9... | collective-permute-start | bytes 503816 | tf_op jit(solution)/shard_map/ppermute | solution.py:531
  18.6 4.9 %collective-permute-done.2.pylo.eylo = f32[328,128]{1,0:T(8,128)S(1)} collective-permute-done((f32[328,128]{1,0:T(8,128)}, f32[328,128]{1,0:T(8,128)S(1)}, u32[]{:S(2)}, u32[]{:S(2)}) %collective-permute-start.2) | collective-permute-done | bytes 167968 | tf_op jit(solution)/shard_map/ppermute | solution.py:530
  23.6 0.7 copy-done.2
  24.2 0.7 copy-done.3
  24.9 10.3 %coarse.2 = (f32[64,64,128]{2,1,0:T(8,128)}, f32[2,2,16,128]{3,2,1,0:T(8,128)}, f32[2,2,16,128]{3,2,1,0:T(8,128)}, f32[2,2,16,128]{3,2,1,0:T(8,128)}, f32[2,2,16,128]{3,2,1,0:T(8,128)}) custom-call(s32[24]{0:T(128)} %pad_add_fusion.meta, f32[64,64,128]{2,1,0:T(8,128)} %q.5, f32[64,64,128]{2,1,0:T(8,128)} %q.4, f32[64,64,128]{2,1,0:T(8,128)} %c.8, ...), custom_call_target="tpu_custom_call" | custom-call | tf_op jit(solution)/shard_map/coarse/pallas_call | solution.py:282
  35.3 1.7 %collective-permute-start.5 = (f32[2,2,16,128]{3,2,1,0:T(8,128)}, f32[2,2,16,128]{3,2,1,0:T(8,128)S(1)}, u32[]{:S(2)}, u32[]{:S(2)}) collective-permute-start(f32[2,2,16,128]{3,2,1,0:T(8,128)} %get-tuple-element.42), channel_id=1, source_target_pairs={{0,64},{1,65},{2,66},{3,67},{4,68},{5,69},{6,70},{7,71},{8,72},{9,... | collective-permute-start | bytes 98312 | tf_op jit(solution)/shard_map/ppermute | solution.py:538
  37.0 3.3 %collective-permute-start.6 = (f32[2,2,16,128]{3,2,1,0:T(8,128)}, f32[2,2,16,128]{3,2,1,0:T(8,128)S(1)}, u32[]{:S(2)}, u32[]{:S(2)}) collective-permute-start(f32[2,2,16,128]{3,2,1,0:T(8,128)} %get-tuple-element.43), channel_id=1, source_target_pairs={{0,65},{1,64},{2,67},{3,66},{4,69},{5,68},{6,71},{7,70},{8,73},{9,... | collective-permute-start | bytes 98312 | tf_op jit(solution)/shard_map/ppermute | solution.py:538
  40.3 0.7 collective-permute-done.5.r2
  41.0 2.5 %collective-permute-done.6.r3 = f32[2,2,16,128]{3,2,1,0:T(8,128)S(1)} collective-permute-done((f32[2,2,16,128]{3,2,1,0:T(8,128)}, f32[2,2,16,128]{3,2,1,0:T(8,128)S(1)}, u32[]{:S(2)}, u32[]{:S(2)}) %collective-permute-start.6) | collective-permute-done | bytes 32800 | tf_op jit(solution)/shard_map/ppermute | solution.py:538
  43.5 0.6 copy-done.17
  44.1 9.8 %fine.2 = (f32[2,48,2304]{2,1,0:T(8,128)}, f32[2,48,2304]{2,1,0:T(8,128)}, f32[2,16,256]{2,1,0:T(8,128)}) custom-call(s32[24]{0:T(128)} %pad_add_fusion.meta, f32[2,48,2304]{2,1,0:T(8,128)} %f.1, f32[2,48,2304]{2,1,0:T(8,128)} %g.1, f32[2,48,2304]{2,1,0:T(8,128)} %c.9, f32[2,48,2304]{2,1,0:T(8,128)} %a.9, f32[2,2,16,128]{3,2,1,0:T(8,128)} %get-tuple-element.40.r0, ...), custom_call_target="tpu_custom_call" | custom-call | tf_op jit(solution)/shard_map/fine/pallas_call | solution.py:436
  53.9 3.3 %collective-permute-start.9 = (f32[2,16,256]{2,1,0:T(8,128)}, f32[2,16,256]{2,1,0:T(8,128)S(1)}, u32[]{:S(2)}, u32[]{:S(2)}) collective-permute-start(f32[2,16,256]{2,1,0:T(8,128)} %get-tuple-element.44.r0), channel_id=1, source_target_pairs={{0,65},{1,64},{2,67},{3,66},{4,69},{5,68},{6,71},{7,70},{8,73},{9,... | collective-permute-start | bytes 98312 | tf_op jit(solution)/shard_map/ppermute | solution.py:538
  57.2 1.6 %collective-permute-start.8 = (f32[2,16,256]{2,1,0:T(8,128)}, f32[2,16,256]{2,1,0:T(8,128)S(1)}, u32[]{:S(2)}, u32[]{:S(2)}) collective-permute-start(f32[2,16,256]{2,1,0:T(8,128)} %get-tuple-element.44.r0), channel_id=1, source_target_pairs={{0,64},{1,65},{2,66},{3,67},{4,68},{5,69},{6,70},{7,71},{8,72},{9,... | collective-permute-start | bytes 98312 | tf_op jit(solution)/shard_map/ppermute | solution.py:538
  58.9 0.1 collective-permute-start.7
  59.0 1.5 %collective-permute-done.9.r3 = f32[2,16,256]{2,1,0:T(8,128)S(1)} collective-permute-done((f32[2,16,256]{2,1,0:T(8,128)}, f32[2,16,256]{2,1,0:T(8,128)S(1)}, u32[]{:S(2)}, u32[]{:S(2)}) %collective-permute-start.9) | collective-permute-done | bytes 32800 | tf_op jit(solution)/shard_map/ppermute | solution.py:538
  60.5 2.4 %collective-permute-done.8.r2 = f32[2,16,256]{2,1,0:T(8,128)S(1)} collective-permute-done((f32[2,16,256]{2,1,0:T(8,128)}, f32[2,16,256]{2,1,0:T(8,128)S(1)}, u32[]{:S(2)}, u32[]{:S(2)}) %collective-permute-start.8) | collective-permute-done | bytes 32800 | tf_op jit(solution)/shard_map/ppermute | solution.py:538
  62.9 0.1 collective-permute-done.7.r1
  63.0 0.5 copy-done.13
  63.5 0.1 copy-done.16
  63.6 4.3 %insert.2 = (f32[64,64,128]{2,1,0:T(8,128)}, f32[2,64,128]{2,1,0:T(8,128)}, f32[2,64,128]{2,1,0:T(8,128)}, f32[136,128]{1,0:T(8,128)}, f32[136,128]{1,0:T(8,128)}) custom-call(s32[24]{0:T(128)} %pad_add_fusion.meta, f32[64,64,128]{2,1,0:T(8,128)} %get-tuple-element.39.new, f32[2,16,256]{2,1,0:T(8,128)} %get-tuple-element.44.r0, f32[2,16,256]{2,1,0:T(8,128)} %copy-done.16, ...), custom_call_target="tpu_custom_call" | custom-call | tf_op jit(solution)/shard_map/insert/pallas_call | solution.py:511
  67.9 2.9 %collective-permute-start.11 = (f32[2,64,128]{2,1,0:T(8,128)}, f32[2,64,128]{2,1,0:T(8,128)S(1)}, u32[]{:S(2)}, u32[]{:S(2)}) collective-permute-start(f32[2,64,128]{2,1,0:T(8,128)} %get-tuple-element.47), channel_id=1, source_target_pairs={{0,112},{16,0},{32,16},{48,32},{64,48},{80,64},{96,80},{112,96},{1... | collective-permute-start | bytes 196616 | tf_op jit(solution)/shard_map/ppermute | solution.py:528
  70.9 2.2 %collective-permute-done.10.xlo.pxlo = f32[2,64,128]{2,1,0:T(8,128)S(1)} collective-permute-done((f32[2,64,128]{2,1,0:T(8,128)}, f32[2,64,128]{2,1,0:T(8,128)S(1)}, u32[]{:S(2)}, u32[]{:S(2)}) %collective-permute-start.10) | collective-permute-done | bytes 65568 | tf_op jit(solution)/shard_map/ppermute | solution.py:527
  73.1 0.6 copy-done.4
  73.7 1.5 %corners.3 = (f32[136,128]{1,0:T(8,128)}, f32[136,128]{1,0:T(8,128)}) custom-call(s32[24]{0:T(128)} %pad_add_fusion.meta, f32[136,128]{1,0:T(8,128)} %get-tuple-element.48.yup, f32[136,128]{1,0:T(8,128)} %get-tuple-element.49.ydn, f32[2,64,128]{2,1,0:T(8,128)} %copy-done.4, f32[2,64,128]{2,1,0:T(8,128)} %copy-done.5), custom_call_target="tpu_custom_call", output_to_operand_aliasing={{0}: (1, {}), {1}: (2, {})} | custom-call | tf_op jit(solution)/shard_map/corners/pallas_call | solution.py:120
  75.3 5.3 %collective-permute-start.13 = (f32[136,128]{1,0:T(8,128)}, f32[136,128]{1,0:T(8,128)S(1)}, u32[]{:S(2)}, u32[]{:S(2)}) collective-permute-start(f32[136,128]{1,0:T(8,128)} %get-tuple-element.51), channel_id=1, source_target_pairs={{0,15},{1,0},{2,1},{3,2},{4,3},{5,4},{6,5},{7,6},{8,7},{9,8},{10,9... | collective-permute-start | bytes 208904 | tf_op jit(solution)/shard_map/ppermute | solution.py:531
  80.7 2.5 %collective-permute-done.12.pylo = f32[136,128]{1,0:T(8,128)S(1)} collective-permute-done((f32[136,128]{1,0:T(8,128)}, f32[136,128]{1,0:T(8,128)S(1)}, u32[]{:S(2)}, u32[]{:S(2)}) %collective-permute-start.12) | collective-permute-done | bytes 69664 | tf_op jit(solution)/shard_map/ppermute | solution.py:530
  83.2 0.6 copy-done.6
  83.8 10.2 %coarse.3 = (f32[64,64,128]{2,1,0:T(8,128)}, f32[2,2,16,128]{3,2,1,0:T(8,128)}, f32[2,2,16,128]{3,2,1,0:T(8,128)}, f32[2,2,16,128]{3,2,1,0:T(8,128)}, f32[2,2,16,128]{3,2,1,0:T(8,128)}) custom-call(s32[24]{0:T(128)} %pad_add_fusion.meta, f32[64,64,128]{2,1,0:T(8,128)} %get-tuple-element.30.p, f32[64,64,128]{2,1,0:T(8,128)} %q.5, f32[64,64,128]{2,1,0:T(8,128)} %c.8, ...), custom_call_target="tpu_custom_call" | custom-call | tf_op jit(solution)/shard_map/coarse/pallas_call | solution.py:282
  94.1 1.2 collective-permute-start.15
  95.3 3.8 %collective-permute-start.16 = (f32[2,2,16,128]{3,2,1,0:T(8,128)}, f32[2,2,16,128]{3,2,1,0:T(8,128)S(1)}, u32[]{:S(2)}, u32[]{:S(2)}) collective-permute-start(f32[2,2,16,128]{3,2,1,0:T(8,128)} %get-tuple-element.58), channel_id=1, source_target_pairs={{0,65},{1,64},{2,67},{3,66},{4,69},{5,68},{6,71},{7,70},{8,73},{9,... | collective-permute-start | bytes 98312 | tf_op jit(solution)/shard_map/ppermute | solution.py:538
  99.1 0.7 collective-permute-done.15.r2
  99.8 2.0 %collective-permute-done.16.r3 = f32[2,2,16,128]{3,2,1,0:T(8,128)S(1)} collective-permute-done((f32[2,2,16,128]{3,2,1,0:T(8,128)}, f32[2,2,16,128]{3,2,1,0:T(8,128)S(1)}, u32[]{:S(2)}, u32[]{:S(2)}) %collective-permute-start.16) | collective-permute-done | bytes 32800 | tf_op jit(solution)/shard_map/ppermute | solution.py:538
  101.9 0.6 copy-done.11
  102.5 9.8 %fine.3 = (f32[2,48,2304]{2,1,0:T(8,128)}, f32[2,48,2304]{2,1,0:T(8,128)}, f32[2,16,256]{2,1,0:T(8,128)}) custom-call(s32[24]{0:T(128)} %pad_add_fusion.meta, f32[2,48,2304]{2,1,0:T(8,128)} %get-tuple-element.53.f, f32[2,48,2304]{2,1,0:T(8,128)} %get-tuple-element.54.g, f32[2,48,2304]{2,1,0:T(8,128)} %c.9, f32[2,48,2304]{2,1,0:T(8,128)} %a.9, ...), custom_call_target="tpu_custom_call" | custom-call | tf_op jit(solution)/shard_map/fine/pallas_call | solution.py:436
  112.2 3.9 %collective-permute-start.19 = (f32[2,16,256]{2,1,0:T(8,128)}, f32[2,16,256]{2,1,0:T(8,128)S(1)}, u32[]{:S(2)}, u32[]{:S(2)}) collective-permute-start(f32[2,16,256]{2,1,0:T(8,128)} %get-tuple-element.59.r0), channel_id=1, source_target_pairs={{0,65},{1,64},{2,67},{3,66},{4,69},{5,68},{6,71},{7,70},{8,73},{9,... | collective-permute-start | bytes 98312 | tf_op jit(solution)/shard_map/ppermute | solution.py:538
  116.1 1.1 collective-permute-start.18
  117.2 0.1 collective-permute-start.17
  117.3 1.5 %collective-permute-done.19.r3 = f32[2,16,256]{2,1,0:T(8,128)S(1)} collective-permute-done((f32[2,16,256]{2,1,0:T(8,128)}, f32[2,16,256]{2,1,0:T(8,128)S(1)}, u32[]{:S(2)}, u32[]{:S(2)}) %collective-permute-start.19) | collective-permute-done | bytes 32800 | tf_op jit(solution)/shard_map/ppermute | solution.py:538
  118.8 2.9 %collective-permute-done.18.r2 = f32[2,16,256]{2,1,0:T(8,128)S(1)} collective-permute-done((f32[2,16,256]{2,1,0:T(8,128)}, f32[2,16,256]{2,1,0:T(8,128)S(1)}, u32[]{:S(2)}, u32[]{:S(2)}) %collective-permute-start.18) | collective-permute-done | bytes 32800 | tf_op jit(solution)/shard_map/ppermute | solution.py:538
  121.7 0.6 copy-done.18
  122.3 4.2 %insert.3 = f32[64,64,128]{2,1,0:T(8,128)} custom-call(s32[24]{0:T(128)} %pad_add_fusion.meta, f32[64,64,128]{2,1,0:T(8,128)} %get-tuple-element.52.new, f32[2,16,256]{2,1,0:T(8,128)} %get-tuple-element.59.r0, f32[2,16,256]{2,1,0:T(8,128)} %copy-done.19, f32[2,16,256]{2,1,0:T(8,128)} %copy-done.18, f32[2,16,256]{2,1,0:T(8,128)} %copy-done.15), custom_call_target="tpu_custom_call" | custom-call | tf_op jit(solution)/shard_map/insert/pallas_call | solution.py:511
  (48 shorter events, 0.7 us)
Async XLA Ops:
  0.6 5.7 %copy-start.21 = (s32[2,3]{1,0:T(2,128)S(1)}, s32[2,3]{1,0:T(2,128)}, u32[]{:S(2)}) copy-start(s32[2,3]{1,0:T(2,128)} %param.22) | copy-start | bytes 76
  0.6 5.8 %copy-start.20 = (s32[1,4,4]{2,1,0:T(4,128)S(1)}, s32[1,4,4]{2,1,0:T(4,128)}, u32[]{:S(2)}) copy-start(s32[1,4,4]{2,1,0:T(4,128)} %param.23) | copy-start | bytes 196
  3.4 6.2 %collective-permute-start = (f32[5,64,128]{2,1,0:T(8,128)}, f32[5,64,128]{2,1,0:T(8,128)S(1)}, u32[]{:S(2)}, u32[]{:S(2)}) collective-permute-start(f32[5,64,128]{2,1,0:T(8,128)} %get-tuple-element.33), channel_id=1, source_target_pairs={{0,16},{16,32},{32,48},{48,64},{64,80},{80,96},{96,112},{112,0},{1... | collective-permute-start | bytes 491528 | tf_op jit(solution)/shard_map/ppermute | solution.py:527
  3.4 6.2 %collective-permute-start.1 = (f32[5,64,128]{2,1,0:T(8,128)}, f32[5,64,128]{2,1,0:T(8,128)S(1)}, u32[]{:S(2)}, u32[]{:S(2)}) collective-permute-start(f32[5,64,128]{2,1,0:T(8,128)} %get-tuple-element.34), channel_id=1, source_target_pairs={{0,112},{16,0},{32,16},{48,32},{64,48},{80,64},{96,80},{112,96},{1... | collective-permute-start | bytes 491528 | tf_op jit(solution)/shard_map/ppermute | solution.py:528
  9.6 0.7 copy-start
  9.6 0.7 copy-start.1
  11.9 11.6 %collective-permute-start.2 = (f32[328,128]{1,0:T(8,128)}, f32[328,128]{1,0:T(8,128)S(1)}, u32[]{:S(2)}, u32[]{:S(2)}) collective-permute-start(f32[328,128]{1,0:T(8,128)} %get-tuple-element.37), channel_id=1, source_target_pairs={{0,1},{1,2},{2,3},{3,4},{4,5},{5,6},{6,7},{7,8},{8,9},{9,10},{10,1... | collective-permute-start | bytes 503816 | tf_op jit(solution)/shard_map/ppermute | solution.py:530
  14.0 9.6 %collective-permute-start.3 = (f32[328,128]{1,0:T(8,128)}, f32[328,128]{1,0:T(8,128)S(1)}, u32[]{:S(2)}, u32[]{:S(2)}) collective-permute-start(f32[328,128]{1,0:T(8,128)} %get-tuple-element.38), channel_id=1, source_target_pairs={{0,15},{1,0},{2,1},{3,2},{4,3},{5,4},{6,5},{7,6},{8,7},{9,8},{10,9... | collective-permute-start | bytes 503816 | tf_op jit(solution)/shard_map/ppermute | solution.py:531
  23.6 0.7 copy-start.2
  24.2 0.7 copy-start.3
  35.2 5.1 %collective-permute-start.4 = (f32[2,2,16,128]{3,2,1,0:T(8,128)}, f32[2,2,16,128]{3,2,1,0:T(8,128)S(1)}, u32[]{:S(2)}, u32[]{:S(2)}) collective-permute-start(f32[2,2,16,128]{3,2,1,0:T(8,128)} %get-tuple-element.41), channel_id=1, source_target_pairs={{0,1},{1,0},{2,3},{3,2},{4,5},{5,4},{6,7},{7,6},{8,9},{9,8},{10,11... | collective-permute-start | bytes 98312 | tf_op jit(solution)/shard_map/ppermute | solution.py:538
  35.3 5.7 %collective-permute-start.5 = (f32[2,2,16,128]{3,2,1,0:T(8,128)}, f32[2,2,16,128]{3,2,1,0:T(8,128)S(1)}, u32[]{:S(2)}, u32[]{:S(2)}) collective-permute-start(f32[2,2,16,128]{3,2,1,0:T(8,128)} %get-tuple-element.42), channel_id=1, source_target_pairs={{0,64},{1,65},{2,66},{3,67},{4,68},{5,69},{6,70},{7,71},{8,72},{9,... | collective-permute-start | bytes 98312 | tf_op jit(solution)/shard_map/ppermute | solution.py:538
  37.0 6.5 %collective-permute-start.6 = (f32[2,2,16,128]{3,2,1,0:T(8,128)}, f32[2,2,16,128]{3,2,1,0:T(8,128)S(1)}, u32[]{:S(2)}, u32[]{:S(2)}) collective-permute-start(f32[2,2,16,128]{3,2,1,0:T(8,128)} %get-tuple-element.43), channel_id=1, source_target_pairs={{0,65},{1,64},{2,67},{3,66},{4,69},{5,68},{6,71},{7,70},{8,73},{9,... | collective-permute-start | bytes 98312 | tf_op jit(solution)/shard_map/ppermute | solution.py:538
  40.3 3.3 %copy-start.12 = (f32[2,2,16,128]{3,2,1,0:T(8,128)}, f32[2,2,16,128]{3,2,1,0:T(8,128)S(1)}, u32[]{:S(2)}) copy-start(f32[2,2,16,128]{3,2,1,0:T(8,128)S(1)} %collective-permute-done.4.r1) | copy-start | bytes 98308
  41.0 2.5 %copy-start.14 = (f32[2,2,16,128]{3,2,1,0:T(8,128)}, f32[2,2,16,128]{3,2,1,0:T(8,128)S(1)}, u32[]{:S(2)}) copy-start(f32[2,2,16,128]{3,2,1,0:T(8,128)S(1)} %collective-permute-done.5.r2) | copy-start | bytes 98308
  43.5 0.6 copy-start.17
  53.9 6.6 %collective-permute-start.9 = (f32[2,16,256]{2,1,0:T(8,128)}, f32[2,16,256]{2,1,0:T(8,128)S(1)}, u32[]{:S(2)}, u32[]{:S(2)}) collective-permute-start(f32[2,16,256]{2,1,0:T(8,128)} %get-tuple-element.44.r0), channel_id=1, source_target_pairs={{0,65},{1,64},{2,67},{3,66},{4,69},{5,68},{6,71},{7,70},{8,73},{9,... | collective-permute-start | bytes 98312 | tf_op jit(solution)/shard_map/ppermute | solution.py:538
  57.2 5.6 %collective-permute-start.8 = (f32[2,16,256]{2,1,0:T(8,128)}, f32[2,16,256]{2,1,0:T(8,128)S(1)}, u32[]{:S(2)}, u32[]{:S(2)}) collective-permute-start(f32[2,16,256]{2,1,0:T(8,128)} %get-tuple-element.44.r0), channel_id=1, source_target_pairs={{0,64},{1,65},{2,66},{3,67},{4,68},{5,69},{6,70},{7,71},{8,72},{9,... | collective-permute-start | bytes 98312 | tf_op jit(solution)/shard_map/ppermute | solution.py:538
  58.9 4.1 %collective-permute-start.7 = (f32[2,16,256]{2,1,0:T(8,128)}, f32[2,16,256]{2,1,0:T(8,128)S(1)}, u32[]{:S(2)}, u32[]{:S(2)}) collective-permute-start(f32[2,16,256]{2,1,0:T(8,128)} %get-tuple-element.44.r0), channel_id=1, source_target_pairs={{0,1},{1,0},{2,3},{3,2},{4,5},{5,4},{6,7},{7,6},{8,9},{9,8},{10,11... | collective-permute-start | bytes 98312 | tf_op jit(solution)/shard_map/ppermute | solution.py:538
  60.5 2.5 %copy-start.10 = (f32[2,16,256]{2,1,0:T(8,128)}, f32[2,16,256]{2,1,0:T(8,128)S(1)}, u32[]{:S(2)}) copy-start(f32[2,16,256]{2,1,0:T(8,128)S(1)} %collective-permute-done.9.r3) | copy-start | bytes 98308
  62.9 0.6 copy-start.13
  63.0 0.6 copy-start.16
  67.9 5.1 %collective-permute-start.10 = (f32[2,64,128]{2,1,0:T(8,128)}, f32[2,64,128]{2,1,0:T(8,128)S(1)}, u32[]{:S(2)}, u32[]{:S(2)}) collective-permute-start(f32[2,64,128]{2,1,0:T(8,128)} %get-tuple-element.46), channel_id=1, source_target_pairs={{0,16},{16,32},{32,48},{48,64},{64,80},{80,96},{96,112},{112,0},{1... | collective-permute-start | bytes 196616 | tf_op jit(solution)/shard_map/ppermute | solution.py:527
  67.9 5.2 %collective-permute-start.11 = (f32[2,64,128]{2,1,0:T(8,128)}, f32[2,64,128]{2,1,0:T(8,128)S(1)}, u32[]{:S(2)}, u32[]{:S(2)}) collective-permute-start(f32[2,64,128]{2,1,0:T(8,128)} %get-tuple-element.47), channel_id=1, source_target_pairs={{0,112},{16,0},{32,16},{48,32},{64,48},{80,64},{96,80},{112,96},{1... | collective-permute-start | bytes 196616 | tf_op jit(solution)/shard_map/ppermute | solution.py:528
  73.0 0.6 copy-start.4
  73.1 0.6 copy-start.5
  75.2 7.9 %collective-permute-start.12 = (f32[136,128]{1,0:T(8,128)}, f32[136,128]{1,0:T(8,128)S(1)}, u32[]{:S(2)}, u32[]{:S(2)}) collective-permute-start(f32[136,128]{1,0:T(8,128)} %get-tuple-element.50), channel_id=1, source_target_pairs={{0,1},{1,2},{2,3},{3,4},{4,5},{5,6},{6,7},{7,8},{8,9},{9,10},{10,1... | collective-permute-start | bytes 208904 | tf_op jit(solution)/shard_map/ppermute | solution.py:530
  75.3 7.8 %collective-permute-start.13 = (f32[136,128]{1,0:T(8,128)}, f32[136,128]{1,0:T(8,128)S(1)}, u32[]{:S(2)}, u32[]{:S(2)}) collective-permute-start(f32[136,128]{1,0:T(8,128)} %get-tuple-element.51), channel_id=1, source_target_pairs={{0,15},{1,0},{2,1},{3,2},{4,3},{5,4},{6,5},{7,6},{8,7},{9,8},{10,9... | collective-permute-start | bytes 208904 | tf_op jit(solution)/shard_map/ppermute | solution.py:531
  83.1 0.6 copy-start.6
  83.2 0.6 copy-start.7
  94.0 5.1 %collective-permute-start.14 = (f32[2,2,16,128]{3,2,1,0:T(8,128)}, f32[2,2,16,128]{3,2,1,0:T(8,128)S(1)}, u32[]{:S(2)}, u32[]{:S(2)}) collective-permute-start(f32[2,2,16,128]{3,2,1,0:T(8,128)} %get-tuple-element.56), channel_id=1, source_target_pairs={{0,1},{1,0},{2,3},{3,2},{4,5},{5,4},{6,7},{7,6},{8,9},{9,8},{10,11... | collective-permute-start | bytes 98312 | tf_op jit(solution)/shard_map/ppermute | solution.py:538
  94.1 5.7 %collective-permute-start.15 = (f32[2,2,16,128]{3,2,1,0:T(8,128)}, f32[2,2,16,128]{3,2,1,0:T(8,128)S(1)}, u32[]{:S(2)}, u32[]{:S(2)}) collective-permute-start(f32[2,2,16,128]{3,2,1,0:T(8,128)} %get-tuple-element.57), channel_id=1, source_target_pairs={{0,64},{1,65},{2,66},{3,67},{4,68},{5,69},{6,70},{7,71},{8,72},{9,... | collective-permute-start | bytes 98312 | tf_op jit(solution)/shard_map/ppermute | solution.py:538
  95.3 6.5 %collective-permute-start.16 = (f32[2,2,16,128]{3,2,1,0:T(8,128)}, f32[2,2,16,128]{3,2,1,0:T(8,128)S(1)}, u32[]{:S(2)}, u32[]{:S(2)}) collective-permute-start(f32[2,2,16,128]{3,2,1,0:T(8,128)} %get-tuple-element.58), channel_id=1, source_target_pairs={{0,65},{1,64},{2,67},{3,66},{4,69},{5,68},{6,71},{7,70},{8,73},{9,... | collective-permute-start | bytes 98312 | tf_op jit(solution)/shard_map/ppermute | solution.py:538
  99.1 2.7 %copy-start.8 = (f32[2,2,16,128]{3,2,1,0:T(8,128)}, f32[2,2,16,128]{3,2,1,0:T(8,128)S(1)}, u32[]{:S(2)}) copy-start(f32[2,2,16,128]{3,2,1,0:T(8,128)S(1)} %collective-permute-done.14.r1) | copy-start | bytes 98308
  99.8 2.0 %copy-start.9 = (f32[2,2,16,128]{3,2,1,0:T(8,128)}, f32[2,2,16,128]{3,2,1,0:T(8,128)S(1)}, u32[]{:S(2)}) copy-start(f32[2,2,16,128]{3,2,1,0:T(8,128)S(1)} %collective-permute-done.15.r2) | copy-start | bytes 98308
  101.9 0.6 copy-start.11
  112.2 6.6 %collective-permute-start.19 = (f32[2,16,256]{2,1,0:T(8,128)}, f32[2,16,256]{2,1,0:T(8,128)S(1)}, u32[]{:S(2)}, u32[]{:S(2)}) collective-permute-start(f32[2,16,256]{2,1,0:T(8,128)} %get-tuple-element.59.r0), channel_id=1, source_target_pairs={{0,65},{1,64},{2,67},{3,66},{4,69},{5,68},{6,71},{7,70},{8,73},{9,... | collective-permute-start | bytes 98312 | tf_op jit(solution)/shard_map/ppermute | solution.py:538
  116.1 5.6 %collective-permute-start.18 = (f32[2,16,256]{2,1,0:T(8,128)}, f32[2,16,256]{2,1,0:T(8,128)S(1)}, u32[]{:S(2)}, u32[]{:S(2)}) collective-permute-start(f32[2,16,256]{2,1,0:T(8,128)} %get-tuple-element.59.r0), channel_id=1, source_target_pairs={{0,64},{1,65},{2,66},{3,67},{4,68},{5,69},{6,70},{7,71},{8,72},{9,... | collective-permute-start | bytes 98312 | tf_op jit(solution)/shard_map/ppermute | solution.py:538
  117.2 4.5 %collective-permute-start.17 = (f32[2,16,256]{2,1,0:T(8,128)}, f32[2,16,256]{2,1,0:T(8,128)S(1)}, u32[]{:S(2)}, u32[]{:S(2)}) collective-permute-start(f32[2,16,256]{2,1,0:T(8,128)} %get-tuple-element.59.r0), channel_id=1, source_target_pairs={{0,1},{1,0},{2,3},{3,2},{4,5},{5,4},{6,7},{7,6},{8,9},{9,8},{10,11... | collective-permute-start | bytes 98312 | tf_op jit(solution)/shard_map/ppermute | solution.py:538
  118.8 2.9 %copy-start.15 = (f32[2,16,256]{2,1,0:T(8,128)}, f32[2,16,256]{2,1,0:T(8,128)S(1)}, u32[]{:S(2)}) copy-start(f32[2,16,256]{2,1,0:T(8,128)S(1)} %collective-permute-done.19.r3) | copy-start | bytes 98308
  121.7 0.6 copy-start.18
  121.7 0.6 copy-start.19

commit v2 on v1

v2 whole, which is shorter than its diff:
```python
import functools

import jax
import jax.numpy as jnp
import numpy as np
from jax import lax
from jax.experimental import pallas as pl
from jax.experimental.pallas import tpu as pltpu
from jax.sharding import PartitionSpec as P

CX = 64
CY = 64
NZ = 128
BC = 16
FINE = 48
PLANE = FINE * FINE
MOST = 4
F32 = jnp.float32
BF16 = jnp.bfloat16
ANY = pl.BlockSpec(memory_space=pl.ANY)
HBM = pl.BlockSpec(memory_space=pltpu.HBM)
VMEM = pl.BlockSpec(memory_space=pltpu.VMEM)
SMEM = pl.BlockSpec(memory_space=pltpu.SMEM)
LIMIT = 20 * 1024 * 1024


def tables():
    flat = np.arange(PLANE)
    y, z = flat // FINE, flat % FINE
    masks = np.stack([z > 0, z < FINE - 1]).astype(np.float32)
    masks = np.repeat(masks[:, None, :], 8, axis=1)
    r = np.arange(BC)[:, None]
    spread = np.zeros((128, PLANE), np.float32)
    spread[0:16] = (y == 0) & (z // 3 == r)
    spread[16:32] = (y == FINE - 1) & (z // 3 == r)
    spread[32:48] = (z == 0) & (y // 3 == r)
    spread[48:64] = (z == FINE - 1) & (y // 3 == r)
    spread[64:80] = z // 3 == r
    spread[80:96] = z // 3 == r
    spread = np.concatenate([spread, spread], axis=0)
    pick = (y // 3 == r).astype(np.float32)
    pool = ((y // 3 * BC + z // 3)[:, None] == np.arange(BC * BC)[None, :]).astype(np.float32)
    return jnp.asarray(masks), jnp.asarray(spread, BF16), jnp.asarray(pick), jnp.asarray(pool, BF16)


def partner_of(meta, device):
    away = (meta[22] * 16 + meta[23]) ^ device
    return (away & 1) + 2 * ((away >> 6) & 1)


def far(value):
    return pltpu.with_memory_space_constraint(value, pltpu.HBM)


def split(value):
    high = value.astype(BF16)
    low = (value - high.astype(F32)).astype(BF16)
    return high, low


def dot(left, right):
    return jnp.dot(left, right, preferred_element_type=F32)


def edges_kernel(p, q, c, a, xup, xdn, yup, ydn, tiles, sem):
    copies = []
    for n, ref in enumerate((p, q, c, a)):
        if n == 0:
            copies.append((ref.at[CX - 2 : CX], xup.at[0:2]))
            copies.append((ref.at[0:2], xdn.at[0:2]))
        else:
            copies.append((ref.at[CX - 1], xup.at[n + 1]))
            copies.append((ref.at[0], xdn.at[n + 1]))
        copies.append((ref.at[:, CY - 8 : CY, :], tiles.at[0, n]))
        copies.append((ref.at[:, 0:8, :], tiles.at[1, n]))
    copies = [pltpu.make_async_copy(*ends, sem.at[n]) for n, ends in enumerate(copies)]
    for copy in copies:
        copy.start()
    for copy in copies:
        copy.wait()

    def plane(side, n, y):
        return tiles.at[side, n].reshape(CX * 8, NZ)[pl.ds(y, CX, stride=8), :]

    yup[0:64, :] = plane(0, 0, 6)
    yup[64:128, :] = plane(0, 0, 7)
    ydn[0:64, :] = plane(1, 0, 0)
    ydn[64:128, :] = plane(1, 0, 1)
    for n in range(1, 4):
        yup[64 * (n + 1) : 64 * (n + 2), :] = plane(0, n, 7)
        ydn[64 * (n + 1) : 64 * (n + 2), :] = plane(1, n, 0)
    yup[320:328, :] = jnp.zeros((8, 128), F32)
    ydn[320:328, :] = jnp.zeros((8, 128), F32)


def edges(p, q, c, a):
    x = jax.ShapeDtypeStruct((5, CY, NZ), F32)
    y = jax.ShapeDtypeStruct((5 * CX + 8, NZ), F32)
    return pl.pallas_call(
        edges_kernel,
        out_shape=(x, x, y, y),
        in_specs=[HBM] * 4,
        out_specs=[VMEM] * 4,
        scratch_shapes=[pltpu.VMEM((2, 4, CX, 8, NZ), F32), pltpu.SemaphoreType.DMA((16,))],
        compiler_params=pltpu.CompilerParams(vmem_limit_bytes=LIMIT),
        name="edges",
    )(*[far(v) for v in (p, q, c, a)])


def corners_kernel(base, meta, yup, ydn, xlo, xhi, yup_out, ydn_out, rows, sem):
    lo = meta[22] > 0
    hi = meta[22] < 7
    for n, y in ((0, CY - 1), (1, 0)):
        rows[n, 0:1, :] = jnp.where(lo, xlo[1, y : y + 1, :], 0.0)
        rows[n, 1:2, :] = jnp.where(hi, xhi[0, y : y + 1, :], 0.0)
    copies = [
        pltpu.make_async_copy(rows.at[0], yup_out.at[base : base + 8, :], sem.at[0]),
        pltpu.make_async_copy(rows.at[1], ydn_out.at[base : base + 8, :], sem.at[1]),
    ]
    for copy in copies:
        copy.start()
    for copy in copies:
        copy.wait()


def corners(meta, yup, ydn, xlo, xhi):
    base = yup.shape[0] - 8
    y = jax.ShapeDtypeStruct(yup.shape, F32)
    return pl.pallas_call(
        functools.partial(corners_kernel, base),
        out_shape=(y, y),
        in_specs=[SMEM, ANY, ANY, VMEM, VMEM],
        out_specs=[ANY, ANY],
        input_output_aliases={1: 0, 2: 1},
        scratch_shapes=[pltpu.VMEM((2, 8, NZ), F32), pltpu.SemaphoreType.DMA((2,))],
        compiler_params=pltpu.CompilerParams(vmem_limit_bytes=LIMIT),
        name="corners",
    )(meta, yup, ydn, xlo, xhi)


def inverse(value):
    guess = pl.reciprocal(value, approx=True)
    guess = guess * (2.0 - value * guess)
    return guess * (2.0 - value * guess)


def lanes_both_ways(here):
    lane = lax.broadcasted_iota(jnp.int32, here.shape, 1)
    before = jnp.where(lane > 0, pltpu.roll(here, 1, 1), 0.0)
    after = jnp.where(lane < NZ - 1, pltpu.roll(here, NZ - 1, 1), 0.0)
    return before + after


def advance(here, beside, before, courant, absorb):
    inv = inverse(1.0 + absorb)
    return before + (2.0 * inv) * (here - before) + (courant * inv) * (beside - 6.0 * here)


CHUNKS = 4
ROWS = CX // CHUNKS
BLOCK = (CX, CY, NZ)
PADDED = (CX + 2, CY + 16, NZ)


def clear_rim(pe):
    edge = jnp.zeros((CX, 8, NZ), F32)
    pe[1 : CX + 1, 0:8, :] = edge
    pe[1 : CX + 1, CY + 8 : CY + 16, :] = edge
    pe[0] = jnp.zeros((CY + 16, NZ), F32)
    pe[CX + 1] = jnp.zeros((CY + 16, NZ), F32)


def around(pe, x):
    here = pe[x + 1, 8 : CY + 8, :]
    beside = pe[x, 8 : CY + 8, :] + pe[x + 2, 8 : CY + 8, :]
    beside = beside + pe[x + 1, 7 : CY + 7, :] + pe[x + 1, 9 : CY + 9, :]
    return here, beside + lanes_both_ways(here)


def first_inner_kernel(p, q, c, a, raw, two, side, here_out, pe, qs, cs, as_, sem):
    copies = []
    for n in range(CHUNKS):
        s = slice(ROWS * n, ROWS * n + ROWS)
        to_rows = slice(1 + ROWS * n, 1 + ROWS * n + ROWS)
        part = [pltpu.make_async_copy(p.at[s], pe.at[to_rows, 8 : CY + 8, :], sem.at[0, n])]
        for m, (ref, to) in enumerate(((q, qs), (c, cs), (a, as_))):
            part.append(pltpu.make_async_copy(ref.at[s], to.at[s], sem.at[m + 1, n]))
        copies.append(part)
    for part in copies:
        for copy in part:
            copy.start()
    clear_rim(pe)
    copies[0][0].wait()

    def body(x, carry):
        here, beside = around(pe, x)
        inv = inverse(1.0 + as_[x])
        twice = 2.0 * inv
        weight = cs[x] * inv
        two[x] = twice
        side[x] = weight
        here_out[x] = here
        raw[x] = qs[x] + twice * (here - qs[x]) + weight * (beside - 6.0 * here)
        return carry

    for n in range(CHUNKS):
        if n + 1 < CHUNKS:
            copies[n + 1][0].wait()
        for copy in copies[n][1:]:
            copy.wait()
        lax.fori_loop(ROWS * n, ROWS * n + ROWS, body, 0, unroll=8)


def first_inner(p, q, c, a):
    block = jax.ShapeDtypeStruct(BLOCK, F32)
    return pl.pallas_call(
        first_inner_kernel,
        out_shape=(block, block, block, block),
        in_specs=[HBM] * 4,
        out_specs=[VMEM] * 4,
        scratch_shapes=[
            pltpu.VMEM(PADDED, F32),
            pltpu.VMEM(BLOCK, F32),
            pltpu.VMEM(BLOCK, F32),
            pltpu.VMEM(BLOCK, F32),
            pltpu.SemaphoreType.DMA((4, CHUNKS)),
        ],
        compiler_params=pltpu.CompilerParams(vmem_limit_bytes=LIMIT),
        cost_estimate=pl.CostEstimate(flops=12000000, bytes_accessed=10000000, transcendentals=0),
        name="first_inner",
    )(*[far(v) for v in (p, q, c, a)])


def second_inner_kernel(p, q, two, side, raw, out, pe, sem):
    store = pltpu.make_async_copy(p, out, sem)
    store.start()
    clear_rim(pe)

    def fill(x, carry):
        pe[x + 1, 8 : CY + 8, :] = p[x]
        return carry

    lax.fori_loop(0, CX, fill, 0, unroll=8)

    def body(x, carry):
        here, beside = around(pe, x)
        raw[x] = q[x] + two[x] * (here - q[x]) + side[x] * (beside - 6.0 * here)
        return carry

    lax.fori_loop(0, CX, body, 0, unroll=8)
    store.wait()


def second_inner(p, q, two, side):
    return pl.pallas_call(
        second_inner_kernel,
        out_shape=(jax.ShapeDtypeStruct(BLOCK, F32),) * 2,
        in_specs=[VMEM] * 4,
        out_specs=[VMEM, ANY],
        scratch_shapes=[pltpu.VMEM(PADDED, F32), pltpu.SemaphoreType.DMA],
        compiler_params=pltpu.CompilerParams(vmem_limit_bytes=LIMIT),
        cost_estimate=pl.CostEstimate(flops=12000000, bytes_accessed=8000000, transcendentals=0),
        name="second_inner",
    )(p, q, two, side)


def coarse_kernel(
    first,
    meta,
    p,
    raw,
    weight,
    pxlo,
    pxhi,
    pylo,
    pyhi,
    exlo,
    exhi,
    eylo,
    eyhi,
    new,
    face0,
    face1,
    face2,
    face3,
    rim,
    ring,
    faces,
):
    tile, bulk = meta[22], meta[23]
    inside_grid = (tile > 0, tile < 7, bulk > 0, bulk < 15)
    base = pylo.shape[0] - 8
    qlo, qhi = (2, 2) if first else (1, 0)

    def keep(n, value):
        return jnp.where(inside_grid[n], value, 0.0)

    def body(x, carry):
        new[x] = raw[x]
        return carry

    lax.fori_loop(0, CX, body, 0, unroll=8)

    def plane(ref, y):
        return ref.reshape(CX * CY, NZ)[pl.ds(y, CX, stride=CY), :]

    def corner(n, ref, at):
        return keep(n, ref[base + at : base + at + 1, :])

    def extra(ref, n):
        return ref[n] if len(ref.shape) == 3 else ref[64 * n : 64 * n + 64, :]

    sides = (
        (pxlo[1], pxlo[0], p[0], corner(2, pylo, 0), corner(3, pyhi, 0), exlo, qlo),
        (pxhi[0], pxhi[1], p[CX - 1], corner(2, pylo, 1), corner(3, pyhi, 1), exhi, qhi),
        (pylo[64:128, :], pylo[0:64, :], plane(p, 0), *[pylo[base + n : base + n + 1, :] for n in (0, 1)], eylo, qlo),
        (pyhi[0:64, :], pyhi[64:128, :], plane(p, CY - 1), *[pyhi[base + n : base + n + 1, :] for n in (0, 1)], eyhi, qhi),
    )
    for n, (here, out, inside, before, after, ref, at_q) in enumerate(sides):
        here = keep(n, here)
        rim[0, n] = here
        ring[n, 7:8, :] = keep(n, before)
        ring[n, 8:72, :] = here
        ring[n, 72:73, :] = keep(n, after)
        beside = ring[n, 7:71, :] + ring[n, 9:73, :] + keep(n, out) + inside + lanes_both_ways(here)
        rim[1, n] = advance(here, beside, *[keep(n, extra(ref, m)) for m in (at_q, 3, 4)])

    new[0] = new[0] + weight[0] * rim[0, 0]
    new[CX - 1] = new[CX - 1] + weight[CX - 1] * rim[0, 1]
    low = (plane(weight, 0) * rim[0, 2])[:, None, :]
    new[:, 0:1, :] = new[:, 0:1, :] + low
    high = (plane(weight, CY - 1) * rim[0, 3])[:, None, :]
    new[:, CY - 1 : CY, :] = new[:, CY - 1 : CY, :] + high

    from_z = lax.broadcasted_iota(jnp.int32, (NZ, NZ), 0)
    to_lane = lax.broadcasted_iota(jnp.int32, (NZ, NZ), 1)
    out_lane = lax.broadcasted_iota(jnp.int32, (BC, NZ), 1)
    deep_lane = lax.broadcasted_iota(jnp.int32, (BC, BC, NZ), 2)
    deep_y = lax.broadcasted_iota(jnp.int32, (BC, BC, NZ), 1)
    diagonal = (deep_lane & 15) == deep_y

    def entry(k, carry):
        ident = meta[k]

        @pl.when(ident >= 0)
        def _():
            ox = pl.multiple_of(meta[4 + k], 16)
            oy = pl.multiple_of(meta[8 + k], 16)
            oz = meta[12 + k]
            where_to = partner_of(meta, ident >> 1) * 2 + (ident & 1)
            low_face = (to_lane >= 32) & (to_lane < 48)
            high_face = (to_lane >= 48) & (to_lane < 64)
            source = jnp.where(
                low_face, oz - 1, jnp.where(high_face, oz + BC, oz + (to_lane & 15))
            )
            mover = jnp.where(from_z == source, 1.0, 0.0).astype(BF16)
            mover = jnp.concatenate([mover, mover], axis=0)
            for t, ref in enumerate((p, new)):
                cube = ref[pl.ds(ox, BC), pl.ds(oy, BC), :].reshape(BC * BC, NZ)
                y = pl.multiple_of(jnp.maximum(oy - 8, 0), 8)
                ym = ref[pl.ds(ox, BC), pl.ds(y, 8), :][:, 7, :]
                ym = jnp.where(oy == 0, rim[t, 2, pl.ds(ox, BC), :], ym)
                y = pl.multiple_of(jnp.minimum(oy + BC, CY - 8), 8)
                yp = ref[pl.ds(ox, BC), pl.ds(y, 8), :][:, 0, :]
                yp = jnp.where(oy == CY - BC, rim[t, 3, pl.ds(ox, BC), :], yp)
                xm = ref[jnp.maximum(ox - 1, 0), pl.ds(oy, BC), :]
                xm = jnp.where(ox == 0, rim[t, 0, pl.ds(oy, BC), :], xm)
                xp = ref[jnp.minimum(ox + BC, CX - 1), pl.ds(oy, BC), :]
                xp = jnp.where(ox == CX - BC, rim[t, 1, pl.ds(oy, BC), :], xp)
                high, low = split(jnp.concatenate([cube, ym, yp, xm, xp], axis=0))
                moved = dot(jnp.concatenate([high, low], axis=1), mover)
                z_face = jnp.where(diagonal, moved[0:256].reshape(BC, BC, NZ), 0.0).sum(axis=1)
                tile_ = jnp.where(out_lane < 80, moved[288:304], moved[304:320])
                tile_ = jnp.where(out_lane < 64, z_face, tile_)
                tile_ = jnp.where(out_lane < 32, moved[272:288], tile_)
                tile_ = jnp.where(out_lane < 16, moved[256:272], tile_)
                faces[where_to, t] = tile_

        return carry

    lax.fori_loop(0, MOST, entry, 0)
    for n, ref in enumerate((face0, face1, face2, face3)):
        ref[...] = faces[2 * n : 2 * n + 2]


def coarse(first, meta, p, raw, weight, halos, extras):
    face = jax.ShapeDtypeStruct((2, 2, BC, NZ), F32)
    return pl.pallas_call(
        functools.partial(coarse_kernel, first),
        out_shape=(jax.ShapeDtypeStruct(BLOCK, F32), face, face, face, face),
        in_specs=[SMEM] + [VMEM] * 11,
        out_specs=[VMEM] * 5,
        scratch_shapes=[
            pltpu.VMEM((2, 4, 64, NZ), F32),
            pltpu.VMEM((4, 80, NZ), F32),
            pltpu.VMEM((8, 2, BC, NZ), F32),
        ],
        compiler_params=pltpu.CompilerParams(vmem_limit_bytes=LIMIT),
        name="coarse",
    )(meta, p, raw, weight, *halos, *extras)


def factors_kernel(c, a, one, two, three, cs, as_, sem):
    copies = []
    for j in range(2):
        copies.append(pltpu.make_async_copy(c.at[j], cs.at[j], sem.at[2 * j]))
        copies.append(pltpu.make_async_copy(a.at[j], as_.at[j], sem.at[2 * j + 1]))
    for copy in copies:
        copy.start()
    for j in range(2):
        copies[2 * j].wait()
        copies[2 * j + 1].wait()

        def body(i, carry):
            s = pl.ds(pl.multiple_of(8 * i, 8), 8)
            inv = inverse(1.0 + as_[j, s, :])
            side = cs[j, s, :] * inv
            three[j, s, :] = side
            one[j, s, :] = 2.0 * inv - 6.0 * side
            two[j, s, :] = 1.0 - 2.0 * inv
            return carry

        lax.fori_loop(0, FINE // 8, body, 0)


def factors(c, a):
    box = jax.ShapeDtypeStruct((2, FINE, PLANE), F32)
    return pl.pallas_call(
        factors_kernel,
        out_shape=(box, box, box),
        in_specs=[HBM] * 2,
        out_specs=[VMEM] * 3,
        scratch_shapes=[pltpu.VMEM(box.shape, F32)] * 2 + [pltpu.SemaphoreType.DMA((4,))],
        compiler_params=pltpu.CompilerParams(vmem_limit_bytes=LIMIT),
        cost_estimate=pl.CostEstimate(flops=3000000, bytes_accessed=4000000, transcendentals=0),
        name="factors",
    )(far(c), far(a))


def turned(v):
    return {d: (pltpu.roll(v, d, 1), pltpu.roll(v, 128 - d, 1)) for d in (1, 48)}


def beside_in_plane(row, masks):
    small = lax.broadcasted_iota(jnp.int32, (8, 128), 1)
    zero = jnp.zeros((8, 128), F32)
    none = {d: (zero, zero) for d in (1, 48)}
    cur = row(0)
    cur_t = turned(cur)
    before_t = none
    for k in range(PLANE // 128):
        ls = slice(128 * k, 128 * k + 128)
        last = k + 1 == PLANE // 128
        nxt = cur if last else row(k + 1)
        nxt_t = none if last else turned(nxt)
        total = jnp.where(small < 48, before_t[48][0], cur_t[48][0])
        total = total + jnp.where(small >= 80, nxt_t[48][1], cur_t[48][1])
        down = jnp.where(small < 1, before_t[1][0], cur_t[1][0])
        up = jnp.where(small >= 127, nxt_t[1][1], cur_t[1][1])
        total = total + down * masks[0, :, ls] + up * masks[1, :, ls]
        yield ls, cur, total
        before_t, cur, cur_t = cur_t, nxt, nxt_t


def ahead_kernel(f, g, one, two, three, masks, raw, buf, sem):
    copies = [pltpu.make_async_copy(f.at[j], buf.at[j, 8:56, :], sem.at[j]) for j in range(2)]
    for copy in copies:
        copy.start()
    for j in range(2):
        buf[j, 0:8, :] = jnp.zeros((8, PLANE), F32)
        buf[j, 56:64, :] = jnp.zeros((8, PLANE), F32)
    for copy in copies:
        copy.wait()

    def box(j, carry):
        for i in range(6):
            s = slice(8 * i, 8 * i + 8)

            def row(k):
                return buf[j, 8 + 8 * i : 16 + 8 * i, 128 * k : 128 * k + 128]

            for ls, cur, total in beside_in_plane(row, masks):
                total = total + buf[j, 7 + 8 * i : 15 + 8 * i, ls] + buf[j, 9 + 8 * i : 17 + 8 * i, ls]
                raw[j, s, ls] = (
                    one[j, s, ls] * cur + two[j, s, ls] * g[j, s, ls] + three[j, s, ls] * total
                )
        return carry

    lax.fori_loop(0, 2, box, 0)


def ahead(f, g, weights, masks):
    box = jax.ShapeDtypeStruct((2, FINE, PLANE), F32)
    return pl.pallas_call(
        ahead_kernel,
        out_shape=box,
        in_specs=[ANY] + [VMEM] * 5,
        out_specs=VMEM,
        scratch_shapes=[pltpu.VMEM((2, 64, PLANE), F32), pltpu.SemaphoreType.DMA((2,))],
        compiler_params=pltpu.CompilerParams(vmem_limit_bytes=LIMIT),
        cost_estimate=pl.CostEstimate(flops=5000000, bytes_accessed=5000000, transcendentals=0),
        name="ahead",
    )(f, g, *weights, masks)


def fine_kernel(
    meta,
    f,
    raw,
    one,
    two,
    three,
    r0,
    r1,
    r2,
    r3,
    masks,
    spread,
    pick,
    pool,
    f_out,
    g_out,
    res,
    buf,
    ghost,
    xrow,
    faces,
    sem,
):
    copy = pltpu.make_async_copy(f, buf.at[0, :, 8:56, :], sem.at[0])
    copy.start()
    for n, ref in enumerate((r0, r1, r2, r3)):
        faces[2 * n : 2 * n + 2] = ref[...]

    lane = lax.broadcasted_iota(jnp.int32, (BC, NZ), 1)
    wide_lane = jnp.concatenate([lane, lane], axis=1)
    tall = lax.broadcasted_iota(jnp.int32, (FINE, BC), 0)
    wide = lax.broadcasted_iota(jnp.int32, (FINE, BC), 1)
    thrice = jnp.where((tall >= 3 * wide) & (tall < 3 * wide + 3), 1.0, 0.0).astype(BF16)
    sides, rows = [], []
    for j in range(2):
        source = (meta[16 + 3 * j] >> 6) * 16 + (meta[17 + 3 * j] >> 6)
        at = partner_of(meta, source) * 2 + j
        old = jnp.where(lane < 96, faces[at, 0], 0.0)
        new = jnp.where(lane < 96, faces[at, 1], 0.0)
        for m in range(3):
            high, low = split(old + (m / 3.0) * (new - old))
            both = jnp.concatenate([high, low], axis=1)
            zero = jnp.zeros_like(both)
            sides.append(jnp.where(wide_lane < 64, both, zero))
            rows.append(jnp.where((wide_lane >= 64) & (wide_lane < 80), both, zero))
            rows.append(jnp.where(wide_lane >= 80, both, zero))
    tall_sides = dot(thrice, jnp.concatenate(sides, axis=1)).astype(BF16)
    sides = [tall_sides[:, 256 * n : 256 * n + 256] for n in range(6)]
    spreaded = dot(jnp.concatenate(sides + rows, axis=0), spread[...])
    for j in range(2):
        for m in range(3):
            at = 48 * (3 * j + m)
            ghost[m, j] = spreaded[at : at + 48]
        for n in range(6):
            at = 288 + 16 * (6 * j + n)
            part = spreaded[at : at + 16] * pick[...]
            xrow[j, n : n + 1, :] = part.sum(axis=0, keepdims=True)
    copy.wait()

    def first(j):
        for i in range(6):
            s = slice(8 * i, 8 * i + 8)
            buf[1, j, 8 + 8 * i : 16 + 8 * i, :] = raw[j, s, :] + three[j, s, :] * ghost[0, j, s, :]
        for n, x in ((0, 0), (1, FINE - 1)):
            buf[1, j, 8 + x : 9 + x, :] = (
                buf[1, j, 8 + x : 9 + x, :] + three[j, x : x + 1, :] * xrow[j, n : n + 1, :]
            )

    def substep(m, j):
        now, old = m % 2, 1 - m % 2
        buf[now, j, 7:8, :] = xrow[j, 2 * m : 2 * m + 1, :]
        buf[now, j, 56:57, :] = xrow[j, 2 * m + 1 : 2 * m + 2, :]
        for i in range(6):
            s = slice(8 * i, 8 * i + 8)

            def row(k):
                return buf[now, j, 8 + 8 * i : 16 + 8 * i, 128 * k : 128 * k + 128]

            for ls, cur, total in beside_in_plane(row, masks):
                total = total + ghost[m, j, s, ls]
                total = total + (
                    buf[now, j, 7 + 8 * i : 15 + 8 * i, ls] + buf[now, j, 9 + 8 * i : 17 + 8 * i, ls]
                )
                buf[old, j, 8 + 8 * i : 16 + 8 * i, ls] = (
                    one[j, s, ls] * cur
                    + two[j, s, ls] * buf[old, j, 8 + 8 * i : 16 + 8 * i, ls]
                    + three[j, s, ls] * total
                )

    def box(j, carry):
        first(j)
        substep(1, j)
        substep(2, j)
        return carry

    lax.fori_loop(0, 2, box, 0)
    stores = [
        pltpu.make_async_copy(buf.at[1, :, 8:56, :], f_out, sem.at[0]),
        pltpu.make_async_copy(buf.at[0, :, 8:56, :], g_out, sem.at[1]),
    ]
    for copy in stores:
        copy.start()
    tall = lax.broadcasted_iota(jnp.int32, (BC, FINE), 1)
    wide = lax.broadcasted_iota(jnp.int32, (BC, FINE), 0)
    gather = jnp.where((tall >= 3 * wide) & (tall < 3 * wide + 3), 1.0, 0.0).astype(BF16)
    parts = [part for j in range(2) for part in split(buf[1, j, 8:56, :])]
    pooled = dot(jnp.concatenate(parts, axis=0), pool[...])
    parts = []
    for j in range(2):
        parts += split(pooled[96 * j : 96 * j + 48] + pooled[96 * j + 48 : 96 * j + 96])
    means = dot(gather, jnp.concatenate(parts, axis=1))
    for j in range(2):
        at = 512 * j
        res[j] = (means[:, at : at + 256] + means[:, at + 256 : at + 512]) * (1.0 / 27.0)
    for copy in stores:
        copy.wait()


def fine(meta, f, raw, weights, received, consts):
    box = jax.ShapeDtypeStruct((2, FINE, PLANE), F32)
    return pl.pallas_call(
        fine_kernel,
        out_shape=(box, box, jax.ShapeDtypeStruct((2, BC, BC * BC), F32)),
        in_specs=[SMEM, ANY] + [VMEM] * 12,
        out_specs=[ANY, ANY, VMEM],
        scratch_shapes=[
            pltpu.VMEM((2, 2, 64, PLANE), F32),
            pltpu.VMEM((3, 2, FINE, PLANE), F32),
            pltpu.VMEM((2, 8, PLANE), F32),
            pltpu.VMEM((8, 2, BC, NZ), F32),
            pltpu.SemaphoreType.DMA((2,)),
        ],
        compiler_params=pltpu.CompilerParams(vmem_limit_bytes=LIMIT),
        name="fine",
    )(meta, f, raw, *weights, *received, *consts)


def moved_box(meta, got, k, mine, from_yz, to_lane):
    ident = meta[k]
    value = got[partner_of(meta, ident >> 1) * 2 + (ident & 1)]
    full = jnp.where(mine, value[:, None, :], 0.0).reshape(BC * BC, BC * BC)
    high, low = split(full)
    mover = jnp.where(to_lane == meta[12 + k] + (from_yz & 15), 1.0, 0.0).astype(BF16)
    moved = dot(jnp.concatenate([high, low], axis=1), jnp.concatenate([mover, mover], axis=0))
    return moved.reshape(BC, BC, NZ)


def box_iotas():
    y_of = lax.broadcasted_iota(jnp.int32, (BC, BC, BC * BC), 1)
    lane_of = lax.broadcasted_iota(jnp.int32, (BC, BC, BC * BC), 2)
    from_yz = lax.broadcasted_iota(jnp.int32, (BC * BC, NZ), 0)
    to_lane = lax.broadcasted_iota(jnp.int32, (BC * BC, NZ), 1)
    return (lane_of >> 4) == y_of, from_yz, to_lane


def insert_kernel(meta, new, r0, r1, r2, r3, out, xup, xdn, yup, ydn, got):
    for n, ref in enumerate((r0, r1, r2, r3)):
        got[2 * n : 2 * n + 2] = ref[...]

    def body(x, carry):
        out[x] = new[x]
        return carry

    lax.fori_loop(0, CX, body, 0, unroll=8)
    lane = lax.broadcasted_iota(jnp.int32, (BC, BC, NZ), 2)
    iotas = box_iotas()

    def entry(k, carry):
        @pl.when(meta[k] >= 0)
        def _():
            at = (pl.ds(meta[4 + k], BC), pl.ds(pl.multiple_of(meta[8 + k], 16), BC))
            moved = moved_box(meta, got, k, *iotas)
            oz = meta[12 + k]
            out[at[0], at[1], :] = jnp.where(
                (lane >= oz) & (lane < oz + BC), moved, out[at[0], at[1], :]
            )

        return carry

    lax.fori_loop(0, MOST, entry, 0)

    def plane(y):
        return out.reshape(CX * CY, NZ)[pl.ds(y, CX, stride=CY), :]

    xup[...] = out[CX - 2 : CX]
    xdn[...] = out[0:2]
    yup[0:64, :] = plane(CY - 2)
    yup[64:128, :] = plane(CY - 1)
    ydn[0:64, :] = plane(0)
    ydn[64:128, :] = plane(1)
    yup[128:136, :] = jnp.zeros((8, NZ), F32)
    ydn[128:136, :] = jnp.zeros((8, NZ), F32)


def insert(meta, new, received):
    x = jax.ShapeDtypeStruct((2, CY, NZ), F32)
    y = jax.ShapeDtypeStruct((2 * CX + 8, NZ), F32)
    return pl.pallas_call(
        insert_kernel,
        out_shape=(jax.ShapeDtypeStruct(BLOCK, F32), x, x, y, y),
        in_specs=[SMEM] + [VMEM] * 5,
        out_specs=[VMEM] * 5,
        scratch_shapes=[pltpu.VMEM((8, BC, BC * BC), F32)],
        compiler_params=pltpu.CompilerParams(vmem_limit_bytes=LIMIT),
        name="insert",
    )(meta, new, *received)


def emit_kernel(new, out, sem):
    copy = pltpu.make_async_copy(new, out, sem)
    copy.start()
    copy.wait()


def emit(new):
    return pl.pallas_call(
        emit_kernel,
        out_shape=jax.ShapeDtypeStruct(BLOCK, F32),
        in_specs=[VMEM],
        out_specs=HBM,
        scratch_shapes=[pltpu.SemaphoreType.DMA],
        compiler_params=pltpu.CompilerParams(vmem_limit_bytes=LIMIT),
        cost_estimate=pl.CostEstimate(flops=0, bytes_accessed=6000000, transcendentals=0),
        name="emit",
    )(new)


def finish_kernel(meta, new, r0, r1, r2, r3, out, got, boxes, sem):
    def region(k):
        return out.at[pl.ds(meta[4 + k], BC), pl.ds(pl.multiple_of(meta[8 + k], 16), BC), :]

    slots = []
    for k in range(MOST):
        slot = k
        for n in reversed(range(k)):
            same = (meta[4 + n] == meta[4 + k]) & (meta[8 + n] == meta[8 + k]) & (meta[n] >= 0)
            slot = jnp.where(same, n, slot)
        slots.append(slot)
    valid = [meta[k] >= 0 for k in range(MOST)]
    leads = [valid[k] & (slots[k] == k) for k in range(MOST)]
    for k in range(MOST):

        @pl.when(leads[k])
        def _():
            pltpu.make_async_copy(region(k), boxes.at[k], sem.at[k]).start()

    for n, ref in enumerate((r0, r1, r2, r3)):
        got[2 * n : 2 * n + 2] = ref[...]
    lane = lax.broadcasted_iota(jnp.int32, (BC, BC, NZ), 2)
    iotas = box_iotas()
    for k in range(MOST):

        @pl.when(leads[k])
        def _():
            pltpu.make_async_copy(region(k), boxes.at[k], sem.at[k]).wait()

        @pl.when(valid[k])
        def _():
            moved = moved_box(meta, got, k, *iotas)
            oz = meta[12 + k]
            boxes[slots[k]] = jnp.where((lane >= oz) & (lane < oz + BC), moved, boxes[slots[k]])

    for k in range(MOST):

        @pl.when(leads[k])
        def _():
            pltpu.make_async_copy(boxes.at[k], region(k), sem.at[k]).start()

    for k in range(MOST):

        @pl.when(leads[k])
        def _():
            pltpu.make_async_copy(boxes.at[k], region(k), sem.at[k]).wait()


def finish(meta, new, received):
    return pl.pallas_call(
        finish_kernel,
        out_shape=jax.ShapeDtypeStruct(BLOCK, F32),
        in_specs=[SMEM, ANY] + [VMEM] * 4,
        out_specs=ANY,
        input_output_aliases={1: 0},
        scratch_shapes=[
            pltpu.VMEM((8, BC, BC * BC), F32),
            pltpu.VMEM((MOST, BC, BC, NZ), F32),
            pltpu.SemaphoreType.DMA((MOST,)),
        ],
        compiler_params=pltpu.CompilerParams(vmem_limit_bytes=LIMIT),
        name="finish",
    )(meta, new, *received)


def ring(size, by):
    return [(i, (i + by) % size) for i in range(size)]


def halo(meta, xup, xdn, yup, ydn):
    xlo = lax.ppermute(xup, "tile", ring(8, 1))
    xhi = lax.ppermute(xdn, "tile", ring(8, -1))
    yup, ydn = corners(meta, yup, ydn, xlo, xhi)
    ylo = lax.ppermute(yup, "bulk", ring(16, 1))
    yhi = lax.ppermute(ydn, "bulk", ring(16, -1))
    return xlo, xhi, ylo, yhi


def trade(values):
    done = [values[0]]
    for value, away in zip(values[1:], (1, 64, 65)):
        done.append(lax.ppermute(value, ("tile", "bulk"), [(d, d ^ away) for d in range(128)]))
    return done


def on_device(
    coarse_now,
    coarse_before,
    coarse_courant,
    coarse_absorb,
    fine_now,
    fine_before,
    fine_courant,
    fine_absorb,
    box_anchor,
    intersection,
):
    place = jnp.stack([lax.axis_index("tile"), lax.axis_index("bulk")]).astype(jnp.int32)
    meta = jnp.concatenate([intersection.reshape(16), box_anchor.reshape(6), place])
    consts = tables()
    extras = halo(meta, *edges(coarse_now, coarse_before, coarse_courant, coarse_absorb))
    weights = factors(fine_courant, fine_absorb)
    first = ahead(fine_now, fine_before, weights, consts[0])
    raw, two, side, start = first_inner(coarse_now, coarse_before, coarse_courant, coarse_absorb)
    new, *faces = coarse(True, meta, start, raw, side, extras, extras)
    f, g, res = fine(meta, fine_now, first, weights, trade(faces), consts)
    middle, *packed = insert(meta, new, trade([res] * 4))
    first = ahead(f, g, weights, consts[0])
    halos = halo(meta, *packed)
    raw, q = second_inner(middle, start, two, side)
    new, *faces = coarse(False, meta, middle, raw, side, halos, extras)
    f, g, res = fine(meta, f, first, weights, trade(faces), consts)
    p = finish(meta, emit(new), trade([res] * 4))
    return p, q, f, g


def solution(mesh):
    grid = P("tile", "bulk", None)
    boxes = P(("tile", "bulk"), None, None)
    in_specs = (grid,) * 4 + (boxes,) * 4 + (P(("tile", "bulk"), None), boxes)
    return jax.shard_map(
        on_device, mesh=mesh, in_specs=in_specs, out_specs=(grid, grid, boxes, boxes), check_vma=False
    )
```

time: 128 us -> 86.2 us (0.67)
  Pallas kernels: 54.4 us -> 32.9 us
  waiting for transfers between devices: 26.5 us -> 12.8 us
  local copies, waits for them, and re-layouts: 5.92 us -> 0.21 us
    pallas_call x2, Pallas kernels: 20.5 us -> 3.21 us  [coarse(): pl.pallas_call(functools.partial(coarse_kernel, first), out_shape=(jax.Sh...]
    pallas_call x2, Pallas kernels: 19.5 us -> 10.4 us  [fine(): pl.pallas_call(fine_kernel, out_shape=(box, box, jax.ShapeDtypeStruct((2,...]
    ppermute x12, waiting for transfers between devices: 14.4 us -> 7.04 us  [trade(): lax.ppermute(value, ('tile', 'bulk'), [(d, d ^ away) for d in range(128)])]
    pallas_call x3 -> x9, Pallas kernels: 11.2 us -> 18.1 us  [the longest x1 4.1 us: first_inner(): pl.pallas_call(first_inner_kernel, out_shape=(block, block, block, block)...]
    ppermute x2, waiting for transfers between devices: 7.42 us -> 1.01 us  [halo(): ylo = lax.ppermute(yup, 'bulk', ring(16, 1))]
    unnamed x44 -> x16, local copies, waits for them, and re-layouts: 5.76 us -> 0.05 us
    pallas_call x2, Pallas kernels: 3.12 us -> 1.16 us  [corners(): pl.pallas_call(functools.partial(corners_kernel, base), out_shape=(y, y),...]
  transfers between devices with their start and end apart: 20 -> 20, of which waited for: 14 -> 9; matrix products, arithmetic and copies ran while one was open for 1% -> 0% of each run, Pallas kernels for 0% -> 14%
where the time goes in v2:
time: 86.2 us; the launch traced here: 85.8 us
  starting transfers between devices  38.7 us (45%)
  Pallas kernels  32.9 us (38%)
  waiting for transfers between devices  12.8 us (15%)
  between operations  1.09 us (1%)
    ppermute x12, starting transfers between devices, trade(): lax.ppermute(value, ('tile', 'bulk'), [(d, d ^ away) for d in range(128)])  20.3 us
    pallas_call x2, Pallas kernels, fine(): pl.pallas_call(fine_kernel, out_shape=(box, box, jax.ShapeDtypeStruct((2,...  10.4 us
    ppermute x2, starting transfers between devices, halo(): yhi = lax.ppermute(ydn, 'bulk', ring(16, -1))  9.74 us
    ppermute x12, waiting for transfers between devices, trade(): lax.ppermute(value, ('tile', 'bulk'), [(d, d ^ away) for d in range(128)])  7.04 us
    ppermute x2, starting transfers between devices, halo(): xhi = lax.ppermute(xdn, 'tile', ring(8, -1))  5.89 us
    ppermute x2, waiting for transfers between devices, halo(): xlo = lax.ppermute(xup, 'tile', ring(8, 1))  4.69 us
    pallas_call x1, Pallas kernels, first_inner(): pl.pallas_call(first_inner_kernel, out_shape=(block, block, block, block)...  4.1 us
    pallas_call x2, Pallas kernels, ahead(): pl.pallas_call(ahead_kernel, out_shape=box, in_specs=[ANY] + [VMEM] * 5,...  3.33 us
  transfers between devices with their start and end apart: 20, of which 9 were waited for; matrix products, arithmetic and copies ran while one was open for 0% of the time, Pallas kernels for 14%

profile of v2, /device:TPU:0, one launch (start us, length us, event | category | flops | bytes accessed | tf_op | source)
XLA Modules:
  0.0 85.8 jit_solution(296631528271267987)
XLA Ops:
  0.7 1.9 %edges.1 = (f32[5,64,128]{2,1,0:T(8,128)S(1)}, f32[5,64,128]{2,1,0:T(8,128)S(1)}, f32[328,128]{1,0:T(8,128)S(1)}, f32[328,128]{1,0:T(8,128)S(1)}) custom-call(f32[64,64,128]{2,1,0:T(8,128)} %p.3, f32[64,64,128]{2,1,0:T(8,128)} %q.3, f32[64,64,128]{2,1,0:T(8,128)} %c.4, f32[64,64,128]{2,1,0:T(8,128)} %a.4), custom_call_target="tpu_custom_call" | custom-call | tf_op jit(solution)/shard_map/edges/pallas_call | solution.py:99
  2.5 0.0 collective-permute-start
  2.6 2.9 %collective-permute-start.1 = (f32[5,64,128]{2,1,0:T(8,128)S(1)}, f32[5,64,128]{2,1,0:T(8,128)S(1)}, u32[]{:S(2)}, u32[]{:S(2)}) collective-permute-start(f32[5,64,128]{2,1,0:T(8,128)S(1)} %get-tuple-element.46), channel_id=1, source_target_pairs={{0,112},{16,0},{32,16},{48,32},{64,48},{80,64},{96,80},{112,96},{1... | collective-permute-start | bytes 491528 | tf_op jit(solution)/shard_map/ppermute | solution.py:805
  5.5 0.1 reshape.15
  5.6 0.1 reshape.14
  5.7 0.1 pad_add_fusion.meta
  5.8 2.7 %collective-permute-done.xlo.pxlo.exlo = f32[5,64,128]{2,1,0:T(8,128)S(1)} collective-permute-done((f32[5,64,128]{2,1,0:T(8,128)S(1)}, f32[5,64,128]{2,1,0:T(8,128)S(1)}, u32[]{:S(2)}, u32[]{:S(2)}) %collective-permute-start) | collective-permute-done | bytes 163872 | tf_op jit(solution)/shard_map/ppermute | solution.py:804
  8.5 0.6 corners.2
  9.1 2.1 %collective-permute-start.2 = (f32[328,128]{1,0:T(8,128)S(1)}, f32[328,128]{1,0:T(8,128)S(1)}, u32[]{:S(2)}, u32[]{:S(2)}) collective-permute-start(f32[328,128]{1,0:T(8,128)S(1)} %get-tuple-element.49), channel_id=1, source_target_pairs={{0,1},{1,2},{2,3},{3,4},{4,5},{5,6},{6,7},{7,8},{8,9},{9,10},{10,1... | collective-permute-start | bytes 503816 | tf_op jit(solution)/shard_map/ppermute | solution.py:807
  11.2 4.7 %collective-permute-start.3 = (f32[328,128]{1,0:T(8,128)S(1)}, f32[328,128]{1,0:T(8,128)S(1)}, u32[]{:S(2)}, u32[]{:S(2)}) collective-permute-start(f32[328,128]{1,0:T(8,128)S(1)} %get-tuple-element.50), channel_id=1, source_target_pairs={{0,15},{1,0},{2,1},{3,2},{4,3},{5,4},{6,5},{7,6},{8,7},{9,8},{10,9... | collective-permute-start | bytes 503816 | tf_op jit(solution)/shard_map/ppermute | solution.py:808
  15.9 4.1 %first_inner.1 = (f32[64,64,128]{2,1,0:T(8,128)S(1)}, f32[64,64,128]{2,1,0:T(8,128)S(1)}, f32[64,64,128]{2,1,0:T(8,128)S(1)}, f32[64,64,128]{2,1,0:T(8,128)S(1)}) custom-call(f32[64,64,128]{2,1,0:T(8,128)} %p.3, f32[64,64,128]{2,1,0:T(8,128)} %q.3, f32[64,64,128]{2,1,0:T(8,128)} %c.4, f32[64,64,128]{2,1,0:T(8,128)} %a.4), custom_call_target="tpu_custom_call" | custom-call | flops 12000000 | bytes 10000000 | tf_op jit(solution)/shard_map/first_inner/pallas_call | solution.py:216
  20.0 0.6 collective-permute-done.2.pylo.eylo
  20.6 1.6 %coarse.2 = (f32[64,64,128]{2,1,0:T(8,128)S(1)}, f32[2,2,16,128]{3,2,1,0:T(8,128)S(1)}, f32[2,2,16,128]{3,2,1,0:T(8,128)S(1)}, f32[2,2,16,128]{3,2,1,0:T(8,128)S(1)}, f32[2,2,16,128]{3,2,1,0:T(8,128)S(1)}) custom-call(s32[24]{0:T(128)S(1)} %pad_add_fusion.meta, f32[64,64,128]{2,1,0:T(8,128)S(1)} %get-tuple-element.42.p.q, ...), custom_call_target="tpu_custom_call" | custom-call | tf_op jit(solution)/shard_map/coarse/pallas_call | solution.py:388
  22.2 0.1 collective-permute-start.4
  22.3 1.6 %collective-permute-start.5 = (f32[2,2,16,128]{3,2,1,0:T(8,128)S(1)}, f32[2,2,16,128]{3,2,1,0:T(8,128)S(1)}, u32[]{:S(2)}, u32[]{:S(2)}) collective-permute-start(f32[2,2,16,128]{3,2,1,0:T(8,128)S(1)} %get-tuple-element.57), channel_id=1, source_target_pairs={{0,64},{1,65},{2,66},{3,67},{4,68},{5,69},{6,70},{7,71},{8,72},{9,... | collective-permute-start | bytes 98312 | tf_op jit(solution)/shard_map/ppermute | solution.py:815
  23.9 3.4 %collective-permute-start.6 = (f32[2,2,16,128]{3,2,1,0:T(8,128)S(1)}, f32[2,2,16,128]{3,2,1,0:T(8,128)S(1)}, u32[]{:S(2)}, u32[]{:S(2)}) collective-permute-start(f32[2,2,16,128]{3,2,1,0:T(8,128)S(1)} %get-tuple-element.58), channel_id=1, source_target_pairs={{0,65},{1,64},{2,67},{3,66},{4,69},{5,68},{6,71},{7,70},{8,73},{9,... | collective-permute-start | bytes 98312 | tf_op jit(solution)/shard_map/ppermute | solution.py:815
  27.3 1.7 %factors.1 = (f32[2,48,2304]{2,1,0:T(8,128)S(1)}, f32[2,48,2304]{2,1,0:T(8,128)S(1)}, f32[2,48,2304]{2,1,0:T(8,128)S(1)}) custom-call(f32[2,48,2304]{2,1,0:T(8,128)} %c.5, f32[2,48,2304]{2,1,0:T(8,128)} %a.5), custom_call_target="tpu_custom_call" | custom-call | flops 3000000 | bytes 4000000 | tf_op jit(solution)/shard_map/factors/pallas_call | solution.py:428
  29.1 1.7 %ahead.2.raw = f32[2,48,2304]{2,1,0:T(8,128)S(1)} custom-call(f32[2,48,2304]{2,1,0:T(8,128)S(1)} %copy-done.2, f32[2,48,2304]{2,1,0:T(8,128)S(1)} %copy-done.4, f32[2,48,2304]{2,1,0:T(8,128)S(1)} %get-tuple-element.52.one, f32[2,48,2304]{2,1,0:T(8,128)S(1)} %get-tuple-element.53.two, f32[2,48,2304]{2,1,0:T(8,128)S(1)} %get-tuple-element.54.three, ...), custom_call_target="tpu_custom_call" | custom-call | flops 5000000 | bytes 5000000 | tf_op jit(solution)/shard_map/ahead/pallas_call | solution.py:494
  30.8 4.9 %fine.2 = (f32[2,48,2304]{2,1,0:T(8,128)S(1)}, f32[2,48,2304]{2,1,0:T(8,128)S(1)}, f32[2,16,256]{2,1,0:T(8,128)S(1)}) custom-call(s32[24]{0:T(128)S(1)} %pad_add_fusion.meta, f32[2,48,2304]{2,1,0:T(8,128)S(1)} %copy-done.2, f32[2,48,2304]{2,1,0:T(8,128)S(1)} %ahead.2.raw, f32[2,48,2304]{2,1,0:T(8,128)S(1)} %get-tuple-element.52.one, ...), custom_call_target="tpu_custom_call" | custom-call | tf_op jit(solution)/shard_map/fine/pallas_call | solution.py:627
  35.7 2.9 %collective-permute-start.9 = (f32[2,16,256]{2,1,0:T(8,128)S(1)}, f32[2,16,256]{2,1,0:T(8,128)S(1)}, u32[]{:S(2)}, u32[]{:S(2)}) collective-permute-start(f32[2,16,256]{2,1,0:T(8,128)S(1)} %get-tuple-element.59.r0), channel_id=1, source_target_pairs={{0,65},{1,64},{2,67},{3,66},{4,69},{5,68},{6,71},{7,70},{8,73},{9,... | collective-permute-start | bytes 98312 | tf_op jit(solution)/shard_map/ppermute | solution.py:815
  38.6 1.6 %collective-permute-start.8 = (f32[2,16,256]{2,1,0:T(8,128)S(1)}, f32[2,16,256]{2,1,0:T(8,128)S(1)}, u32[]{:S(2)}, u32[]{:S(2)}) collective-permute-start(f32[2,16,256]{2,1,0:T(8,128)S(1)} %get-tuple-element.59.r0), channel_id=1, source_target_pairs={{0,64},{1,65},{2,66},{3,67},{4,68},{5,69},{6,70},{7,71},{8,72},{9,... | collective-permute-start | bytes 98312 | tf_op jit(solution)/shard_map/ppermute | solution.py:815
  40.2 0.6 collective-permute-start.7
  40.8 1.3 %collective-permute-done.9.r3 = f32[2,16,256]{2,1,0:T(8,128)S(1)} collective-permute-done((f32[2,16,256]{2,1,0:T(8,128)S(1)}, f32[2,16,256]{2,1,0:T(8,128)S(1)}, u32[]{:S(2)}, u32[]{:S(2)}) %collective-permute-start.9) | collective-permute-done | bytes 32800 | tf_op jit(solution)/shard_map/ppermute | solution.py:815
  42.1 1.9 %collective-permute-done.8.r2 = f32[2,16,256]{2,1,0:T(8,128)S(1)} collective-permute-done((f32[2,16,256]{2,1,0:T(8,128)S(1)}, f32[2,16,256]{2,1,0:T(8,128)S(1)}, u32[]{:S(2)}, u32[]{:S(2)}) %collective-permute-start.8) | collective-permute-done | bytes 32800 | tf_op jit(solution)/shard_map/ppermute | solution.py:815
  44.1 0.1 collective-permute-done.7.r1
  44.1 1.3 %insert.1 = (f32[64,64,128]{2,1,0:T(8,128)S(1)}, f32[2,64,128]{2,1,0:T(8,128)S(1)}, f32[2,64,128]{2,1,0:T(8,128)S(1)}, f32[136,128]{1,0:T(8,128)S(1)}, f32[136,128]{1,0:T(8,128)S(1)}) custom-call(s32[24]{0:T(128)S(1)} %pad_add_fusion.meta, f32[64,64,128]{2,1,0:T(8,128)S(1)} %get-tuple-element.51.new, f32[2,16,256]{2,1,0:T(8,128)S(1)} %get-tuple-element.59.r0, ...), custom_call_target="tpu_custom_call" | custom-call | tf_op jit(solution)/shard_map/insert/pallas_call | solution.py:704
  45.4 0.0 collective-permute-start.10
  45.4 2.9 %collective-permute-start.11 = (f32[2,64,128]{2,1,0:T(8,128)S(1)}, f32[2,64,128]{2,1,0:T(8,128)S(1)}, u32[]{:S(2)}, u32[]{:S(2)}) collective-permute-start(f32[2,64,128]{2,1,0:T(8,128)S(1)} %get-tuple-element.64), channel_id=1, source_target_pairs={{0,112},{16,0},{32,16},{48,32},{64,48},{80,64},{96,80},{112,96},{1... | collective-permute-start | bytes 196616 | tf_op jit(solution)/shard_map/ppermute | solution.py:805
  48.4 1.9 %collective-permute-done.10.xlo.pxlo = f32[2,64,128]{2,1,0:T(8,128)S(1)} collective-permute-done((f32[2,64,128]{2,1,0:T(8,128)S(1)}, f32[2,64,128]{2,1,0:T(8,128)S(1)}, u32[]{:S(2)}, u32[]{:S(2)}) %collective-permute-start.10) | collective-permute-done | bytes 65568 | tf_op jit(solution)/shard_map/ppermute | solution.py:804
  50.3 0.6 corners.3
  50.9 0.7 collective-permute-start.12
  51.6 5.1 %collective-permute-start.13 = (f32[136,128]{1,0:T(8,128)S(1)}, f32[136,128]{1,0:T(8,128)S(1)}, u32[]{:S(2)}, u32[]{:S(2)}) collective-permute-start(f32[136,128]{1,0:T(8,128)S(1)} %get-tuple-element.68), channel_id=1, source_target_pairs={{0,15},{1,0},{2,1},{3,2},{4,3},{5,4},{6,5},{7,6},{8,7},{9,8},{10,9... | collective-permute-start | bytes 208904 | tf_op jit(solution)/shard_map/ppermute | solution.py:808
  56.7 1.9 %second_inner.1 = (f32[64,64,128]{2,1,0:T(8,128)S(1)}, f32[64,64,128]{2,1,0:T(8,128)}) custom-call(f32[64,64,128]{2,1,0:T(8,128)S(1)} %get-tuple-element.60.p, f32[64,64,128]{2,1,0:T(8,128)S(1)} %get-tuple-element.42.p.q, f32[64,64,128]{2,1,0:T(8,128)S(1)} %get-tuple-element.61.two, f32[64,64,128]{2,1,0:T(8,128)S(1)} %get-tuple-element.44.weight.side), custom_call_target="tpu_custom_call" | custom-call | flops 12000000 | bytes 8000000 | tf_op jit(solution)/shard_map/second_inner/pallas_call | solution.py:255
  58.6 0.4 collective-permute-done.12.pylo
  59.0 1.6 %coarse.3 = (f32[64,64,128]{2,1,0:T(8,128)S(1)}, f32[2,2,16,128]{3,2,1,0:T(8,128)S(1)}, f32[2,2,16,128]{3,2,1,0:T(8,128)S(1)}, f32[2,2,16,128]{3,2,1,0:T(8,128)S(1)}, f32[2,2,16,128]{3,2,1,0:T(8,128)S(1)}) custom-call(s32[24]{0:T(128)S(1)} %pad_add_fusion.meta, f32[64,64,128]{2,1,0:T(8,128)S(1)} %get-tuple-element.60.p, ...), custom_call_target="tpu_custom_call" | custom-call | tf_op jit(solution)/shard_map/coarse/pallas_call | solution.py:388
  60.6 0.1 collective-permute-start.14
  60.7 0.5 collective-permute-start.15
  61.1 4.5 %collective-permute-start.16 = (f32[2,2,16,128]{3,2,1,0:T(8,128)S(1)}, f32[2,2,16,128]{3,2,1,0:T(8,128)S(1)}, u32[]{:S(2)}, u32[]{:S(2)}) collective-permute-start(f32[2,2,16,128]{3,2,1,0:T(8,128)S(1)} %get-tuple-element.75), channel_id=1, source_target_pairs={{0,65},{1,64},{2,67},{3,66},{4,69},{5,68},{6,71},{7,70},{8,73},{9,... | collective-permute-start | bytes 98312 | tf_op jit(solution)/shard_map/ppermute | solution.py:815
  65.6 1.6 %ahead.3.raw = f32[2,48,2304]{2,1,0:T(8,128)S(1)} custom-call(f32[2,48,2304]{2,1,0:T(8,128)S(1)} %get-tuple-element.70.f, f32[2,48,2304]{2,1,0:T(8,128)S(1)} %get-tuple-element.71.g, f32[2,48,2304]{2,1,0:T(8,128)S(1)} %get-tuple-element.52.one, f32[2,48,2304]{2,1,0:T(8,128)S(1)} %get-tuple-element.53.two, f32[2,48,2304]{2,1,0:T(8,128)S(1)} %get-tuple-element.54.three, ...), custom_call_target="tpu_custom_call" | custom-call | flops 5000000 | bytes 5000000 | tf_op jit(solution)/shard_map/ahead/pallas_call | solution.py:494
  67.3 0.8 collective-permute-done.16.r3
  68.1 5.5 %fine.3 = (f32[2,48,2304]{2,1,0:T(8,128)}, f32[2,48,2304]{2,1,0:T(8,128)}, f32[2,16,256]{2,1,0:T(8,128)S(1)}) custom-call(s32[24]{0:T(128)S(1)} %pad_add_fusion.meta, f32[2,48,2304]{2,1,0:T(8,128)S(1)} %get-tuple-element.70.f, f32[2,48,2304]{2,1,0:T(8,128)S(1)} %ahead.3.raw, f32[2,48,2304]{2,1,0:T(8,128)S(1)} %get-tuple-element.52.one, ...), custom_call_target="tpu_custom_call" | custom-call | tf_op jit(solution)/shard_map/fine/pallas_call | solution.py:627
  73.6 3.9 %collective-permute-start.19 = (f32[2,16,256]{2,1,0:T(8,128)S(1)}, f32[2,16,256]{2,1,0:T(8,128)S(1)}, u32[]{:S(2)}, u32[]{:S(2)}) collective-permute-start(f32[2,16,256]{2,1,0:T(8,128)S(1)} %get-tuple-element.76.r0), channel_id=1, source_target_pairs={{0,65},{1,64},{2,67},{3,66},{4,69},{5,68},{6,71},{7,70},{8,73},{9,... | collective-permute-start | bytes 98312 | tf_op jit(solution)/shard_map/ppermute | solution.py:815
  77.6 0.4 collective-permute-start.18
  78.0 0.7 collective-permute-start.17
  78.7 1.3 %emit.1.new = f32[64,64,128]{2,1,0:T(8,128)} custom-call(f32[64,64,128]{2,1,0:T(8,128)S(1)} %get-tuple-element.69.new), custom_call_target="tpu_custom_call" | custom-call | bytes 6000000 | tf_op jit(solution)/shard_map/emit/pallas_call | solution.py:722
  80.0 0.0 collective-permute-done.19.r3
  80.1 2.9 %collective-permute-done.18.r2 = f32[2,16,256]{2,1,0:T(8,128)S(1)} collective-permute-done((f32[2,16,256]{2,1,0:T(8,128)S(1)}, f32[2,16,256]{2,1,0:T(8,128)S(1)}, u32[]{:S(2)}, u32[]{:S(2)}) %collective-permute-start.18) | collective-permute-done | bytes 32800 | tf_op jit(solution)/shard_map/ppermute | solution.py:815
  83.0 2.6 %finish.1 = f32[64,64,128]{2,1,0:T(8,128)} custom-call(s32[24]{0:T(128)S(1)} %pad_add_fusion.meta, f32[64,64,128]{2,1,0:T(8,128)} %emit.1.new, f32[2,16,256]{2,1,0:T(8,128)S(1)} %get-tuple-element.76.r0, f32[2,16,256]{2,1,0:T(8,128)S(1)} %collective-permute-done.17.r1, f32[2,16,256]{2,1,0:T(8,128)S(1)} %collective-permute-done.18.r2, ...), custom_call_target="tpu_custom_call", output_to_operand_aliasing={{}: (1, {})} | custom-call | tf_op jit(solution)/shard_map/finish/pallas_call | solution.py:783
  (26 shorter events, 0.1 us)
Async XLA Ops:
  0.6 4.9 %copy-start.7 = (s32[2,3]{1,0:T(2,128)S(1)}, s32[2,3]{1,0:T(2,128)}, u32[]{:S(2)}) copy-start(s32[2,3]{1,0:T(2,128)} %param.22) | copy-start | bytes 76
  0.6 5.0 %copy-start.6 = (s32[1,4,4]{2,1,0:T(4,128)S(1)}, s32[1,4,4]{2,1,0:T(4,128)}, u32[]{:S(2)}) copy-start(s32[1,4,4]{2,1,0:T(4,128)} %param.23) | copy-start | bytes 196
  2.5 6.0 %collective-permute-start = (f32[5,64,128]{2,1,0:T(8,128)S(1)}, f32[5,64,128]{2,1,0:T(8,128)S(1)}, u32[]{:S(2)}, u32[]{:S(2)}) collective-permute-start(f32[5,64,128]{2,1,0:T(8,128)S(1)} %get-tuple-element.45), channel_id=1, source_target_pairs={{0,16},{16,32},{32,48},{48,64},{64,80},{80,96},{96,112},{112,0},{1... | collective-permute-start | bytes 491528 | tf_op jit(solution)/shard_map/ppermute | solution.py:804
  2.6 5.9 %collective-permute-start.1 = (f32[5,64,128]{2,1,0:T(8,128)S(1)}, f32[5,64,128]{2,1,0:T(8,128)S(1)}, u32[]{:S(2)}, u32[]{:S(2)}) collective-permute-start(f32[5,64,128]{2,1,0:T(8,128)S(1)} %get-tuple-element.46), channel_id=1, source_target_pairs={{0,112},{16,0},{32,16},{48,32},{64,48},{80,64},{96,80},{112,96},{1... | collective-permute-start | bytes 491528 | tf_op jit(solution)/shard_map/ppermute | solution.py:805
  9.1 11.5 %collective-permute-start.2 = (f32[328,128]{1,0:T(8,128)S(1)}, f32[328,128]{1,0:T(8,128)S(1)}, u32[]{:S(2)}, u32[]{:S(2)}) collective-permute-start(f32[328,128]{1,0:T(8,128)S(1)} %get-tuple-element.49), channel_id=1, source_target_pairs={{0,1},{1,2},{2,3},{3,4},{4,5},{5,6},{6,7},{7,8},{8,9},{9,10},{10,1... | collective-permute-start | bytes 503816 | tf_op jit(solution)/shard_map/ppermute | solution.py:807
  11.2 9.4 %collective-permute-start.3 = (f32[328,128]{1,0:T(8,128)S(1)}, f32[328,128]{1,0:T(8,128)S(1)}, u32[]{:S(2)}, u32[]{:S(2)}) collective-permute-start(f32[328,128]{1,0:T(8,128)S(1)} %get-tuple-element.50), channel_id=1, source_target_pairs={{0,15},{1,0},{2,1},{3,2},{4,3},{5,4},{6,5},{7,6},{8,7},{9,8},{10,9... | collective-permute-start | bytes 503816 | tf_op jit(solution)/shard_map/ppermute | solution.py:808
  20.6 8.4 %copy-start.3 = (f32[2,8,2304]{2,1,0:T(8,128)S(1)}, f32[2,8,2304]{2,1,0:T(8,128)}, u32[]{:S(2)}) copy-start(f32[2,8,2304]{2,1,0:T(8,128)} %constant.17.clone.masks) | copy-start | bytes 442372
  22.2 6.8 %copy-start.2 = (f32[2,48,2304]{2,1,0:T(8,128)S(1)}, f32[2,48,2304]{2,1,0:T(8,128)}, u32[]{:S(2)}) copy-start(f32[2,48,2304]{2,1,0:T(8,128)} %f.3) | copy-start | bytes 2654212
  22.2 6.8 %copy-start.4 = (f32[2,48,2304]{2,1,0:T(8,128)S(1)}, f32[2,48,2304]{2,1,0:T(8,128)}, u32[]{:S(2)}) copy-start(f32[2,48,2304]{2,1,0:T(8,128)} %g.1) | copy-start | bytes 2654212
  22.2 8.5 %collective-permute-start.4 = (f32[2,2,16,128]{3,2,1,0:T(8,128)S(1)}, f32[2,2,16,128]{3,2,1,0:T(8,128)S(1)}, u32[]{:S(2)}, u32[]{:S(2)}) collective-permute-start(f32[2,2,16,128]{3,2,1,0:T(8,128)S(1)} %get-tuple-element.56), channel_id=1, source_target_pairs={{0,1},{1,0},{2,3},{3,2},{4,5},{5,4},{6,7},{7,6},{8,9},{9,8},{10,11... | collective-permute-start | bytes 98312 | tf_op jit(solution)/shard_map/ppermute | solution.py:815
  22.3 8.4 %collective-permute-start.5 = (f32[2,2,16,128]{3,2,1,0:T(8,128)S(1)}, f32[2,2,16,128]{3,2,1,0:T(8,128)S(1)}, u32[]{:S(2)}, u32[]{:S(2)}) collective-permute-start(f32[2,2,16,128]{3,2,1,0:T(8,128)S(1)} %get-tuple-element.57), channel_id=1, source_target_pairs={{0,64},{1,65},{2,66},{3,67},{4,68},{5,69},{6,70},{7,71},{8,72},{9,... | collective-permute-start | bytes 98312 | tf_op jit(solution)/shard_map/ppermute | solution.py:815
  23.9 6.8 %collective-permute-start.6 = (f32[2,2,16,128]{3,2,1,0:T(8,128)S(1)}, f32[2,2,16,128]{3,2,1,0:T(8,128)S(1)}, u32[]{:S(2)}, u32[]{:S(2)}) collective-permute-start(f32[2,2,16,128]{3,2,1,0:T(8,128)S(1)} %get-tuple-element.58), channel_id=1, source_target_pairs={{0,65},{1,64},{2,67},{3,66},{4,69},{5,68},{6,71},{7,70},{8,73},{9,... | collective-permute-start | bytes 98312 | tf_op jit(solution)/shard_map/ppermute | solution.py:815
  29.0 1.8 %copy-start = (bf16[2304,256]{1,0:T(8,128)(2,1)S(1)}, bf16[2304,256]{1,0:T(8,128)(2,1)}, u32[]{:S(2)}) copy-start(bf16[2304,256]{1,0:T(8,128)(2,1)} %constant.20.clone.pool) | copy-start | bytes 3538948
  29.0 1.8 %copy-start.1 = (bf16[256,2304]{1,0:T(8,128)(2,1)S(1)}, bf16[256,2304]{1,0:T(8,128)(2,1)}, u32[]{:S(2)}) copy-start(bf16[256,2304]{1,0:T(8,128)(2,1)} %constant.18.clone.spread) | copy-start | bytes 3538948
  29.1 1.8 %copy-start.5 = (f32[16,2304]{1,0:T(8,128)S(1)}, f32[16,2304]{1,0:T(8,128)}, u32[]{:S(2)}) copy-start(f32[16,2304]{1,0:T(8,128)} %constant.19.clone.pick) | copy-start | bytes 442372
  35.7 6.4 %collective-permute-start.9 = (f32[2,16,256]{2,1,0:T(8,128)S(1)}, f32[2,16,256]{2,1,0:T(8,128)S(1)}, u32[]{:S(2)}, u32[]{:S(2)}) collective-permute-start(f32[2,16,256]{2,1,0:T(8,128)S(1)} %get-tuple-element.59.r0), channel_id=1, source_target_pairs={{0,65},{1,64},{2,67},{3,66},{4,69},{5,68},{6,71},{7,70},{8,73},{9,... | collective-permute-start | bytes 98312 | tf_op jit(solution)/shard_map/ppermute | solution.py:815
  38.6 5.4 %collective-permute-start.8 = (f32[2,16,256]{2,1,0:T(8,128)S(1)}, f32[2,16,256]{2,1,0:T(8,128)S(1)}, u32[]{:S(2)}, u32[]{:S(2)}) collective-permute-start(f32[2,16,256]{2,1,0:T(8,128)S(1)} %get-tuple-element.59.r0), channel_id=1, source_target_pairs={{0,64},{1,65},{2,66},{3,67},{4,68},{5,69},{6,70},{7,71},{8,72},{9,... | collective-permute-start | bytes 98312 | tf_op jit(solution)/shard_map/ppermute | solution.py:815
  40.2 3.9 %collective-permute-start.7 = (f32[2,16,256]{2,1,0:T(8,128)S(1)}, f32[2,16,256]{2,1,0:T(8,128)S(1)}, u32[]{:S(2)}, u32[]{:S(2)}) collective-permute-start(f32[2,16,256]{2,1,0:T(8,128)S(1)} %get-tuple-element.59.r0), channel_id=1, source_target_pairs={{0,1},{1,0},{2,3},{3,2},{4,5},{5,4},{6,7},{7,6},{8,9},{9,8},{10,11... | collective-permute-start | bytes 98312 | tf_op jit(solution)/shard_map/ppermute | solution.py:815
  45.4 4.9 %collective-permute-start.10 = (f32[2,64,128]{2,1,0:T(8,128)S(1)}, f32[2,64,128]{2,1,0:T(8,128)S(1)}, u32[]{:S(2)}, u32[]{:S(2)}) collective-permute-start(f32[2,64,128]{2,1,0:T(8,128)S(1)} %get-tuple-element.63), channel_id=1, source_target_pairs={{0,16},{16,32},{32,48},{48,64},{64,80},{80,96},{96,112},{112,0},{1... | collective-permute-start | bytes 196616 | tf_op jit(solution)/shard_map/ppermute | solution.py:804
  45.4 4.9 %collective-permute-start.11 = (f32[2,64,128]{2,1,0:T(8,128)S(1)}, f32[2,64,128]{2,1,0:T(8,128)S(1)}, u32[]{:S(2)}, u32[]{:S(2)}) collective-permute-start(f32[2,64,128]{2,1,0:T(8,128)S(1)} %get-tuple-element.64), channel_id=1, source_target_pairs={{0,112},{16,0},{32,16},{48,32},{64,48},{80,64},{96,80},{112,96},{1... | collective-permute-start | bytes 196616 | tf_op jit(solution)/shard_map/ppermute | solution.py:805
  50.9 8.1 %collective-permute-start.12 = (f32[136,128]{1,0:T(8,128)S(1)}, f32[136,128]{1,0:T(8,128)S(1)}, u32[]{:S(2)}, u32[]{:S(2)}) collective-permute-start(f32[136,128]{1,0:T(8,128)S(1)} %get-tuple-element.67), channel_id=1, source_target_pairs={{0,1},{1,2},{2,3},{3,4},{4,5},{5,6},{6,7},{7,8},{8,9},{9,10},{10,1... | collective-permute-start | bytes 208904 | tf_op jit(solution)/shard_map/ppermute | solution.py:807
  51.6 7.4 %collective-permute-start.13 = (f32[136,128]{1,0:T(8,128)S(1)}, f32[136,128]{1,0:T(8,128)S(1)}, u32[]{:S(2)}, u32[]{:S(2)}) collective-permute-start(f32[136,128]{1,0:T(8,128)S(1)} %get-tuple-element.68), channel_id=1, source_target_pairs={{0,15},{1,0},{2,1},{3,2},{4,3},{5,4},{6,5},{7,6},{8,7},{9,8},{10,9... | collective-permute-start | bytes 208904 | tf_op jit(solution)/shard_map/ppermute | solution.py:808
  60.6 6.7 %collective-permute-start.14 = (f32[2,2,16,128]{3,2,1,0:T(8,128)S(1)}, f32[2,2,16,128]{3,2,1,0:T(8,128)S(1)}, u32[]{:S(2)}, u32[]{:S(2)}) collective-permute-start(f32[2,2,16,128]{3,2,1,0:T(8,128)S(1)} %get-tuple-element.73), channel_id=1, source_target_pairs={{0,1},{1,0},{2,3},{3,2},{4,5},{5,4},{6,7},{7,6},{8,9},{9,8},{10,11... | collective-permute-start | bytes 98312 | tf_op jit(solution)/shard_map/ppermute | solution.py:815
  60.7 6.7 %collective-permute-start.15 = (f32[2,2,16,128]{3,2,1,0:T(8,128)S(1)}, f32[2,2,16,128]{3,2,1,0:T(8,128)S(1)}, u32[]{:S(2)}, u32[]{:S(2)}) collective-permute-start(f32[2,2,16,128]{3,2,1,0:T(8,128)S(1)} %get-tuple-element.74), channel_id=1, source_target_pairs={{0,64},{1,65},{2,66},{3,67},{4,68},{5,69},{6,70},{7,71},{8,72},{9,... | collective-permute-start | bytes 98312 | tf_op jit(solution)/shard_map/ppermute | solution.py:815
  61.1 7.0 %collective-permute-start.16 = (f32[2,2,16,128]{3,2,1,0:T(8,128)S(1)}, f32[2,2,16,128]{3,2,1,0:T(8,128)S(1)}, u32[]{:S(2)}, u32[]{:S(2)}) collective-permute-start(f32[2,2,16,128]{3,2,1,0:T(8,128)S(1)} %get-tuple-element.75), channel_id=1, source_target_pairs={{0,65},{1,64},{2,67},{3,66},{4,69},{5,68},{6,71},{7,70},{8,73},{9,... | collective-permute-start | bytes 98312 | tf_op jit(solution)/shard_map/ppermute | solution.py:815
  73.6 6.4 %collective-permute-start.19 = (f32[2,16,256]{2,1,0:T(8,128)S(1)}, f32[2,16,256]{2,1,0:T(8,128)S(1)}, u32[]{:S(2)}, u32[]{:S(2)}) collective-permute-start(f32[2,16,256]{2,1,0:T(8,128)S(1)} %get-tuple-element.76.r0), channel_id=1, source_target_pairs={{0,65},{1,64},{2,67},{3,66},{4,69},{5,68},{6,71},{7,70},{8,73},{9,... | collective-permute-start | bytes 98312 | tf_op jit(solution)/shard_map/ppermute | solution.py:815
  77.6 5.4 %collective-permute-start.18 = (f32[2,16,256]{2,1,0:T(8,128)S(1)}, f32[2,16,256]{2,1,0:T(8,128)S(1)}, u32[]{:S(2)}, u32[]{:S(2)}) collective-permute-start(f32[2,16,256]{2,1,0:T(8,128)S(1)} %get-tuple-element.76.r0), channel_id=1, source_target_pairs={{0,64},{1,65},{2,66},{3,67},{4,68},{5,69},{6,70},{7,71},{8,72},{9,... | collective-permute-start | bytes 98312 | tf_op jit(solution)/shard_map/ppermute | solution.py:815
  78.0 5.0 %collective-permute-start.17 = (f32[2,16,256]{2,1,0:T(8,128)S(1)}, f32[2,16,256]{2,1,0:T(8,128)S(1)}, u32[]{:S(2)}, u32[]{:S(2)}) collective-permute-start(f32[2,16,256]{2,1,0:T(8,128)S(1)} %get-tuple-element.76.r0), channel_id=1, source_target_pairs={{0,1},{1,0},{2,3},{3,2},{4,5},{5,4},{6,7},{7,6},{8,9},{9,8},{10,11... | collective-permute-start | bytes 98312 | tf_op jit(solution)/shard_map/ppermute | solution.py:815

commit v3 on v2

--- a/solution.py
+++ b/solution.py
@@ -62,18 +62,37 @@
     return jnp.dot(left, right, preferred_element_type=F32)
 
 
-def edges_kernel(p, q, c, a, xup, xdn, yup, ydn, tiles, sem):
-    copies = []
+def x_edges_kernel(p, q, c, a, xup, xdn, sem):
+    ends = [(p.at[CX - 2 : CX], xup.at[0:2]), (p.at[0:2], xdn.at[0:2])]
+    for n, ref in enumerate((q, c, a)):
+        ends.append((ref.at[CX - 1], xup.at[n + 2]))
+        ends.append((ref.at[0], xdn.at[n + 2]))
+    copies = [pltpu.make_async_copy(*pair, sem.at[n]) for n, pair in enumerate(ends)]
+    for copy in copies:
+        copy.start()
+    for copy in copies:
+        copy.wait()
+
+
+def x_edges(p, q, c, a):
+    x = jax.ShapeDtypeStruct((5, CY, NZ), F32)
+    return pl.pallas_call(
+        x_edges_kernel,
+        out_shape=(x, x),
+        in_specs=[HBM] * 4,
+        out_specs=[VMEM] * 2,
+        scratch_shapes=[pltpu.SemaphoreType.DMA((8,))],
+        compiler_params=pltpu.CompilerParams(vmem_limit_bytes=LIMIT),
+        name="x_edges",
+    )(*[far(v) for v in (p, q, c, a)])
+
+
+def y_edges_kernel(p, q, c, a, yup, ydn, tiles, sem):
+    ends = []
     for n, ref in enumerate((p, q, c, a)):
-        if n == 0:
-            copies.append((ref.at[CX - 2 : CX], xup.at[0:2]))
-            copies.append((ref.at[0:2], xdn.at[0:2]))
-        else:
-            copies.append((ref.at[CX - 1], xup.at[n + 1]))
-            copies.append((ref.at[0], xdn.at[n + 1]))
-        copies.append((ref.at[:, CY - 8 : CY, :], tiles.at[0, n]))
-        copies.append((ref.at[:, 0:8, :], tiles.at[1, n]))
-    copies = [pltpu.make_async_copy(*ends, sem.at[n]) for n, ends in enumerate(copies)]
+        ends.append((ref.at[:, CY - 8 : CY, :], tiles.at[0, n]))
+        ends.append((ref.at[:, 0:8, :], tiles.at[1, n]))
+    copies = [pltpu.make_async_copy(*pair, sem.at[n]) for n, pair in enumerate(ends)]
     for copy in copies:
         copy.start()
     for copy in copies:
@@ -89,21 +108,21 @@
     for n in range(1, 4):
         yup[64 * (n + 1) : 64 * (n + 2), :] = plane(0, n, 7)
         ydn[64 * (n + 1) : 64 * (n + 2), :] = plane(1, n, 0)
-    yup[320:328, :] = jnp.zeros((8, 128), F32)
-    ydn[320:328, :] = jnp.zeros((8, 128), F32)
-
-
-def edges(p, q, c, a):
-    x = jax.ShapeDtypeStruct((5, CY, NZ), F32)
+    yup[320:328, :] = jnp.zeros((8, NZ), F32)
+    ydn[320:328, :] = jnp.zeros((8, NZ), F32)
+
+
+def y_edges(p, q, c, a):
     y = jax.ShapeDtypeStruct((5 * CX + 8, NZ), F32)
     return pl.pallas_call(
-        edges_kernel,
-        out_shape=(x, x, y, y),
+        y_edges_kernel,
+        out_shape=(y, y),
         in_specs=[HBM] * 4,
-        out_specs=[VMEM] * 4,
-        scratch_shapes=[pltpu.VMEM((2, 4, CX, 8, NZ), F32), pltpu.SemaphoreType.DMA((16,))],
-        compiler_params=pltpu.CompilerParams(vmem_limit_bytes=LIMIT),
-        name="edges",
+        out_specs=[VMEM] * 2,
+        scratch_shapes=[pltpu.VMEM((2, 4, CX, 8, NZ), F32), pltpu.SemaphoreType.DMA((8,))],
+        compiler_params=pltpu.CompilerParams(vmem_limit_bytes=LIMIT),
+        cost_estimate=pl.CostEstimate(flops=0, bytes_accessed=5000000, transcendentals=0),
+        name="y_edges",
     )(*[far(v) for v in (p, q, c, a)])
 
 
@@ -525,10 +544,7 @@
     ghost,
     xrow,
     faces,
-    sem,
 ):
-    copy = pltpu.make_async_copy(f, buf.at[0, :, 8:56, :], sem.at[0])
-    copy.start()
     for n, ref in enumerate((r0, r1, r2, r3)):
         faces[2 * n : 2 * n + 2] = ref[...]
 
@@ -561,37 +577,39 @@
             at = 288 + 16 * (6 * j + n)
             part = spreaded[at : at + 16] * pick[...]
             xrow[j, n : n + 1, :] = part.sum(axis=0, keepdims=True)
-    copy.wait()
 
     def first(j):
         for i in range(6):
             s = slice(8 * i, 8 * i + 8)
-            buf[1, j, 8 + 8 * i : 16 + 8 * i, :] = raw[j, s, :] + three[j, s, :] * ghost[0, j, s, :]
+            buf[0, j, 8 + 8 * i : 16 + 8 * i, :] = raw[j, s, :] + three[j, s, :] * ghost[0, j, s, :]
         for n, x in ((0, 0), (1, FINE - 1)):
-            buf[1, j, 8 + x : 9 + x, :] = (
-                buf[1, j, 8 + x : 9 + x, :] + three[j, x : x + 1, :] * xrow[j, n : n + 1, :]
+            buf[0, j, 8 + x : 9 + x, :] = (
+                buf[0, j, 8 + x : 9 + x, :] + three[j, x : x + 1, :] * xrow[j, n : n + 1, :]
             )
 
     def substep(m, j):
-        now, old = m % 2, 1 - m % 2
-        buf[now, j, 7:8, :] = xrow[j, 2 * m : 2 * m + 1, :]
-        buf[now, j, 56:57, :] = xrow[j, 2 * m + 1 : 2 * m + 2, :]
+        buf[m - 1, j, 7:8, :] = xrow[j, 2 * m : 2 * m + 1, :]
+        buf[m - 1, j, 56:57, :] = xrow[j, 2 * m + 1 : 2 * m + 2, :]
         for i in range(6):
             s = slice(8 * i, 8 * i + 8)
+            pad = slice(8 + 8 * i, 16 + 8 * i)
 
             def row(k):
-                return buf[now, j, 8 + 8 * i : 16 + 8 * i, 128 * k : 128 * k + 128]
+                return buf[m - 1, j, pad, 128 * k : 128 * k + 128]
 
             for ls, cur, total in beside_in_plane(row, masks):
                 total = total + ghost[m, j, s, ls]
                 total = total + (
-                    buf[now, j, 7 + 8 * i : 15 + 8 * i, ls] + buf[now, j, 9 + 8 * i : 17 + 8 * i, ls]
+                    buf[m - 1, j, 7 + 8 * i : 15 + 8 * i, ls]
+                    + buf[m - 1, j, 9 + 8 * i : 17 + 8 * i, ls]
                 )
-                buf[old, j, 8 + 8 * i : 16 + 8 * i, ls] = (
-                    one[j, s, ls] * cur
-                    + two[j, s, ls] * buf[old, j, 8 + 8 * i : 16 + 8 * i, ls]
-                    + three[j, s, ls] * total
-                )
+                old = f[j, s, ls] if m == 1 else buf[0, j, pad, ls]
+                value = one[j, s, ls] * cur + two[j, s, ls] * old + three[j, s, ls] * total
+                if m == 1:
+                    buf[1, j, pad, ls] = value
+                    g_out[j, s, ls] = value
+                else:
+                    f_out[j, s, ls] = value
 
     def box(j, carry):
         first(j)
@@ -600,16 +618,10 @@
         return carry
 
     lax.fori_loop(0, 2, box, 0)
-    stores = [
-        pltpu.make_async_copy(buf.at[1, :, 8:56, :], f_out, sem.at[0]),
-        pltpu.make_async_copy(buf.at[0, :, 8:56, :], g_out, sem.at[1]),
-    ]
-    for copy in stores:
-        copy.start()
     tall = lax.broadcasted_iota(jnp.int32, (BC, FINE), 1)
     wide = lax.broadcasted_iota(jnp.int32, (BC, FINE), 0)
     gather = jnp.where((tall >= 3 * wide) & (tall < 3 * wide + 3), 1.0, 0.0).astype(BF16)
-    parts = [part for j in range(2) for part in split(buf[1, j, 8:56, :])]
+    parts = [part for j in range(2) for part in split(f_out[j])]
     pooled = dot(jnp.concatenate(parts, axis=0), pool[...])
     parts = []
     for j in range(2):
@@ -618,8 +630,6 @@
     for j in range(2):
         at = 512 * j
         res[j] = (means[:, at : at + 256] + means[:, at + 256 : at + 512]) * (1.0 / 27.0)
-    for copy in stores:
-        copy.wait()
 
 
 def fine(meta, f, raw, weights, received, consts):
@@ -627,14 +637,13 @@
     return pl.pallas_call(
         fine_kernel,
         out_shape=(box, box, jax.ShapeDtypeStruct((2, BC, BC * BC), F32)),
-        in_specs=[SMEM, ANY] + [VMEM] * 12,
-        out_specs=[ANY, ANY, VMEM],
+        in_specs=[SMEM] + [VMEM] * 13,
+        out_specs=[VMEM] * 3,
         scratch_shapes=[
             pltpu.VMEM((2, 2, 64, PLANE), F32),
             pltpu.VMEM((3, 2, FINE, PLANE), F32),
             pltpu.VMEM((2, 8, PLANE), F32),
             pltpu.VMEM((8, 2, BC, NZ), F32),
-            pltpu.SemaphoreType.DMA((2,)),
         ],
         compiler_params=pltpu.CompilerParams(vmem_limit_bytes=LIMIT),
         name="fine",
@@ -712,28 +721,36 @@
     )(meta, new, *received)
 
 
-def emit_kernel(new, out, sem):
-    copy = pltpu.make_async_copy(new, out, sem)
-    copy.start()
-    copy.wait()
-
-
-def emit(new):
+def emit_kernel(new, f, g, new_out, f_out, g_out, sem):
+    ends = ((new, new_out), (f, f_out), (g, g_out))
+    copies = [pltpu.make_async_copy(*pair, sem.at[n]) for n, pair in enumerate(ends)]
+    for copy in copies:
+        copy.start()
+    for copy in copies:
+        copy.wait()
+
+
+def emit(new, f, g):
+    box = jax.ShapeDtypeStruct((2, FINE, PLANE), F32)
     return pl.pallas_call(
         emit_kernel,
-        out_shape=jax.ShapeDtypeStruct(BLOCK, F32),
-        in_specs=[VMEM],
-        out_specs=HBM,
-        scratch_shapes=[pltpu.SemaphoreType.DMA],
-        compiler_params=pltpu.CompilerParams(vmem_limit_bytes=LIMIT),
-        cost_estimate=pl.CostEstimate(flops=0, bytes_accessed=6000000, transcendentals=0),
+        out_shape=(jax.ShapeDtypeStruct(BLOCK, F32), box, box),
+        in_specs=[VMEM] * 3,
+        out_specs=[HBM] * 3,
+        scratch_shapes=[pltpu.SemaphoreType.DMA((3,))],
+        compiler_params=pltpu.CompilerParams(vmem_limit_bytes=LIMIT),
+        cost_estimate=pl.CostEstimate(flops=0, bytes_accessed=9000000, transcendentals=0),
         name="emit",
-    )(new)
-
-
-def finish_kernel(meta, new, r0, r1, r2, r3, out, got, boxes, sem):
+    )(new, f, g)
+
+
+def finish_kernel(meta, new, written, r0, r1, r2, r3, out, got, boxes, sem):
     def region(k):
-        return out.at[pl.ds(meta[4 + k], BC), pl.ds(pl.multiple_of(meta[8 + k], 16), BC), :]
+        return pl.ds(meta[4 + k], BC), pl.ds(pl.multiple_of(meta[8 + k], 16), BC)
+
+    def store(k):
+        x, y = region(k)
+        return pltpu.make_async_copy(boxes.at[k], out.at[x, y, :], sem.at[k])
 
     slots = []
     for k in range(MOST):
@@ -742,50 +759,45 @@
             same = (meta[4 + n] == meta[4 + k]) & (meta[8 + n] == meta[8 + k]) & (meta[n] >= 0)
             slot = jnp.where(same, n, slot)
         slots.append(slot)
-    valid = [meta[k] >= 0 for k in range(MOST)]
-    leads = [valid[k] & (slots[k] == k) for k in range(MOST)]
-    for k in range(MOST):
-
-        @pl.when(leads[k])
-        def _():
-            pltpu.make_async_copy(region(k), boxes.at[k], sem.at[k]).start()
-
     for n, ref in enumerate((r0, r1, r2, r3)):
         got[2 * n : 2 * n + 2] = ref[...]
     lane = lax.broadcasted_iota(jnp.int32, (BC, BC, NZ), 2)
     iotas = box_iotas()
     for k in range(MOST):
 
-        @pl.when(leads[k])
+        @pl.when(meta[k] >= 0)
         def _():
-            pltpu.make_async_copy(region(k), boxes.at[k], sem.at[k]).wait()
-
-        @pl.when(valid[k])
-        def _():
+            slot = slots[k]
+
+            @pl.when(slot == k)
+            def _():
+                x, y = region(k)
+                boxes[k] = new[x, y, :]
+
             moved = moved_box(meta, got, k, *iotas)
             oz = meta[12 + k]
-            boxes[slots[k]] = jnp.where((lane >= oz) & (lane < oz + BC), moved, boxes[slots[k]])
+            boxes[slot] = jnp.where((lane >= oz) & (lane < oz + BC), moved, boxes[slot])
 
     for k in range(MOST):
 
-        @pl.when(leads[k])
+        @pl.when((meta[k] >= 0) & (slots[k] == k))
         def _():
-            pltpu.make_async_copy(boxes.at[k], region(k), sem.at[k]).start()
+            store(k).start()
 
     for k in range(MOST):
 
-        @pl.when(leads[k])
+        @pl.when((meta[k] >= 0) & (slots[k] == k))
         def _():
-            pltpu.make_async_copy(boxes.at[k], region(k), sem.at[k]).wait()
-
-
-def finish(meta, new, received):
+            store(k).wait()
+
+
+def finish(meta, new, written, received):
     return pl.pallas_call(
         finish_kernel,
         out_shape=jax.ShapeDtypeStruct(BLOCK, F32),
-        in_specs=[SMEM, ANY] + [VMEM] * 4,
+        in_specs=[SMEM, VMEM, ANY] + [VMEM] * 4,
         out_specs=ANY,
-        input_output_aliases={1: 0},
+        input_output_aliases={2: 0},
         scratch_shapes=[
             pltpu.VMEM((8, BC, BC * BC), F32),
             pltpu.VMEM((MOST, BC, BC, NZ), F32),
@@ -793,7 +805,7 @@
         ],
         compiler_params=pltpu.CompilerParams(vmem_limit_bytes=LIMIT),
         name="finish",
-    )(meta, new, *received)
+    )(meta, new, written, *received)
 
 
 def ring(size, by):
@@ -831,10 +843,11 @@
     place = jnp.stack([lax.axis_index("tile"), lax.axis_index("bulk")]).astype(jnp.int32)
     meta = jnp.concatenate([intersection.reshape(16), box_anchor.reshape(6), place])
     consts = tables()
-    extras = halo(meta, *edges(coarse_now, coarse_before, coarse_courant, coarse_absorb))
+    inputs = (coarse_now, coarse_before, coarse_courant, coarse_absorb)
+    extras = halo(meta, *x_edges(*inputs), *y_edges(*inputs))
     weights = factors(fine_courant, fine_absorb)
     first = ahead(fine_now, fine_before, weights, consts[0])
-    raw, two, side, start = first_inner(coarse_now, coarse_before, coarse_courant, coarse_absorb)
+    raw, two, side, start = first_inner(*inputs)
     new, *faces = coarse(True, meta, start, raw, side, extras, extras)
     f, g, res = fine(meta, fine_now, first, weights, trade(faces), consts)
     middle, *packed = insert(meta, new, trade([res] * 4))
@@ -843,7 +856,8 @@
     raw, q = second_inner(middle, start, two, side)
     new, *faces = coarse(False, meta, middle, raw, side, halos, extras)
     f, g, res = fine(meta, f, first, weights, trade(faces), consts)
-    p = finish(meta, emit(new), trade([res] * 4))
+    written, f, g = emit(new, f, g)
+    p = finish(meta, new, written, trade([res] * 4))
     return p, q, f, g
 
 

time: 86.2 us -> 82.8 us (0.961)
  waiting for transfers between devices: 12.8 us -> 10.3 us
    ppermute x2, waiting for transfers between devices: 4.69 us -> 2.98 us  [halo(): xlo = lax.ppermute(xup, 'tile', ring(8, 1))]
    pallas_call x2 -> x3, Pallas kernels: 3.22 us -> 4.58 us  [the longest x1 1.92 us: emit(): pl.pallas_call(emit_kernel, out_shape=(jax.ShapeDtypeStruct(BLOCK, F32),...]
    pallas_call x2, Pallas kernels: 10.4 us -> 9.14 us  [fine(): pl.pallas_call(fine_kernel, out_shape=(box, box, jax.ShapeDtypeStruct((2,...]
  transfers between devices with their start and end apart: 20 -> 20, of which waited for: 9 -> 8; matrix products, arithmetic and copies ran while one was open for 0% -> 0% of each run, Pallas kernels for 14% -> 18%
where the time goes in v3:
time: 82.8 us; the launch traced here: 83.2 us
  starting transfers between devices  38.4 us (46%)
  Pallas kernels  33.1 us (40%)
  waiting for transfers between devices  10.3 us (12%)
  between operations  1.09 us (1%)
    ppermute x12, starting transfers between devices, trade(): lax.ppermute(value, ('tile', 'bulk'), [(d, d ^ away) for d in range(128)])  20.1 us
    ppermute x2, starting transfers between devices, halo(): yhi = lax.ppermute(ydn, 'bulk', ring(16, -1))  9.98 us
    pallas_call x2, Pallas kernels, fine(): pl.pallas_call(fine_kernel, out_shape=(box, box, jax.ShapeDtypeStruct((2,...  9.14 us
    ppermute x12, waiting for transfers between devices, trade(): lax.ppermute(value, ('tile', 'bulk'), [(d, d ^ away) for d in range(128)])  6.4 us
    ppermute x2, starting transfers between devices, halo(): xhi = lax.ppermute(xdn, 'tile', ring(8, -1))  5.89 us
    pallas_call x1, Pallas kernels, first_inner(): pl.pallas_call(first_inner_kernel, out_shape=(block, block, block, block)...  4.1 us
    pallas_call x2, Pallas kernels, coarse(): pl.pallas_call(functools.partial(coarse_kernel, first), out_shape=(jax.Sh...  3.7 us
    pallas_call x2, Pallas kernels, ahead(): pl.pallas_call(ahead_kernel, out_shape=box, in_specs=[ANY] + [VMEM] * 5,...  3.33 us
  transfers between devices with their start and end apart: 20, of which 8 were waited for; matrix products, arithmetic and copies ran while one was open for 0% of the time, Pallas kernels for 18%

profile of v3, /device:TPU:0, one launch (start us, length us, event | category | flops | bytes accessed | tf_op | source)
XLA Modules:
  0.0 83.2 jit_solution(16243694742296366059)
XLA Ops:
  0.6 1.0 %x_edges.1 = (f32[5,64,128]{2,1,0:T(8,128)S(1)}, f32[5,64,128]{2,1,0:T(8,128)S(1)}) custom-call(f32[64,64,128]{2,1,0:T(8,128)} %p.5, f32[64,64,128]{2,1,0:T(8,128)} %q.5, f32[64,64,128]{2,1,0:T(8,128)} %c.6, f32[64,64,128]{2,1,0:T(8,128)} %a.6), custom_call_target="tpu_custom_call" | custom-call | tf_op jit(solution)/shard_map/x_edges/pallas_call | solution.py:79
  1.6 0.0 collective-permute-start
  1.6 2.9 %collective-permute-start.1 = (f32[5,64,128]{2,1,0:T(8,128)S(1)}, f32[5,64,128]{2,1,0:T(8,128)S(1)}, u32[]{:S(2)}, u32[]{:S(2)}) collective-permute-start(f32[5,64,128]{2,1,0:T(8,128)S(1)} %get-tuple-element.49), channel_id=1, source_target_pairs={{0,112},{16,0},{32,16},{48,32},{64,48},{80,64},{96,80},{112,96},{1... | collective-permute-start | bytes 491528 | tf_op jit(solution)/shard_map/ppermute | solution.py:817
  4.6 1.7 %y_edges.1 = (f32[328,128]{1,0:T(8,128)S(1)}, f32[328,128]{1,0:T(8,128)S(1)}) custom-call(f32[64,64,128]{2,1,0:T(8,128)} %p.5, f32[64,64,128]{2,1,0:T(8,128)} %q.5, f32[64,64,128]{2,1,0:T(8,128)} %c.6, f32[64,64,128]{2,1,0:T(8,128)} %a.6), custom_call_target="tpu_custom_call" | custom-call | bytes 5000000 | tf_op jit(solution)/shard_map/y_edges/pallas_call | solution.py:117
  6.3 0.1 reshape.15
  6.4 0.1 reshape.14
  6.5 0.1 pad_add_fusion.meta
  6.5 1.0 %collective-permute-done.xlo.pxlo.exlo = f32[5,64,128]{2,1,0:T(8,128)S(1)} collective-permute-done((f32[5,64,128]{2,1,0:T(8,128)S(1)}, f32[5,64,128]{2,1,0:T(8,128)S(1)}, u32[]{:S(2)}, u32[]{:S(2)}) %collective-permute-start) | collective-permute-done | bytes 163872 | tf_op jit(solution)/shard_map/ppermute | solution.py:816
  7.6 0.6 corners.2
  8.2 2.1 %collective-permute-start.2 = (f32[328,128]{1,0:T(8,128)S(1)}, f32[328,128]{1,0:T(8,128)S(1)}, u32[]{:S(2)}, u32[]{:S(2)}) collective-permute-start(f32[328,128]{1,0:T(8,128)S(1)} %get-tuple-element.52), channel_id=1, source_target_pairs={{0,1},{1,2},{2,3},{3,4},{4,5},{5,6},{6,7},{7,8},{8,9},{9,10},{10,1... | collective-permute-start | bytes 503816 | tf_op jit(solution)/shard_map/ppermute | solution.py:819
  10.3 4.7 %collective-permute-start.3 = (f32[328,128]{1,0:T(8,128)S(1)}, f32[328,128]{1,0:T(8,128)S(1)}, u32[]{:S(2)}, u32[]{:S(2)}) collective-permute-start(f32[328,128]{1,0:T(8,128)S(1)} %get-tuple-element.53), channel_id=1, source_target_pairs={{0,15},{1,0},{2,1},{3,2},{4,3},{5,4},{6,5},{7,6},{8,7},{9,8},{10,9... | collective-permute-start | bytes 503816 | tf_op jit(solution)/shard_map/ppermute | solution.py:820
  14.9 4.1 %first_inner.1 = (f32[64,64,128]{2,1,0:T(8,128)S(1)}, f32[64,64,128]{2,1,0:T(8,128)S(1)}, f32[64,64,128]{2,1,0:T(8,128)S(1)}, f32[64,64,128]{2,1,0:T(8,128)S(1)}) custom-call(f32[64,64,128]{2,1,0:T(8,128)} %p.5, f32[64,64,128]{2,1,0:T(8,128)} %q.5, f32[64,64,128]{2,1,0:T(8,128)} %c.6, f32[64,64,128]{2,1,0:T(8,128)} %a.6), custom_call_target="tpu_custom_call" | custom-call | flops 12000000 | bytes 10000000 | tf_op jit(solution)/shard_map/first_inner/pallas_call | solution.py:235
  19.0 0.6 collective-permute-done.2.pylo.eylo
  19.7 1.8 %coarse.2 = (f32[64,64,128]{2,1,0:T(8,128)S(1)}, f32[2,2,16,128]{3,2,1,0:T(8,128)S(1)}, f32[2,2,16,128]{3,2,1,0:T(8,128)S(1)}, f32[2,2,16,128]{3,2,1,0:T(8,128)S(1)}, f32[2,2,16,128]{3,2,1,0:T(8,128)S(1)}) custom-call(s32[24]{0:T(128)S(1)} %pad_add_fusion.meta, f32[64,64,128]{2,1,0:T(8,128)S(1)} %get-tuple-element.45.p.q, ...), custom_call_target="tpu_custom_call" | custom-call | tf_op jit(solution)/shard_map/coarse/pallas_call | solution.py:407
  21.5 0.1 collective-permute-start.4
  21.6 1.4 %collective-permute-start.5 = (f32[2,2,16,128]{3,2,1,0:T(8,128)S(1)}, f32[2,2,16,128]{3,2,1,0:T(8,128)S(1)}, u32[]{:S(2)}, u32[]{:S(2)}) collective-permute-start(f32[2,2,16,128]{3,2,1,0:T(8,128)S(1)} %get-tuple-element.60), channel_id=1, source_target_pairs={{0,64},{1,65},{2,66},{3,67},{4,68},{5,69},{6,70},{7,71},{8,72},{9,... | collective-permute-start | bytes 98312 | tf_op jit(solution)/shard_map/ppermute | solution.py:827
  23.0 3.6 %collective-permute-start.6 = (f32[2,2,16,128]{3,2,1,0:T(8,128)S(1)}, f32[2,2,16,128]{3,2,1,0:T(8,128)S(1)}, u32[]{:S(2)}, u32[]{:S(2)}) collective-permute-start(f32[2,2,16,128]{3,2,1,0:T(8,128)S(1)} %get-tuple-element.61), channel_id=1, source_target_pairs={{0,65},{1,64},{2,67},{3,66},{4,69},{5,68},{6,71},{7,70},{8,73},{9,... | collective-permute-start | bytes 98312 | tf_op jit(solution)/shard_map/ppermute | solution.py:827
  26.6 1.7 %factors.1 = (f32[2,48,2304]{2,1,0:T(8,128)S(1)}, f32[2,48,2304]{2,1,0:T(8,128)S(1)}, f32[2,48,2304]{2,1,0:T(8,128)S(1)}) custom-call(f32[2,48,2304]{2,1,0:T(8,128)} %c.7, f32[2,48,2304]{2,1,0:T(8,128)} %a.7), custom_call_target="tpu_custom_call" | custom-call | flops 3000000 | bytes 4000000 | tf_op jit(solution)/shard_map/factors/pallas_call | solution.py:447
  28.3 0.0 copy-start
  28.4 1.7 %ahead.2.raw = f32[2,48,2304]{2,1,0:T(8,128)S(1)} custom-call(f32[2,48,2304]{2,1,0:T(8,128)S(1)} %copy-done.2, f32[2,48,2304]{2,1,0:T(8,128)S(1)} %copy-done.4, f32[2,48,2304]{2,1,0:T(8,128)S(1)} %get-tuple-element.55.one, f32[2,48,2304]{2,1,0:T(8,128)S(1)} %get-tuple-element.56.two, f32[2,48,2304]{2,1,0:T(8,128)S(1)} %get-tuple-element.57.three, ...), custom_call_target="tpu_custom_call" | custom-call | flops 5000000 | bytes 5000000 | tf_op jit(solution)/shard_map/ahead/pallas_call | solution.py:513
  30.1 4.6 %fine.2 = (f32[2,48,2304]{2,1,0:T(8,128)S(1)}, f32[2,48,2304]{2,1,0:T(8,128)S(1)}, f32[2,16,256]{2,1,0:T(8,128)S(1)}) custom-call(s32[24]{0:T(128)S(1)} %pad_add_fusion.meta, f32[2,48,2304]{2,1,0:T(8,128)S(1)} %copy-done.2, f32[2,48,2304]{2,1,0:T(8,128)S(1)} %ahead.2.raw, f32[2,48,2304]{2,1,0:T(8,128)S(1)} %get-tuple-element.55.one, ...), custom_call_target="tpu_custom_call" | custom-call | tf_op jit(solution)/shard_map/fine/pallas_call | solution.py:637
  34.7 2.8 %collective-permute-start.9 = (f32[2,16,256]{2,1,0:T(8,128)S(1)}, f32[2,16,256]{2,1,0:T(8,128)S(1)}, u32[]{:S(2)}, u32[]{:S(2)}) collective-permute-start(f32[2,16,256]{2,1,0:T(8,128)S(1)} %get-tuple-element.62.r0), channel_id=1, source_target_pairs={{0,65},{1,64},{2,67},{3,66},{4,69},{5,68},{6,71},{7,70},{8,73},{9,... | collective-permute-start | bytes 98312 | tf_op jit(solution)/shard_map/ppermute | solution.py:827
  37.5 1.3 %collective-permute-start.8 = (f32[2,16,256]{2,1,0:T(8,128)S(1)}, f32[2,16,256]{2,1,0:T(8,128)S(1)}, u32[]{:S(2)}, u32[]{:S(2)}) collective-permute-start(f32[2,16,256]{2,1,0:T(8,128)S(1)} %get-tuple-element.62.r0), channel_id=1, source_target_pairs={{0,64},{1,65},{2,66},{3,67},{4,68},{5,69},{6,70},{7,71},{8,72},{9,... | collective-permute-start | bytes 98312 | tf_op jit(solution)/shard_map/ppermute | solution.py:827
  38.8 0.9 %collective-permute-start.7 = (f32[2,16,256]{2,1,0:T(8,128)S(1)}, f32[2,16,256]{2,1,0:T(8,128)S(1)}, u32[]{:S(2)}, u32[]{:S(2)}) collective-permute-start(f32[2,16,256]{2,1,0:T(8,128)S(1)} %get-tuple-element.62.r0), channel_id=1, source_target_pairs={{0,1},{1,0},{2,3},{3,2},{4,5},{5,4},{6,7},{7,6},{8,9},{9,8},{10,11... | collective-permute-start | bytes 98312 | tf_op jit(solution)/shard_map/ppermute | solution.py:827
  39.7 1.6 %collective-permute-done.9.r3 = f32[2,16,256]{2,1,0:T(8,128)S(1)} collective-permute-done((f32[2,16,256]{2,1,0:T(8,128)S(1)}, f32[2,16,256]{2,1,0:T(8,128)S(1)}, u32[]{:S(2)}, u32[]{:S(2)}) %collective-permute-start.9) | collective-permute-done | bytes 32800 | tf_op jit(solution)/shard_map/ppermute | solution.py:827
  41.3 1.6 %collective-permute-done.8.r2 = f32[2,16,256]{2,1,0:T(8,128)S(1)} collective-permute-done((f32[2,16,256]{2,1,0:T(8,128)S(1)}, f32[2,16,256]{2,1,0:T(8,128)S(1)}, u32[]{:S(2)}, u32[]{:S(2)}) %collective-permute-start.8) | collective-permute-done | bytes 32800 | tf_op jit(solution)/shard_map/ppermute | solution.py:827
  43.0 1.5 %insert.1 = (f32[64,64,128]{2,1,0:T(8,128)S(1)}, f32[2,64,128]{2,1,0:T(8,128)S(1)}, f32[2,64,128]{2,1,0:T(8,128)S(1)}, f32[136,128]{1,0:T(8,128)S(1)}, f32[136,128]{1,0:T(8,128)S(1)}) custom-call(s32[24]{0:T(128)S(1)} %pad_add_fusion.meta, f32[64,64,128]{2,1,0:T(8,128)S(1)} %get-tuple-element.54.new, f32[2,16,256]{2,1,0:T(8,128)S(1)} %get-tuple-element.62.r0, ...), custom_call_target="tpu_custom_call" | custom-call | tf_op jit(solution)/shard_map/insert/pallas_call | solution.py:713
  44.5 0.0 collective-permute-start.10
  44.5 2.9 %collective-permute-start.11 = (f32[2,64,128]{2,1,0:T(8,128)S(1)}, f32[2,64,128]{2,1,0:T(8,128)S(1)}, u32[]{:S(2)}, u32[]{:S(2)}) collective-permute-start(f32[2,64,128]{2,1,0:T(8,128)S(1)} %get-tuple-element.67), channel_id=1, source_target_pairs={{0,112},{16,0},{32,16},{48,32},{64,48},{80,64},{96,80},{112,96},{1... | collective-permute-start | bytes 196616 | tf_op jit(solution)/shard_map/ppermute | solution.py:817
  47.4 1.9 %collective-permute-done.10.xlo.pxlo = f32[2,64,128]{2,1,0:T(8,128)S(1)} collective-permute-done((f32[2,64,128]{2,1,0:T(8,128)S(1)}, f32[2,64,128]{2,1,0:T(8,128)S(1)}, u32[]{:S(2)}, u32[]{:S(2)}) %collective-permute-start.10) | collective-permute-done | bytes 65568 | tf_op jit(solution)/shard_map/ppermute | solution.py:816
  49.4 0.6 corners.3
  50.0 0.3 collective-permute-start.12
  50.3 5.3 %collective-permute-start.13 = (f32[136,128]{1,0:T(8,128)S(1)}, f32[136,128]{1,0:T(8,128)S(1)}, u32[]{:S(2)}, u32[]{:S(2)}) collective-permute-start(f32[136,128]{1,0:T(8,128)S(1)} %get-tuple-element.71), channel_id=1, source_target_pairs={{0,15},{1,0},{2,1},{3,2},{4,3},{5,4},{6,5},{7,6},{8,7},{9,8},{10,9... | collective-permute-start | bytes 208904 | tf_op jit(solution)/shard_map/ppermute | solution.py:820
  55.6 1.9 %second_inner.1 = (f32[64,64,128]{2,1,0:T(8,128)S(1)}, f32[64,64,128]{2,1,0:T(8,128)}) custom-call(f32[64,64,128]{2,1,0:T(8,128)S(1)} %get-tuple-element.63.p, f32[64,64,128]{2,1,0:T(8,128)S(1)} %get-tuple-element.45.p.q, f32[64,64,128]{2,1,0:T(8,128)S(1)} %get-tuple-element.64.two, f32[64,64,128]{2,1,0:T(8,128)S(1)} %get-tuple-element.47.weight.side), custom_call_target="tpu_custom_call" | custom-call | flops 12000000 | bytes 8000000 | tf_op jit(solution)/shard_map/second_inner/pallas_call | solution.py:274
  57.5 0.3 collective-permute-done.12.pylo
  57.8 1.9 %coarse.3 = (f32[64,64,128]{2,1,0:T(8,128)S(1)}, f32[2,2,16,128]{3,2,1,0:T(8,128)S(1)}, f32[2,2,16,128]{3,2,1,0:T(8,128)S(1)}, f32[2,2,16,128]{3,2,1,0:T(8,128)S(1)}, f32[2,2,16,128]{3,2,1,0:T(8,128)S(1)}) custom-call(s32[24]{0:T(128)S(1)} %pad_add_fusion.meta, f32[64,64,128]{2,1,0:T(8,128)S(1)} %get-tuple-element.63.p, ...), custom_call_target="tpu_custom_call" | custom-call | tf_op jit(solution)/shard_map/coarse/pallas_call | solution.py:407
  59.7 0.1 collective-permute-start.14
  59.8 0.8 collective-permute-start.15
  60.6 4.2 %collective-permute-start.16 = (f32[2,2,16,128]{3,2,1,0:T(8,128)S(1)}, f32[2,2,16,128]{3,2,1,0:T(8,128)S(1)}, u32[]{:S(2)}, u32[]{:S(2)}) collective-permute-start(f32[2,2,16,128]{3,2,1,0:T(8,128)S(1)} %get-tuple-element.78), channel_id=1, source_target_pairs={{0,65},{1,64},{2,67},{3,66},{4,69},{5,68},{6,71},{7,70},{8,73},{9,... | collective-permute-start | bytes 98312 | tf_op jit(solution)/shard_map/ppermute | solution.py:827
  64.7 1.6 %ahead.3.raw = f32[2,48,2304]{2,1,0:T(8,128)S(1)} custom-call(f32[2,48,2304]{2,1,0:T(8,128)S(1)} %get-tuple-element.73.f, f32[2,48,2304]{2,1,0:T(8,128)S(1)} %get-tuple-element.74.g, f32[2,48,2304]{2,1,0:T(8,128)S(1)} %get-tuple-element.55.one, f32[2,48,2304]{2,1,0:T(8,128)S(1)} %get-tuple-element.56.two, f32[2,48,2304]{2,1,0:T(8,128)S(1)} %get-tuple-element.57.three, ...), custom_call_target="tpu_custom_call" | custom-call | flops 5000000 | bytes 5000000 | tf_op jit(solution)/shard_map/ahead/pallas_call | solution.py:513
  66.4 0.6 collective-permute-done.16.r3
  67.0 4.5 %fine.3 = (f32[2,48,2304]{2,1,0:T(8,128)S(1)}, f32[2,48,2304]{2,1,0:T(8,128)S(1)}, f32[2,16,256]{2,1,0:T(8,128)S(1)}) custom-call(s32[24]{0:T(128)S(1)} %pad_add_fusion.meta, f32[2,48,2304]{2,1,0:T(8,128)S(1)} %get-tuple-element.73.f, f32[2,48,2304]{2,1,0:T(8,128)S(1)} %ahead.3.raw, f32[2,48,2304]{2,1,0:T(8,128)S(1)} %get-tuple-element.55.one, ...), custom_call_target="tpu_custom_call" | custom-call | tf_op jit(solution)/shard_map/fine/pallas_call | solution.py:637
  71.5 4.1 %collective-permute-start.19 = (f32[2,16,256]{2,1,0:T(8,128)S(1)}, f32[2,16,256]{2,1,0:T(8,128)S(1)}, u32[]{:S(2)}, u32[]{:S(2)}) collective-permute-start(f32[2,16,256]{2,1,0:T(8,128)S(1)} %get-tuple-element.82.r0), channel_id=1, source_target_pairs={{0,65},{1,64},{2,67},{3,66},{4,69},{5,68},{6,71},{7,70},{8,73},{9,... | collective-permute-start | bytes 98312 | tf_op jit(solution)/shard_map/ppermute | solution.py:827
  75.6 0.7 collective-permute-start.18
  76.4 0.2 collective-permute-start.17
  76.5 1.9 %emit.1 = (f32[64,64,128]{2,1,0:T(8,128)}, f32[2,48,2304]{2,1,0:T(8,128)}, f32[2,48,2304]{2,1,0:T(8,128)}) custom-call(f32[64,64,128]{2,1,0:T(8,128)S(1)} %get-tuple-element.72.new, f32[2,48,2304]{2,1,0:T(8,128)S(1)} %get-tuple-element.79.f, f32[2,48,2304]{2,1,0:T(8,128)S(1)} %get-tuple-element.80.g), custom_call_target="tpu_custom_call" | custom-call | bytes 9000000 | tf_op jit(solution)/shard_map/emit/pallas_call | solution.py:735
  78.5 2.6 %collective-permute-done.18.r2 = f32[2,16,256]{2,1,0:T(8,128)S(1)} collective-permute-done((f32[2,16,256]{2,1,0:T(8,128)S(1)}, f32[2,16,256]{2,1,0:T(8,128)S(1)}, u32[]{:S(2)}, u32[]{:S(2)}) %collective-permute-start.18) | collective-permute-done | bytes 32800 | tf_op jit(solution)/shard_map/ppermute | solution.py:827
  81.0 2.0 %finish.1 = f32[64,64,128]{2,1,0:T(8,128)} custom-call(s32[24]{0:T(128)S(1)} %pad_add_fusion.meta, f32[64,64,128]{2,1,0:T(8,128)S(1)} %get-tuple-element.72.new, f32[64,64,128]{2,1,0:T(8,128)} %get-tuple-element.81.written, f32[2,16,256]{2,1,0:T(8,128)S(1)} %get-tuple-element.82.r0, ...), custom_call_target="tpu_custom_call", output_to_operand_aliasing={{}: (2, {})} | custom-call | tf_op jit(solution)/shard_map/finish/pallas_call | solution.py:795
  (27 shorter events, 0.1 us)
Async XLA Ops:
  1.6 6.0 %collective-permute-start = (f32[5,64,128]{2,1,0:T(8,128)S(1)}, f32[5,64,128]{2,1,0:T(8,128)S(1)}, u32[]{:S(2)}, u32[]{:S(2)}) collective-permute-start(f32[5,64,128]{2,1,0:T(8,128)S(1)} %get-tuple-element.48), channel_id=1, source_target_pairs={{0,16},{16,32},{32,48},{48,64},{64,80},{80,96},{96,112},{112,0},{1... | collective-permute-start | bytes 491528 | tf_op jit(solution)/shard_map/ppermute | solution.py:816
  1.6 5.9 %collective-permute-start.1 = (f32[5,64,128]{2,1,0:T(8,128)S(1)}, f32[5,64,128]{2,1,0:T(8,128)S(1)}, u32[]{:S(2)}, u32[]{:S(2)}) collective-permute-start(f32[5,64,128]{2,1,0:T(8,128)S(1)} %get-tuple-element.49), channel_id=1, source_target_pairs={{0,112},{16,0},{32,16},{48,32},{64,48},{80,64},{96,80},{112,96},{1... | collective-permute-start | bytes 491528 | tf_op jit(solution)/shard_map/ppermute | solution.py:817
  4.6 1.7 %copy-start.7 = (s32[2,3]{1,0:T(2,128)S(1)}, s32[2,3]{1,0:T(2,128)}, u32[]{:S(2)}) copy-start(s32[2,3]{1,0:T(2,128)} %param.22) | copy-start | bytes 76
  4.6 1.8 %copy-start.6 = (s32[1,4,4]{2,1,0:T(4,128)S(1)}, s32[1,4,4]{2,1,0:T(4,128)}, u32[]{:S(2)}) copy-start(s32[1,4,4]{2,1,0:T(4,128)} %param.23) | copy-start | bytes 196
  8.2 11.5 %collective-permute-start.2 = (f32[328,128]{1,0:T(8,128)S(1)}, f32[328,128]{1,0:T(8,128)S(1)}, u32[]{:S(2)}, u32[]{:S(2)}) collective-permute-start(f32[328,128]{1,0:T(8,128)S(1)} %get-tuple-element.52), channel_id=1, source_target_pairs={{0,1},{1,2},{2,3},{3,4},{4,5},{5,6},{6,7},{7,8},{8,9},{9,10},{10,1... | collective-permute-start | bytes 503816 | tf_op jit(solution)/shard_map/ppermute | solution.py:819
  10.3 9.4 %collective-permute-start.3 = (f32[328,128]{1,0:T(8,128)S(1)}, f32[328,128]{1,0:T(8,128)S(1)}, u32[]{:S(2)}, u32[]{:S(2)}) collective-permute-start(f32[328,128]{1,0:T(8,128)S(1)} %get-tuple-element.53), channel_id=1, source_target_pairs={{0,15},{1,0},{2,1},{3,2},{4,3},{5,4},{6,5},{7,6},{8,7},{9,8},{10,9... | collective-permute-start | bytes 503816 | tf_op jit(solution)/shard_map/ppermute | solution.py:820
  19.7 8.6 %copy-start.3 = (f32[2,8,2304]{2,1,0:T(8,128)S(1)}, f32[2,8,2304]{2,1,0:T(8,128)}, u32[]{:S(2)}) copy-start(f32[2,8,2304]{2,1,0:T(8,128)} %constant.17.clone.masks) | copy-start | bytes 442372
  21.5 6.8 %copy-start.2 = (f32[2,48,2304]{2,1,0:T(8,128)S(1)}, f32[2,48,2304]{2,1,0:T(8,128)}, u32[]{:S(2)}) copy-start(f32[2,48,2304]{2,1,0:T(8,128)} %f.3) | copy-start | bytes 2654212
  21.5 6.8 %copy-start.4 = (f32[2,48,2304]{2,1,0:T(8,128)S(1)}, f32[2,48,2304]{2,1,0:T(8,128)}, u32[]{:S(2)}) copy-start(f32[2,48,2304]{2,1,0:T(8,128)} %g.1) | copy-start | bytes 2654212
  21.5 8.5 %collective-permute-start.4 = (f32[2,2,16,128]{3,2,1,0:T(8,128)S(1)}, f32[2,2,16,128]{3,2,1,0:T(8,128)S(1)}, u32[]{:S(2)}, u32[]{:S(2)}) collective-permute-start(f32[2,2,16,128]{3,2,1,0:T(8,128)S(1)} %get-tuple-element.59), channel_id=1, source_target_pairs={{0,1},{1,0},{2,3},{3,2},{4,5},{5,4},{6,7},{7,6},{8,9},{9,8},{10,11... | collective-permute-start | bytes 98312 | tf_op jit(solution)/shard_map/ppermute | solution.py:827
  21.6 8.4 %collective-permute-start.5 = (f32[2,2,16,128]{3,2,1,0:T(8,128)S(1)}, f32[2,2,16,128]{3,2,1,0:T(8,128)S(1)}, u32[]{:S(2)}, u32[]{:S(2)}) collective-permute-start(f32[2,2,16,128]{3,2,1,0:T(8,128)S(1)} %get-tuple-element.60), channel_id=1, source_target_pairs={{0,64},{1,65},{2,66},{3,67},{4,68},{5,69},{6,70},{7,71},{8,72},{9,... | collective-permute-start | bytes 98312 | tf_op jit(solution)/shard_map/ppermute | solution.py:827
  23.0 7.1 %collective-permute-start.6 = (f32[2,2,16,128]{3,2,1,0:T(8,128)S(1)}, f32[2,2,16,128]{3,2,1,0:T(8,128)S(1)}, u32[]{:S(2)}, u32[]{:S(2)}) collective-permute-start(f32[2,2,16,128]{3,2,1,0:T(8,128)S(1)} %get-tuple-element.61), channel_id=1, source_target_pairs={{0,65},{1,64},{2,67},{3,66},{4,69},{5,68},{6,71},{7,70},{8,73},{9,... | collective-permute-start | bytes 98312 | tf_op jit(solution)/shard_map/ppermute | solution.py:827
  28.3 1.8 %copy-start = (bf16[2304,256]{1,0:T(8,128)(2,1)S(1)}, bf16[2304,256]{1,0:T(8,128)(2,1)}, u32[]{:S(2)}) copy-start(bf16[2304,256]{1,0:T(8,128)(2,1)} %constant.20.clone.pool) | copy-start | bytes 3538948
  28.3 1.8 %copy-start.1 = (bf16[256,2304]{1,0:T(8,128)(2,1)S(1)}, bf16[256,2304]{1,0:T(8,128)(2,1)}, u32[]{:S(2)}) copy-start(bf16[256,2304]{1,0:T(8,128)(2,1)} %constant.18.clone.spread) | copy-start | bytes 3538948
  28.4 1.8 %copy-start.5 = (f32[16,2304]{1,0:T(8,128)S(1)}, f32[16,2304]{1,0:T(8,128)}, u32[]{:S(2)}) copy-start(f32[16,2304]{1,0:T(8,128)} %constant.19.clone.pick) | copy-start | bytes 442372
  34.7 6.6 %collective-permute-start.9 = (f32[2,16,256]{2,1,0:T(8,128)S(1)}, f32[2,16,256]{2,1,0:T(8,128)S(1)}, u32[]{:S(2)}, u32[]{:S(2)}) collective-permute-start(f32[2,16,256]{2,1,0:T(8,128)S(1)} %get-tuple-element.62.r0), channel_id=1, source_target_pairs={{0,65},{1,64},{2,67},{3,66},{4,69},{5,68},{6,71},{7,70},{8,73},{9,... | collective-permute-start | bytes 98312 | tf_op jit(solution)/shard_map/ppermute | solution.py:827
  37.5 5.4 %collective-permute-start.8 = (f32[2,16,256]{2,1,0:T(8,128)S(1)}, f32[2,16,256]{2,1,0:T(8,128)S(1)}, u32[]{:S(2)}, u32[]{:S(2)}) collective-permute-start(f32[2,16,256]{2,1,0:T(8,128)S(1)} %get-tuple-element.62.r0), channel_id=1, source_target_pairs={{0,64},{1,65},{2,66},{3,67},{4,68},{5,69},{6,70},{7,71},{8,72},{9,... | collective-permute-start | bytes 98312 | tf_op jit(solution)/shard_map/ppermute | solution.py:827
  38.8 4.1 %collective-permute-start.7 = (f32[2,16,256]{2,1,0:T(8,128)S(1)}, f32[2,16,256]{2,1,0:T(8,128)S(1)}, u32[]{:S(2)}, u32[]{:S(2)}) collective-permute-start(f32[2,16,256]{2,1,0:T(8,128)S(1)} %get-tuple-element.62.r0), channel_id=1, source_target_pairs={{0,1},{1,0},{2,3},{3,2},{4,5},{5,4},{6,7},{7,6},{8,9},{9,8},{10,11... | collective-permute-start | bytes 98312 | tf_op jit(solution)/shard_map/ppermute | solution.py:827
  44.5 4.9 %collective-permute-start.10 = (f32[2,64,128]{2,1,0:T(8,128)S(1)}, f32[2,64,128]{2,1,0:T(8,128)S(1)}, u32[]{:S(2)}, u32[]{:S(2)}) collective-permute-start(f32[2,64,128]{2,1,0:T(8,128)S(1)} %get-tuple-element.66), channel_id=1, source_target_pairs={{0,16},{16,32},{32,48},{48,64},{64,80},{80,96},{96,112},{112,0},{1... | collective-permute-start | bytes 196616 | tf_op jit(solution)/shard_map/ppermute | solution.py:816
  44.5 4.9 %collective-permute-start.11 = (f32[2,64,128]{2,1,0:T(8,128)S(1)}, f32[2,64,128]{2,1,0:T(8,128)S(1)}, u32[]{:S(2)}, u32[]{:S(2)}) collective-permute-start(f32[2,64,128]{2,1,0:T(8,128)S(1)} %get-tuple-element.67), channel_id=1, source_target_pairs={{0,112},{16,0},{32,16},{48,32},{64,48},{80,64},{96,80},{112,96},{1... | collective-permute-start | bytes 196616 | tf_op jit(solution)/shard_map/ppermute | solution.py:817
  50.0 7.8 %collective-permute-start.12 = (f32[136,128]{1,0:T(8,128)S(1)}, f32[136,128]{1,0:T(8,128)S(1)}, u32[]{:S(2)}, u32[]{:S(2)}) collective-permute-start(f32[136,128]{1,0:T(8,128)S(1)} %get-tuple-element.70), channel_id=1, source_target_pairs={{0,1},{1,2},{2,3},{3,4},{4,5},{5,6},{6,7},{7,8},{8,9},{9,10},{10,1... | collective-permute-start | bytes 208904 | tf_op jit(solution)/shard_map/ppermute | solution.py:819
  50.3 7.5 %collective-permute-start.13 = (f32[136,128]{1,0:T(8,128)S(1)}, f32[136,128]{1,0:T(8,128)S(1)}, u32[]{:S(2)}, u32[]{:S(2)}) collective-permute-start(f32[136,128]{1,0:T(8,128)S(1)} %get-tuple-element.71), channel_id=1, source_target_pairs={{0,15},{1,0},{2,1},{3,2},{4,3},{5,4},{6,5},{7,6},{8,7},{9,8},{10,9... | collective-permute-start | bytes 208904 | tf_op jit(solution)/shard_map/ppermute | solution.py:820
  59.7 6.7 %collective-permute-start.14 = (f32[2,2,16,128]{3,2,1,0:T(8,128)S(1)}, f32[2,2,16,128]{3,2,1,0:T(8,128)S(1)}, u32[]{:S(2)}, u32[]{:S(2)}) collective-permute-start(f32[2,2,16,128]{3,2,1,0:T(8,128)S(1)} %get-tuple-element.76), channel_id=1, source_target_pairs={{0,1},{1,0},{2,3},{3,2},{4,5},{5,4},{6,7},{7,6},{8,9},{9,8},{10,11... | collective-permute-start | bytes 98312 | tf_op jit(solution)/shard_map/ppermute | solution.py:827
  59.8 6.7 %collective-permute-start.15 = (f32[2,2,16,128]{3,2,1,0:T(8,128)S(1)}, f32[2,2,16,128]{3,2,1,0:T(8,128)S(1)}, u32[]{:S(2)}, u32[]{:S(2)}) collective-permute-start(f32[2,2,16,128]{3,2,1,0:T(8,128)S(1)} %get-tuple-element.77), channel_id=1, source_target_pairs={{0,64},{1,65},{2,66},{3,67},{4,68},{5,69},{6,70},{7,71},{8,72},{9,... | collective-permute-start | bytes 98312 | tf_op jit(solution)/shard_map/ppermute | solution.py:827
  60.6 6.4 %collective-permute-start.16 = (f32[2,2,16,128]{3,2,1,0:T(8,128)S(1)}, f32[2,2,16,128]{3,2,1,0:T(8,128)S(1)}, u32[]{:S(2)}, u32[]{:S(2)}) collective-permute-start(f32[2,2,16,128]{3,2,1,0:T(8,128)S(1)} %get-tuple-element.78), channel_id=1, source_target_pairs={{0,65},{1,64},{2,67},{3,66},{4,69},{5,68},{6,71},{7,70},{8,73},{9,... | collective-permute-start | bytes 98312 | tf_op jit(solution)/shard_map/ppermute | solution.py:827
  71.5 6.9 %collective-permute-start.19 = (f32[2,16,256]{2,1,0:T(8,128)S(1)}, f32[2,16,256]{2,1,0:T(8,128)S(1)}, u32[]{:S(2)}, u32[]{:S(2)}) collective-permute-start(f32[2,16,256]{2,1,0:T(8,128)S(1)} %get-tuple-element.82.r0), channel_id=1, source_target_pairs={{0,65},{1,64},{2,67},{3,66},{4,69},{5,68},{6,71},{7,70},{8,73},{9,... | collective-permute-start | bytes 98312 | tf_op jit(solution)/shard_map/ppermute | solution.py:827
  75.6 5.4 %collective-permute-start.18 = (f32[2,16,256]{2,1,0:T(8,128)S(1)}, f32[2,16,256]{2,1,0:T(8,128)S(1)}, u32[]{:S(2)}, u32[]{:S(2)}) collective-permute-start(f32[2,16,256]{2,1,0:T(8,128)S(1)} %get-tuple-element.82.r0), channel_id=1, source_target_pairs={{0,64},{1,65},{2,66},{3,67},{4,68},{5,69},{6,70},{7,71},{8,72},{9,... | collective-permute-start | bytes 98312 | tf_op jit(solution)/shard_map/ppermute | solution.py:827
  76.4 4.7 %collective-permute-start.17 = (f32[2,16,256]{2,1,0:T(8,128)S(1)}, f32[2,16,256]{2,1,0:T(8,128)S(1)}, u32[]{:S(2)}, u32[]{:S(2)}) collective-permute-start(f32[2,16,256]{2,1,0:T(8,128)S(1)} %get-tuple-element.82.r0), channel_id=1, source_target_pairs={{0,1},{1,0},{2,3},{3,2},{4,5},{5,4},{6,7},{7,6},{8,9},{9,8},{10,11... | collective-permute-start | bytes 98312 | tf_op jit(solution)/shard_map/ppermute | solution.py:827

commit v4 on v3

--- a/solution.py
+++ b/solution.py
@@ -28,7 +28,7 @@
     flat = np.arange(PLANE)
     y, z = flat // FINE, flat % FINE
     masks = np.stack([z > 0, z < FINE - 1]).astype(np.float32)
-    masks = np.repeat(masks[:, None, :], 8, axis=1)
+    masks = np.repeat(masks[:, None, :384], 8, axis=1)
     r = np.arange(BC)[:, None]
     spread = np.zeros((128, PLANE), np.float32)
     spread[0:16] = (y == 0) & (z // 3 == r)
@@ -467,6 +467,7 @@
     cur = row(0)
     cur_t = turned(cur)
     before_t = none
+    masks = [[masks[n, :, 128 * r : 128 * r + 128] for r in range(3)] for n in range(2)]
     for k in range(PLANE // 128):
         ls = slice(128 * k, 128 * k + 128)
         last = k + 1 == PLANE // 128
@@ -476,7 +477,7 @@
         total = total + jnp.where(small >= 80, nxt_t[48][1], cur_t[48][1])
         down = jnp.where(small < 1, before_t[1][0], cur_t[1][0])
         up = jnp.where(small >= 127, nxt_t[1][1], cur_t[1][1])
-        total = total + down * masks[0, :, ls] + up * masks[1, :, ls]
+        total = total + down * masks[0][k % 3] + up * masks[1][k % 3]
         yield ls, cur, total
         before_t, cur, cur_t = cur_t, nxt, nxt_t
 
@@ -617,7 +618,7 @@
         substep(2, j)
         return carry
 
-    lax.fori_loop(0, 2, box, 0)
+    lax.fori_loop(0, 2, box, 0, unroll=True)
     tall = lax.broadcasted_iota(jnp.int32, (BC, FINE), 1)
     wide = lax.broadcasted_iota(jnp.int32, (BC, FINE), 0)
     gather = jnp.where((tall >= 3 * wide) & (tall < 3 * wide + 3), 1.0, 0.0).astype(BF16)

time: 82.8 us -> 81.3 us (0.982); the launches traced: 83.2 us -> 80.8 us
  Pallas kernels: 33.1 us -> 29.3 us
  waiting for transfers between devices: 10.3 us -> 11.3 us
    pallas_call x2, Pallas kernels: 9.14 us -> 7.43 us  [fine(): pl.pallas_call(fine_kernel, out_shape=(box, box, jax.ShapeDtypeStruct((2,...]
    pallas_call x2, Pallas kernels: 3.7 us -> 2.68 us  [coarse(): pl.pallas_call(functools.partial(coarse_kernel, first), out_shape=(jax.Sh...]
    ppermute x12, waiting for transfers between devices: 6.4 us -> 7.37 us  [trade(): lax.ppermute(value, ('tile', 'bulk'), [(d, d ^ away) for d in range(128)])]
  transfers between devices with their start and end apart: 20 -> 20, of which waited for: 8 -> 11; matrix products, arithmetic and copies ran while one was open for 0% -> 0% of each run, Pallas kernels for 18% -> 18%
where the time goes in v4:
time: 81.3 us; the launch traced here: 80.8 us
  starting transfers between devices  38.8 us (48%)
  Pallas kernels  29.3 us (36%)
  waiting for transfers between devices  11.3 us (14%)
  between operations  1.06 us (1%)
    ppermute x12, starting transfers between devices, trade(): lax.ppermute(value, ('tile', 'bulk'), [(d, d ^ away) for d in range(128)])  20.1 us
    ppermute x2, starting transfers between devices, halo(): yhi = lax.ppermute(ydn, 'bulk', ring(16, -1))  10.5 us
    pallas_call x2, Pallas kernels, fine(): pl.pallas_call(fine_kernel, out_shape=(box, box, jax.ShapeDtypeStruct((2,...  7.43 us
    ppermute x12, waiting for transfers between devices, trade(): lax.ppermute(value, ('tile', 'bulk'), [(d, d ^ away) for d in range(128)])  7.37 us
    ppermute x2, starting transfers between devices, halo(): xhi = lax.ppermute(xdn, 'tile', ring(8, -1))  5.89 us
    pallas_call x1, Pallas kernels, first_inner(): pl.pallas_call(first_inner_kernel, out_shape=(block, block, block, block)...  4.1 us
    pallas_call x2, Pallas kernels, ahead(): pl.pallas_call(ahead_kernel, out_shape=box, in_specs=[ANY] + [VMEM] * 5,...  3.27 us
    ppermute x2, waiting for transfers between devices, halo(): xlo = lax.ppermute(xup, 'tile', ring(8, 1))  2.98 us
  transfers between devices with their start and end apart: 20, of which 11 were waited for; matrix products, arithmetic and copies ran while one was open for 0% of the time, Pallas kernels for 18%

profile of v4, /device:TPU:0, one launch (start us, length us, event | category | flops | bytes accessed | tf_op | source)
XLA Modules:
  0.0 80.8 jit_solution(8591854895969348049)
XLA Ops:
  0.6 1.0 %x_edges.1 = (f32[5,64,128]{2,1,0:T(8,128)S(1)}, f32[5,64,128]{2,1,0:T(8,128)S(1)}) custom-call(f32[64,64,128]{2,1,0:T(8,128)} %p.5, f32[64,64,128]{2,1,0:T(8,128)} %q.5, f32[64,64,128]{2,1,0:T(8,128)} %c.6, f32[64,64,128]{2,1,0:T(8,128)} %a.6), custom_call_target="tpu_custom_call" | custom-call | tf_op jit(solution)/shard_map/x_edges/pallas_call | solution.py:79
  1.6 2.9 %collective-permute-start.1 = (f32[5,64,128]{2,1,0:T(8,128)S(1)}, f32[5,64,128]{2,1,0:T(8,128)S(1)}, u32[]{:S(2)}, u32[]{:S(2)}) collective-permute-start(f32[5,64,128]{2,1,0:T(8,128)S(1)} %get-tuple-element.49), channel_id=1, source_target_pairs={{0,112},{16,0},{32,16},{48,32},{64,48},{80,64},{96,80},{112,96},{1... | collective-permute-start | bytes 491528 | tf_op jit(solution)/shard_map/ppermute | solution.py:818
  4.6 1.7 %y_edges.1 = (f32[328,128]{1,0:T(8,128)S(1)}, f32[328,128]{1,0:T(8,128)S(1)}) custom-call(f32[64,64,128]{2,1,0:T(8,128)} %p.5, f32[64,64,128]{2,1,0:T(8,128)} %q.5, f32[64,64,128]{2,1,0:T(8,128)} %c.6, f32[64,64,128]{2,1,0:T(8,128)} %a.6), custom_call_target="tpu_custom_call" | custom-call | bytes 5000000 | tf_op jit(solution)/shard_map/y_edges/pallas_call | solution.py:117
  6.3 0.1 reshape.15
  6.4 0.1 reshape.14
  6.5 0.1 pad_add_fusion.meta
  6.5 1.0 %collective-permute-done.xlo.pxlo.exlo = f32[5,64,128]{2,1,0:T(8,128)S(1)} collective-permute-done((f32[5,64,128]{2,1,0:T(8,128)S(1)}, f32[5,64,128]{2,1,0:T(8,128)S(1)}, u32[]{:S(2)}, u32[]{:S(2)}) %collective-permute-start) | collective-permute-done | bytes 163872 | tf_op jit(solution)/shard_map/ppermute | solution.py:817
  7.6 0.6 corners.2
  8.2 2.1 %collective-permute-start.2 = (f32[328,128]{1,0:T(8,128)S(1)}, f32[328,128]{1,0:T(8,128)S(1)}, u32[]{:S(2)}, u32[]{:S(2)}) collective-permute-start(f32[328,128]{1,0:T(8,128)S(1)} %get-tuple-element.52), channel_id=1, source_target_pairs={{0,1},{1,2},{2,3},{3,4},{4,5},{5,6},{6,7},{7,8},{8,9},{9,10},{10,1... | collective-permute-start | bytes 503816 | tf_op jit(solution)/shard_map/ppermute | solution.py:820
  10.3 4.7 %collective-permute-start.3 = (f32[328,128]{1,0:T(8,128)S(1)}, f32[328,128]{1,0:T(8,128)S(1)}, u32[]{:S(2)}, u32[]{:S(2)}) collective-permute-start(f32[328,128]{1,0:T(8,128)S(1)} %get-tuple-element.53), channel_id=1, source_target_pairs={{0,15},{1,0},{2,1},{3,2},{4,3},{5,4},{6,5},{7,6},{8,7},{9,8},{10,9... | collective-permute-start | bytes 503816 | tf_op jit(solution)/shard_map/ppermute | solution.py:821
  14.9 4.1 %first_inner.1 = (f32[64,64,128]{2,1,0:T(8,128)S(1)}, f32[64,64,128]{2,1,0:T(8,128)S(1)}, f32[64,64,128]{2,1,0:T(8,128)S(1)}, f32[64,64,128]{2,1,0:T(8,128)S(1)}) custom-call(f32[64,64,128]{2,1,0:T(8,128)} %p.5, f32[64,64,128]{2,1,0:T(8,128)} %q.5, f32[64,64,128]{2,1,0:T(8,128)} %c.6, f32[64,64,128]{2,1,0:T(8,128)} %a.6), custom_call_target="tpu_custom_call" | custom-call | flops 12000000 | bytes 10000000 | tf_op jit(solution)/shard_map/first_inner/pallas_call | solution.py:235
  19.0 0.6 collective-permute-done.2.pylo.eylo
  19.7 1.3 %coarse.2 = (f32[64,64,128]{2,1,0:T(8,128)S(1)}, f32[2,2,16,128]{3,2,1,0:T(8,128)S(1)}, f32[2,2,16,128]{3,2,1,0:T(8,128)S(1)}, f32[2,2,16,128]{3,2,1,0:T(8,128)S(1)}, f32[2,2,16,128]{3,2,1,0:T(8,128)S(1)}) custom-call(s32[24]{0:T(128)S(1)} %pad_add_fusion.meta, f32[64,64,128]{2,1,0:T(8,128)S(1)} %get-tuple-element.45.p.q, ...), custom_call_target="tpu_custom_call" | custom-call | tf_op jit(solution)/shard_map/coarse/pallas_call | solution.py:407
  21.0 0.1 collective-permute-start.4
  21.1 2.1 %collective-permute-start.5 = (f32[2,2,16,128]{3,2,1,0:T(8,128)S(1)}, f32[2,2,16,128]{3,2,1,0:T(8,128)S(1)}, u32[]{:S(2)}, u32[]{:S(2)}) collective-permute-start(f32[2,2,16,128]{3,2,1,0:T(8,128)S(1)} %get-tuple-element.60), channel_id=1, source_target_pairs={{0,64},{1,65},{2,66},{3,67},{4,68},{5,69},{6,70},{7,71},{8,72},{9,... | collective-permute-start | bytes 98312 | tf_op jit(solution)/shard_map/ppermute | solution.py:828
  23.3 2.8 %collective-permute-start.6 = (f32[2,2,16,128]{3,2,1,0:T(8,128)S(1)}, f32[2,2,16,128]{3,2,1,0:T(8,128)S(1)}, u32[]{:S(2)}, u32[]{:S(2)}) collective-permute-start(f32[2,2,16,128]{3,2,1,0:T(8,128)S(1)} %get-tuple-element.61), channel_id=1, source_target_pairs={{0,65},{1,64},{2,67},{3,66},{4,69},{5,68},{6,71},{7,70},{8,73},{9,... | collective-permute-start | bytes 98312 | tf_op jit(solution)/shard_map/ppermute | solution.py:828
  26.1 1.7 %factors.1 = (f32[2,48,2304]{2,1,0:T(8,128)S(1)}, f32[2,48,2304]{2,1,0:T(8,128)S(1)}, f32[2,48,2304]{2,1,0:T(8,128)S(1)}) custom-call(f32[2,48,2304]{2,1,0:T(8,128)} %c.7, f32[2,48,2304]{2,1,0:T(8,128)} %a.7), custom_call_target="tpu_custom_call" | custom-call | flops 3000000 | bytes 4000000 | tf_op jit(solution)/shard_map/factors/pallas_call | solution.py:447
  27.9 1.6 %ahead.2.raw = f32[2,48,2304]{2,1,0:T(8,128)S(1)} custom-call(f32[2,48,2304]{2,1,0:T(8,128)S(1)} %copy-done.2, f32[2,48,2304]{2,1,0:T(8,128)S(1)} %copy-done.3, f32[2,48,2304]{2,1,0:T(8,128)S(1)} %get-tuple-element.55.one, f32[2,48,2304]{2,1,0:T(8,128)S(1)} %get-tuple-element.56.two, f32[2,48,2304]{2,1,0:T(8,128)S(1)} %get-tuple-element.57.three, ...), custom_call_target="tpu_custom_call" | custom-call | flops 5000000 | bytes 5000000 | tf_op jit(solution)/shard_map/ahead/pallas_call | solution.py:514
  29.5 0.1 collective-permute-done.6.r3
  29.6 3.7 %fine.2 = (f32[2,48,2304]{2,1,0:T(8,128)S(1)}, f32[2,48,2304]{2,1,0:T(8,128)S(1)}, f32[2,16,256]{2,1,0:T(8,128)S(1)}) custom-call(s32[24]{0:T(128)S(1)} %pad_add_fusion.meta, f32[2,48,2304]{2,1,0:T(8,128)S(1)} %copy-done.2, f32[2,48,2304]{2,1,0:T(8,128)S(1)} %ahead.2.raw, f32[2,48,2304]{2,1,0:T(8,128)S(1)} %get-tuple-element.55.one, ...), custom_call_target="tpu_custom_call" | custom-call | tf_op jit(solution)/shard_map/fine/pallas_call | solution.py:638
  33.3 2.8 %collective-permute-start.9 = (f32[2,16,256]{2,1,0:T(8,128)S(1)}, f32[2,16,256]{2,1,0:T(8,128)S(1)}, u32[]{:S(2)}, u32[]{:S(2)}) collective-permute-start(f32[2,16,256]{2,1,0:T(8,128)S(1)} %get-tuple-element.62.r0), channel_id=1, source_target_pairs={{0,65},{1,64},{2,67},{3,66},{4,69},{5,68},{6,71},{7,70},{8,73},{9,... | collective-permute-start | bytes 98312 | tf_op jit(solution)/shard_map/ppermute | solution.py:828
  36.2 2.1 %collective-permute-start.8 = (f32[2,16,256]{2,1,0:T(8,128)S(1)}, f32[2,16,256]{2,1,0:T(8,128)S(1)}, u32[]{:S(2)}, u32[]{:S(2)}) collective-permute-start(f32[2,16,256]{2,1,0:T(8,128)S(1)} %get-tuple-element.62.r0), channel_id=1, source_target_pairs={{0,64},{1,65},{2,66},{3,67},{4,68},{5,69},{6,70},{7,71},{8,72},{9,... | collective-permute-start | bytes 98312 | tf_op jit(solution)/shard_map/ppermute | solution.py:828
  38.2 0.1 collective-permute-start.7
  38.3 1.4 %collective-permute-done.9.r3 = f32[2,16,256]{2,1,0:T(8,128)S(1)} collective-permute-done((f32[2,16,256]{2,1,0:T(8,128)S(1)}, f32[2,16,256]{2,1,0:T(8,128)S(1)}, u32[]{:S(2)}, u32[]{:S(2)}) %collective-permute-start.9) | collective-permute-done | bytes 32800 | tf_op jit(solution)/shard_map/ppermute | solution.py:828
  39.7 1.9 %collective-permute-done.8.r2 = f32[2,16,256]{2,1,0:T(8,128)S(1)} collective-permute-done((f32[2,16,256]{2,1,0:T(8,128)S(1)}, f32[2,16,256]{2,1,0:T(8,128)S(1)}, u32[]{:S(2)}, u32[]{:S(2)}) %collective-permute-start.8) | collective-permute-done | bytes 32800 | tf_op jit(solution)/shard_map/ppermute | solution.py:828
  41.6 0.6 collective-permute-done.7.r1
  42.1 1.1 %insert.1 = (f32[64,64,128]{2,1,0:T(8,128)S(1)}, f32[2,64,128]{2,1,0:T(8,128)S(1)}, f32[2,64,128]{2,1,0:T(8,128)S(1)}, f32[136,128]{1,0:T(8,128)S(1)}, f32[136,128]{1,0:T(8,128)S(1)}) custom-call(s32[24]{0:T(128)S(1)} %pad_add_fusion.meta, f32[64,64,128]{2,1,0:T(8,128)S(1)} %get-tuple-element.54.new, f32[2,16,256]{2,1,0:T(8,128)S(1)} %get-tuple-element.62.r0, ...), custom_call_target="tpu_custom_call" | custom-call | tf_op jit(solution)/shard_map/insert/pallas_call | solution.py:714
  43.2 2.9 %collective-permute-start.11 = (f32[2,64,128]{2,1,0:T(8,128)S(1)}, f32[2,64,128]{2,1,0:T(8,128)S(1)}, u32[]{:S(2)}, u32[]{:S(2)}) collective-permute-start(f32[2,64,128]{2,1,0:T(8,128)S(1)} %get-tuple-element.67), channel_id=1, source_target_pairs={{0,112},{16,0},{32,16},{48,32},{64,48},{80,64},{96,80},{112,96},{1... | collective-permute-start | bytes 196616 | tf_op jit(solution)/shard_map/ppermute | solution.py:818
  46.2 1.9 %collective-permute-done.10.xlo.pxlo = f32[2,64,128]{2,1,0:T(8,128)S(1)} collective-permute-done((f32[2,64,128]{2,1,0:T(8,128)S(1)}, f32[2,64,128]{2,1,0:T(8,128)S(1)}, u32[]{:S(2)}, u32[]{:S(2)}) %collective-permute-start.10) | collective-permute-done | bytes 65568 | tf_op jit(solution)/shard_map/ppermute | solution.py:817
  48.1 0.6 corners.3
  48.7 0.2 collective-permute-start.12
  48.9 5.9 %collective-permute-start.13 = (f32[136,128]{1,0:T(8,128)S(1)}, f32[136,128]{1,0:T(8,128)S(1)}, u32[]{:S(2)}, u32[]{:S(2)}) collective-permute-start(f32[136,128]{1,0:T(8,128)S(1)} %get-tuple-element.71), channel_id=1, source_target_pairs={{0,15},{1,0},{2,1},{3,2},{4,3},{5,4},{6,5},{7,6},{8,7},{9,8},{10,9... | collective-permute-start | bytes 208904 | tf_op jit(solution)/shard_map/ppermute | solution.py:821
  54.8 1.9 %second_inner.1 = (f32[64,64,128]{2,1,0:T(8,128)S(1)}, f32[64,64,128]{2,1,0:T(8,128)}) custom-call(f32[64,64,128]{2,1,0:T(8,128)S(1)} %get-tuple-element.63.p, f32[64,64,128]{2,1,0:T(8,128)S(1)} %get-tuple-element.45.p.q, f32[64,64,128]{2,1,0:T(8,128)S(1)} %get-tuple-element.64.two, f32[64,64,128]{2,1,0:T(8,128)S(1)} %get-tuple-element.47.weight.side), custom_call_target="tpu_custom_call" | custom-call | flops 12000000 | bytes 8000000 | tf_op jit(solution)/shard_map/second_inner/pallas_call | solution.py:274
  56.6 0.3 collective-permute-done.12.pylo
  57.0 1.3 %coarse.3 = (f32[64,64,128]{2,1,0:T(8,128)S(1)}, f32[2,2,16,128]{3,2,1,0:T(8,128)S(1)}, f32[2,2,16,128]{3,2,1,0:T(8,128)S(1)}, f32[2,2,16,128]{3,2,1,0:T(8,128)S(1)}, f32[2,2,16,128]{3,2,1,0:T(8,128)S(1)}) custom-call(s32[24]{0:T(128)S(1)} %pad_add_fusion.meta, f32[64,64,128]{2,1,0:T(8,128)S(1)} %get-tuple-element.63.p, ...), custom_call_target="tpu_custom_call" | custom-call | tf_op jit(solution)/shard_map/coarse/pallas_call | solution.py:407
  58.3 0.1 collective-permute-start.14
  58.4 1.9 %collective-permute-start.15 = (f32[2,2,16,128]{3,2,1,0:T(8,128)S(1)}, f32[2,2,16,128]{3,2,1,0:T(8,128)S(1)}, u32[]{:S(2)}, u32[]{:S(2)}) collective-permute-start(f32[2,2,16,128]{3,2,1,0:T(8,128)S(1)} %get-tuple-element.77), channel_id=1, source_target_pairs={{0,64},{1,65},{2,66},{3,67},{4,68},{5,69},{6,70},{7,71},{8,72},{9,... | collective-permute-start | bytes 98312 | tf_op jit(solution)/shard_map/ppermute | solution.py:828
  60.3 3.1 %collective-permute-start.16 = (f32[2,2,16,128]{3,2,1,0:T(8,128)S(1)}, f32[2,2,16,128]{3,2,1,0:T(8,128)S(1)}, u32[]{:S(2)}, u32[]{:S(2)}) collective-permute-start(f32[2,2,16,128]{3,2,1,0:T(8,128)S(1)} %get-tuple-element.78), channel_id=1, source_target_pairs={{0,65},{1,64},{2,67},{3,66},{4,69},{5,68},{6,71},{7,70},{8,73},{9,... | collective-permute-start | bytes 98312 | tf_op jit(solution)/shard_map/ppermute | solution.py:828
  63.4 1.6 %ahead.3.raw = f32[2,48,2304]{2,1,0:T(8,128)S(1)} custom-call(f32[2,48,2304]{2,1,0:T(8,128)S(1)} %get-tuple-element.73.f, f32[2,48,2304]{2,1,0:T(8,128)S(1)} %get-tuple-element.74.g, f32[2,48,2304]{2,1,0:T(8,128)S(1)} %get-tuple-element.55.one, f32[2,48,2304]{2,1,0:T(8,128)S(1)} %get-tuple-element.56.two, f32[2,48,2304]{2,1,0:T(8,128)S(1)} %get-tuple-element.57.three, ...), custom_call_target="tpu_custom_call" | custom-call | flops 5000000 | bytes 5000000 | tf_op jit(solution)/shard_map/ahead/pallas_call | solution.py:514
  65.1 1.6 %collective-permute-done.16.r3 = f32[2,2,16,128]{3,2,1,0:T(8,128)S(1)} collective-permute-done((f32[2,2,16,128]{3,2,1,0:T(8,128)S(1)}, f32[2,2,16,128]{3,2,1,0:T(8,128)S(1)}, u32[]{:S(2)}, u32[]{:S(2)}) %collective-permute-start.16) | collective-permute-done | bytes 32800 | tf_op jit(solution)/shard_map/ppermute | solution.py:828
  66.7 3.7 %fine.3 = (f32[2,48,2304]{2,1,0:T(8,128)S(1)}, f32[2,48,2304]{2,1,0:T(8,128)S(1)}, f32[2,16,256]{2,1,0:T(8,128)S(1)}) custom-call(s32[24]{0:T(128)S(1)} %pad_add_fusion.meta, f32[2,48,2304]{2,1,0:T(8,128)S(1)} %get-tuple-element.73.f, f32[2,48,2304]{2,1,0:T(8,128)S(1)} %ahead.3.raw, f32[2,48,2304]{2,1,0:T(8,128)S(1)} %get-tuple-element.55.one, ...), custom_call_target="tpu_custom_call" | custom-call | tf_op jit(solution)/shard_map/fine/pallas_call | solution.py:638
  70.3 3.1 %collective-permute-start.19 = (f32[2,16,256]{2,1,0:T(8,128)S(1)}, f32[2,16,256]{2,1,0:T(8,128)S(1)}, u32[]{:S(2)}, u32[]{:S(2)}) collective-permute-start(f32[2,16,256]{2,1,0:T(8,128)S(1)} %get-tuple-element.82.r0), channel_id=1, source_target_pairs={{0,65},{1,64},{2,67},{3,66},{4,69},{5,68},{6,71},{7,70},{8,73},{9,... | collective-permute-start | bytes 98312 | tf_op jit(solution)/shard_map/ppermute | solution.py:828
  73.4 1.8 %collective-permute-start.18 = (f32[2,16,256]{2,1,0:T(8,128)S(1)}, f32[2,16,256]{2,1,0:T(8,128)S(1)}, u32[]{:S(2)}, u32[]{:S(2)}) collective-permute-start(f32[2,16,256]{2,1,0:T(8,128)S(1)} %get-tuple-element.82.r0), channel_id=1, source_target_pairs={{0,64},{1,65},{2,66},{3,67},{4,68},{5,69},{6,70},{7,71},{8,72},{9,... | collective-permute-start | bytes 98312 | tf_op jit(solution)/shard_map/ppermute | solution.py:828
  75.3 0.1 collective-permute-start.17
  75.3 1.9 %emit.1 = (f32[64,64,128]{2,1,0:T(8,128)}, f32[2,48,2304]{2,1,0:T(8,128)}, f32[2,48,2304]{2,1,0:T(8,128)}) custom-call(f32[64,64,128]{2,1,0:T(8,128)S(1)} %get-tuple-element.72.new, f32[2,48,2304]{2,1,0:T(8,128)S(1)} %get-tuple-element.79.f, f32[2,48,2304]{2,1,0:T(8,128)S(1)} %get-tuple-element.80.g), custom_call_target="tpu_custom_call" | custom-call | bytes 9000000 | tf_op jit(solution)/shard_map/emit/pallas_call | solution.py:736
  77.3 1.6 %collective-permute-done.18.r2 = f32[2,16,256]{2,1,0:T(8,128)S(1)} collective-permute-done((f32[2,16,256]{2,1,0:T(8,128)S(1)}, f32[2,16,256]{2,1,0:T(8,128)S(1)}, u32[]{:S(2)}, u32[]{:S(2)}) %collective-permute-start.18) | collective-permute-done | bytes 32800 | tf_op jit(solution)/shard_map/ppermute | solution.py:828
  78.8 0.3 collective-permute-done.17.r1
  79.2 1.5 %finish.1 = f32[64,64,128]{2,1,0:T(8,128)} custom-call(s32[24]{0:T(128)S(1)} %pad_add_fusion.meta, f32[64,64,128]{2,1,0:T(8,128)S(1)} %get-tuple-element.72.new, f32[64,64,128]{2,1,0:T(8,128)} %get-tuple-element.81.written, f32[2,16,256]{2,1,0:T(8,128)S(1)} %get-tuple-element.82.r0, ...), custom_call_target="tpu_custom_call", output_to_operand_aliasing={{}: (2, {})} | custom-call | tf_op jit(solution)/shard_map/finish/pallas_call | solution.py:796
  (27 shorter events, 0.1 us)
Async XLA Ops:
  1.6 6.0 %collective-permute-start = (f32[5,64,128]{2,1,0:T(8,128)S(1)}, f32[5,64,128]{2,1,0:T(8,128)S(1)}, u32[]{:S(2)}, u32[]{:S(2)}) collective-permute-start(f32[5,64,128]{2,1,0:T(8,128)S(1)} %get-tuple-element.48), channel_id=1, source_target_pairs={{0,16},{16,32},{32,48},{48,64},{64,80},{80,96},{96,112},{112,0},{1... | collective-permute-start | bytes 491528 | tf_op jit(solution)/shard_map/ppermute | solution.py:817
  1.6 5.9 %collective-permute-start.1 = (f32[5,64,128]{2,1,0:T(8,128)S(1)}, f32[5,64,128]{2,1,0:T(8,128)S(1)}, u32[]{:S(2)}, u32[]{:S(2)}) collective-permute-start(f32[5,64,128]{2,1,0:T(8,128)S(1)} %get-tuple-element.49), channel_id=1, source_target_pairs={{0,112},{16,0},{32,16},{48,32},{64,48},{80,64},{96,80},{112,96},{1... | collective-permute-start | bytes 491528 | tf_op jit(solution)/shard_map/ppermute | solution.py:818
  4.6 1.7 %copy-start.7 = (s32[2,3]{1,0:T(2,128)S(1)}, s32[2,3]{1,0:T(2,128)}, u32[]{:S(2)}) copy-start(s32[2,3]{1,0:T(2,128)} %param.22) | copy-start | bytes 76
  4.6 1.8 %copy-start.6 = (s32[1,4,4]{2,1,0:T(4,128)S(1)}, s32[1,4,4]{2,1,0:T(4,128)}, u32[]{:S(2)}) copy-start(s32[1,4,4]{2,1,0:T(4,128)} %param.23) | copy-start | bytes 196
  8.2 11.5 %collective-permute-start.2 = (f32[328,128]{1,0:T(8,128)S(1)}, f32[328,128]{1,0:T(8,128)S(1)}, u32[]{:S(2)}, u32[]{:S(2)}) collective-permute-start(f32[328,128]{1,0:T(8,128)S(1)} %get-tuple-element.52), channel_id=1, source_target_pairs={{0,1},{1,2},{2,3},{3,4},{4,5},{5,6},{6,7},{7,8},{8,9},{9,10},{10,1... | collective-permute-start | bytes 503816 | tf_op jit(solution)/shard_map/ppermute | solution.py:820
  10.3 9.4 %collective-permute-start.3 = (f32[328,128]{1,0:T(8,128)S(1)}, f32[328,128]{1,0:T(8,128)S(1)}, u32[]{:S(2)}, u32[]{:S(2)}) collective-permute-start(f32[328,128]{1,0:T(8,128)S(1)} %get-tuple-element.53), channel_id=1, source_target_pairs={{0,15},{1,0},{2,1},{3,2},{4,3},{5,4},{6,5},{7,6},{8,7},{9,8},{10,9... | collective-permute-start | bytes 503816 | tf_op jit(solution)/shard_map/ppermute | solution.py:821
  19.7 8.1 %copy-start.5 = (f32[2,8,384]{2,1,0:T(8,128)S(1)}, f32[2,8,384]{2,1,0:T(8,128)}, u32[]{:S(2)}) copy-start(f32[2,8,384]{2,1,0:T(8,128)} %constant.17.clone.masks) | copy-start | bytes 73732
  21.0 6.8 %copy-start.2 = (f32[2,48,2304]{2,1,0:T(8,128)S(1)}, f32[2,48,2304]{2,1,0:T(8,128)}, u32[]{:S(2)}) copy-start(f32[2,48,2304]{2,1,0:T(8,128)} %f.3) | copy-start | bytes 2654212
  21.0 6.8 %copy-start.3 = (f32[2,48,2304]{2,1,0:T(8,128)S(1)}, f32[2,48,2304]{2,1,0:T(8,128)}, u32[]{:S(2)}) copy-start(f32[2,48,2304]{2,1,0:T(8,128)} %g.1) | copy-start | bytes 2654212
  21.0 8.5 %collective-permute-start.4 = (f32[2,2,16,128]{3,2,1,0:T(8,128)S(1)}, f32[2,2,16,128]{3,2,1,0:T(8,128)S(1)}, u32[]{:S(2)}, u32[]{:S(2)}) collective-permute-start(f32[2,2,16,128]{3,2,1,0:T(8,128)S(1)} %get-tuple-element.59), channel_id=1, source_target_pairs={{0,1},{1,0},{2,3},{3,2},{4,5},{5,4},{6,7},{7,6},{8,9},{9,8},{10,11... | collective-permute-start | bytes 98312 | tf_op jit(solution)/shard_map/ppermute | solution.py:828
  21.1 8.4 %collective-permute-start.5 = (f32[2,2,16,128]{3,2,1,0:T(8,128)S(1)}, f32[2,2,16,128]{3,2,1,0:T(8,128)S(1)}, u32[]{:S(2)}, u32[]{:S(2)}) collective-permute-start(f32[2,2,16,128]{3,2,1,0:T(8,128)S(1)} %get-tuple-element.60), channel_id=1, source_target_pairs={{0,64},{1,65},{2,66},{3,67},{4,68},{5,69},{6,70},{7,71},{8,72},{9,... | collective-permute-start | bytes 98312 | tf_op jit(solution)/shard_map/ppermute | solution.py:828
  23.3 6.3 %collective-permute-start.6 = (f32[2,2,16,128]{3,2,1,0:T(8,128)S(1)}, f32[2,2,16,128]{3,2,1,0:T(8,128)S(1)}, u32[]{:S(2)}, u32[]{:S(2)}) collective-permute-start(f32[2,2,16,128]{3,2,1,0:T(8,128)S(1)} %get-tuple-element.61), channel_id=1, source_target_pairs={{0,65},{1,64},{2,67},{3,66},{4,69},{5,68},{6,71},{7,70},{8,73},{9,... | collective-permute-start | bytes 98312 | tf_op jit(solution)/shard_map/ppermute | solution.py:828
  27.8 1.8 %copy-start = (bf16[2304,256]{1,0:T(8,128)(2,1)S(1)}, bf16[2304,256]{1,0:T(8,128)(2,1)}, u32[]{:S(2)}) copy-start(bf16[2304,256]{1,0:T(8,128)(2,1)} %constant.20.clone.pool) | copy-start | bytes 3538948
  27.8 1.7 %copy-start.1 = (bf16[256,2304]{1,0:T(8,128)(2,1)S(1)}, bf16[256,2304]{1,0:T(8,128)(2,1)}, u32[]{:S(2)}) copy-start(bf16[256,2304]{1,0:T(8,128)(2,1)} %constant.18.clone.spread) | copy-start | bytes 3538948
  27.9 1.7 %copy-start.4 = (f32[16,2304]{1,0:T(8,128)S(1)}, f32[16,2304]{1,0:T(8,128)}, u32[]{:S(2)}) copy-start(f32[16,2304]{1,0:T(8,128)} %constant.19.clone.pick) | copy-start | bytes 442372
  33.3 6.4 %collective-permute-start.9 = (f32[2,16,256]{2,1,0:T(8,128)S(1)}, f32[2,16,256]{2,1,0:T(8,128)S(1)}, u32[]{:S(2)}, u32[]{:S(2)}) collective-permute-start(f32[2,16,256]{2,1,0:T(8,128)S(1)} %get-tuple-element.62.r0), channel_id=1, source_target_pairs={{0,65},{1,64},{2,67},{3,66},{4,69},{5,68},{6,71},{7,70},{8,73},{9,... | collective-permute-start | bytes 98312 | tf_op jit(solution)/shard_map/ppermute | solution.py:828
  36.2 5.4 %collective-permute-start.8 = (f32[2,16,256]{2,1,0:T(8,128)S(1)}, f32[2,16,256]{2,1,0:T(8,128)S(1)}, u32[]{:S(2)}, u32[]{:S(2)}) collective-permute-start(f32[2,16,256]{2,1,0:T(8,128)S(1)} %get-tuple-element.62.r0), channel_id=1, source_target_pairs={{0,64},{1,65},{2,66},{3,67},{4,68},{5,69},{6,70},{7,71},{8,72},{9,... | collective-permute-start | bytes 98312 | tf_op jit(solution)/shard_map/ppermute | solution.py:828
  38.2 3.9 %collective-permute-start.7 = (f32[2,16,256]{2,1,0:T(8,128)S(1)}, f32[2,16,256]{2,1,0:T(8,128)S(1)}, u32[]{:S(2)}, u32[]{:S(2)}) collective-permute-start(f32[2,16,256]{2,1,0:T(8,128)S(1)} %get-tuple-element.62.r0), channel_id=1, source_target_pairs={{0,1},{1,0},{2,3},{3,2},{4,5},{5,4},{6,7},{7,6},{8,9},{9,8},{10,11... | collective-permute-start | bytes 98312 | tf_op jit(solution)/shard_map/ppermute | solution.py:828
  43.2 4.9 %collective-permute-start.10 = (f32[2,64,128]{2,1,0:T(8,128)S(1)}, f32[2,64,128]{2,1,0:T(8,128)S(1)}, u32[]{:S(2)}, u32[]{:S(2)}) collective-permute-start(f32[2,64,128]{2,1,0:T(8,128)S(1)} %get-tuple-element.66), channel_id=1, source_target_pairs={{0,16},{16,32},{32,48},{48,64},{64,80},{80,96},{96,112},{112,0},{1... | collective-permute-start | bytes 196616 | tf_op jit(solution)/shard_map/ppermute | solution.py:817
  43.2 4.9 %collective-permute-start.11 = (f32[2,64,128]{2,1,0:T(8,128)S(1)}, f32[2,64,128]{2,1,0:T(8,128)S(1)}, u32[]{:S(2)}, u32[]{:S(2)}) collective-permute-start(f32[2,64,128]{2,1,0:T(8,128)S(1)} %get-tuple-element.67), channel_id=1, source_target_pairs={{0,112},{16,0},{32,16},{48,32},{64,48},{80,64},{96,80},{112,96},{1... | collective-permute-start | bytes 196616 | tf_op jit(solution)/shard_map/ppermute | solution.py:818
  48.7 8.2 %collective-permute-start.12 = (f32[136,128]{1,0:T(8,128)S(1)}, f32[136,128]{1,0:T(8,128)S(1)}, u32[]{:S(2)}, u32[]{:S(2)}) collective-permute-start(f32[136,128]{1,0:T(8,128)S(1)} %get-tuple-element.70), channel_id=1, source_target_pairs={{0,1},{1,2},{2,3},{3,4},{4,5},{5,6},{6,7},{7,8},{8,9},{9,10},{10,1... | collective-permute-start | bytes 208904 | tf_op jit(solution)/shard_map/ppermute | solution.py:820
  48.9 8.1 %collective-permute-start.13 = (f32[136,128]{1,0:T(8,128)S(1)}, f32[136,128]{1,0:T(8,128)S(1)}, u32[]{:S(2)}, u32[]{:S(2)}) collective-permute-start(f32[136,128]{1,0:T(8,128)S(1)} %get-tuple-element.71), channel_id=1, source_target_pairs={{0,15},{1,0},{2,1},{3,2},{4,3},{5,4},{6,5},{7,6},{8,7},{9,8},{10,9... | collective-permute-start | bytes 208904 | tf_op jit(solution)/shard_map/ppermute | solution.py:821
  58.3 6.7 %collective-permute-start.14 = (f32[2,2,16,128]{3,2,1,0:T(8,128)S(1)}, f32[2,2,16,128]{3,2,1,0:T(8,128)S(1)}, u32[]{:S(2)}, u32[]{:S(2)}) collective-permute-start(f32[2,2,16,128]{3,2,1,0:T(8,128)S(1)} %get-tuple-element.76), channel_id=1, source_target_pairs={{0,1},{1,0},{2,3},{3,2},{4,5},{5,4},{6,7},{7,6},{8,9},{9,8},{10,11... | collective-permute-start | bytes 98312 | tf_op jit(solution)/shard_map/ppermute | solution.py:828
  58.4 6.6 %collective-permute-start.15 = (f32[2,2,16,128]{3,2,1,0:T(8,128)S(1)}, f32[2,2,16,128]{3,2,1,0:T(8,128)S(1)}, u32[]{:S(2)}, u32[]{:S(2)}) collective-permute-start(f32[2,2,16,128]{3,2,1,0:T(8,128)S(1)} %get-tuple-element.77), channel_id=1, source_target_pairs={{0,64},{1,65},{2,66},{3,67},{4,68},{5,69},{6,70},{7,71},{8,72},{9,... | collective-permute-start | bytes 98312 | tf_op jit(solution)/shard_map/ppermute | solution.py:828
  60.3 6.3 %collective-permute-start.16 = (f32[2,2,16,128]{3,2,1,0:T(8,128)S(1)}, f32[2,2,16,128]{3,2,1,0:T(8,128)S(1)}, u32[]{:S(2)}, u32[]{:S(2)}) collective-permute-start(f32[2,2,16,128]{3,2,1,0:T(8,128)S(1)} %get-tuple-element.78), channel_id=1, source_target_pairs={{0,65},{1,64},{2,67},{3,66},{4,69},{5,68},{6,71},{7,70},{8,73},{9,... | collective-permute-start | bytes 98312 | tf_op jit(solution)/shard_map/ppermute | solution.py:828
  70.3 6.9 %collective-permute-start.19 = (f32[2,16,256]{2,1,0:T(8,128)S(1)}, f32[2,16,256]{2,1,0:T(8,128)S(1)}, u32[]{:S(2)}, u32[]{:S(2)}) collective-permute-start(f32[2,16,256]{2,1,0:T(8,128)S(1)} %get-tuple-element.82.r0), channel_id=1, source_target_pairs={{0,65},{1,64},{2,67},{3,66},{4,69},{5,68},{6,71},{7,70},{8,73},{9,... | collective-permute-start | bytes 98312 | tf_op jit(solution)/shard_map/ppermute | solution.py:828
  73.4 5.4 %collective-permute-start.18 = (f32[2,16,256]{2,1,0:T(8,128)S(1)}, f32[2,16,256]{2,1,0:T(8,128)S(1)}, u32[]{:S(2)}, u32[]{:S(2)}) collective-permute-start(f32[2,16,256]{2,1,0:T(8,128)S(1)} %get-tuple-element.82.r0), channel_id=1, source_target_pairs={{0,64},{1,65},{2,66},{3,67},{4,68},{5,69},{6,70},{7,71},{8,72},{9,... | collective-permute-start | bytes 98312 | tf_op jit(solution)/shard_map/ppermute | solution.py:828
  75.3 3.9 %collective-permute-start.17 = (f32[2,16,256]{2,1,0:T(8,128)S(1)}, f32[2,16,256]{2,1,0:T(8,128)S(1)}, u32[]{:S(2)}, u32[]{:S(2)}) collective-permute-start(f32[2,16,256]{2,1,0:T(8,128)S(1)} %get-tuple-element.82.r0), channel_id=1, source_target_pairs={{0,1},{1,0},{2,3},{3,2},{4,5},{5,4},{6,7},{7,6},{8,9},{9,8},{10,11... | collective-permute-start | bytes 98312 | tf_op jit(solution)/shard_map/ppermute | solution.py:828

commit v5 on v4

--- a/solution.py
+++ b/solution.py
@@ -439,7 +439,7 @@
             two[j, s, :] = 1.0 - 2.0 * inv
             return carry
 
-        lax.fori_loop(0, FINE // 8, body, 0)
+        lax.fori_loop(0, FINE // 8, body, 0, unroll=2)
 
 
 def factors(c, a):
@@ -506,7 +506,7 @@
                 )
         return carry
 
-    lax.fori_loop(0, 2, box, 0)
+    lax.fori_loop(0, 2, box, 0, unroll=True)
 
 
 def ahead(f, g, weights, masks):

time: 81.3 us -> 81.4 us (level)
  no operation moved by 1% of the time
where the time goes in v5:
time: 81.4 us; the launch traced here: 80.8 us
  starting transfers between devices  38.2 us (47%)
  Pallas kernels  29.3 us (36%)
  waiting for transfers between devices  12 us (15%)
  between operations  1.06 us (1%)
    ppermute x12, starting transfers between devices, trade(): lax.ppermute(value, ('tile', 'bulk'), [(d, d ^ away) for d in range(128)])  20.1 us
    ppermute x2, starting transfers between devices, halo(): yhi = lax.ppermute(ydn, 'bulk', ring(16, -1))  9.91 us
    ppermute x12, waiting for transfers between devices, trade(): lax.ppermute(value, ('tile', 'bulk'), [(d, d ^ away) for d in range(128)])  7.98 us
    pallas_call x2, Pallas kernels, fine(): pl.pallas_call(fine_kernel, out_shape=(box, box, jax.ShapeDtypeStruct((2,...  7.43 us
    ppermute x2, starting transfers between devices, halo(): xhi = lax.ppermute(xdn, 'tile', ring(8, -1))  5.89 us
    pallas_call x1, Pallas kernels, first_inner(): pl.pallas_call(first_inner_kernel, out_shape=(block, block, block, block)...  4.1 us
    pallas_call x2, Pallas kernels, ahead(): pl.pallas_call(ahead_kernel, out_shape=box, in_specs=[ANY] + [VMEM] * 5,...  3.13 us
    ppermute x2, waiting for transfers between devices, halo(): xlo = lax.ppermute(xup, 'tile', ring(8, 1))  2.98 us
  transfers between devices with their start and end apart: 20, of which 11 were waited for; matrix products, arithmetic and copies ran while one was open for 0% of the time, Pallas kernels for 18%

profile of v5, /device:TPU:0, one launch (start us, length us, event | category | flops | bytes accessed | tf_op | source)
XLA Modules:
  0.0 80.8 jit_solution(1181070212056935252)
XLA Ops:
  0.6 1.0 %x_edges.1 = (f32[5,64,128]{2,1,0:T(8,128)S(1)}, f32[5,64,128]{2,1,0:T(8,128)S(1)}) custom-call(f32[64,64,128]{2,1,0:T(8,128)} %p.5, f32[64,64,128]{2,1,0:T(8,128)} %q.5, f32[64,64,128]{2,1,0:T(8,128)} %c.6, f32[64,64,128]{2,1,0:T(8,128)} %a.6), custom_call_target="tpu_custom_call" | custom-call | tf_op jit(solution)/shard_map/x_edges/pallas_call | solution.py:79
  1.6 2.9 %collective-permute-start.1 = (f32[5,64,128]{2,1,0:T(8,128)S(1)}, f32[5,64,128]{2,1,0:T(8,128)S(1)}, u32[]{:S(2)}, u32[]{:S(2)}) collective-permute-start(f32[5,64,128]{2,1,0:T(8,128)S(1)} %get-tuple-element.49), channel_id=1, source_target_pairs={{0,112},{16,0},{32,16},{48,32},{64,48},{80,64},{96,80},{112,96},{1... | collective-permute-start | bytes 491528 | tf_op jit(solution)/shard_map/ppermute | solution.py:818
  4.6 1.7 %y_edges.1 = (f32[328,128]{1,0:T(8,128)S(1)}, f32[328,128]{1,0:T(8,128)S(1)}) custom-call(f32[64,64,128]{2,1,0:T(8,128)} %p.5, f32[64,64,128]{2,1,0:T(8,128)} %q.5, f32[64,64,128]{2,1,0:T(8,128)} %c.6, f32[64,64,128]{2,1,0:T(8,128)} %a.6), custom_call_target="tpu_custom_call" | custom-call | bytes 5000000 | tf_op jit(solution)/shard_map/y_edges/pallas_call | solution.py:117
  6.3 0.1 reshape.15
  6.4 0.1 reshape.14
  6.5 0.1 pad_add_fusion.meta
  6.5 1.0 %collective-permute-done.xlo.pxlo.exlo = f32[5,64,128]{2,1,0:T(8,128)S(1)} collective-permute-done((f32[5,64,128]{2,1,0:T(8,128)S(1)}, f32[5,64,128]{2,1,0:T(8,128)S(1)}, u32[]{:S(2)}, u32[]{:S(2)}) %collective-permute-start) | collective-permute-done | bytes 163872 | tf_op jit(solution)/shard_map/ppermute | solution.py:817
  7.6 0.6 corners.2
  8.2 2.1 %collective-permute-start.2 = (f32[328,128]{1,0:T(8,128)S(1)}, f32[328,128]{1,0:T(8,128)S(1)}, u32[]{:S(2)}, u32[]{:S(2)}) collective-permute-start(f32[328,128]{1,0:T(8,128)S(1)} %get-tuple-element.52), channel_id=1, source_target_pairs={{0,1},{1,2},{2,3},{3,4},{4,5},{5,6},{6,7},{7,8},{8,9},{9,10},{10,1... | collective-permute-start | bytes 503816 | tf_op jit(solution)/shard_map/ppermute | solution.py:820
  10.3 4.7 %collective-permute-start.3 = (f32[328,128]{1,0:T(8,128)S(1)}, f32[328,128]{1,0:T(8,128)S(1)}, u32[]{:S(2)}, u32[]{:S(2)}) collective-permute-start(f32[328,128]{1,0:T(8,128)S(1)} %get-tuple-element.53), channel_id=1, source_target_pairs={{0,15},{1,0},{2,1},{3,2},{4,3},{5,4},{6,5},{7,6},{8,7},{9,8},{10,9... | collective-permute-start | bytes 503816 | tf_op jit(solution)/shard_map/ppermute | solution.py:821
  14.9 4.1 %first_inner.1 = (f32[64,64,128]{2,1,0:T(8,128)S(1)}, f32[64,64,128]{2,1,0:T(8,128)S(1)}, f32[64,64,128]{2,1,0:T(8,128)S(1)}, f32[64,64,128]{2,1,0:T(8,128)S(1)}) custom-call(f32[64,64,128]{2,1,0:T(8,128)} %p.5, f32[64,64,128]{2,1,0:T(8,128)} %q.5, f32[64,64,128]{2,1,0:T(8,128)} %c.6, f32[64,64,128]{2,1,0:T(8,128)} %a.6), custom_call_target="tpu_custom_call" | custom-call | flops 12000000 | bytes 10000000 | tf_op jit(solution)/shard_map/first_inner/pallas_call | solution.py:235
  19.0 0.6 collective-permute-done.2.pylo.eylo
  19.7 1.3 %coarse.2 = (f32[64,64,128]{2,1,0:T(8,128)S(1)}, f32[2,2,16,128]{3,2,1,0:T(8,128)S(1)}, f32[2,2,16,128]{3,2,1,0:T(8,128)S(1)}, f32[2,2,16,128]{3,2,1,0:T(8,128)S(1)}, f32[2,2,16,128]{3,2,1,0:T(8,128)S(1)}) custom-call(s32[24]{0:T(128)S(1)} %pad_add_fusion.meta, f32[64,64,128]{2,1,0:T(8,128)S(1)} %get-tuple-element.45.p.q, ...), custom_call_target="tpu_custom_call" | custom-call | tf_op jit(solution)/shard_map/coarse/pallas_call | solution.py:407
  21.0 0.1 collective-permute-start.4
  21.1 2.4 %collective-permute-start.5 = (f32[2,2,16,128]{3,2,1,0:T(8,128)S(1)}, f32[2,2,16,128]{3,2,1,0:T(8,128)S(1)}, u32[]{:S(2)}, u32[]{:S(2)}) collective-permute-start(f32[2,2,16,128]{3,2,1,0:T(8,128)S(1)} %get-tuple-element.60), channel_id=1, source_target_pairs={{0,64},{1,65},{2,66},{3,67},{4,68},{5,69},{6,70},{7,71},{8,72},{9,... | collective-permute-start | bytes 98312 | tf_op jit(solution)/shard_map/ppermute | solution.py:828
  23.5 2.6 %collective-permute-start.6 = (f32[2,2,16,128]{3,2,1,0:T(8,128)S(1)}, f32[2,2,16,128]{3,2,1,0:T(8,128)S(1)}, u32[]{:S(2)}, u32[]{:S(2)}) collective-permute-start(f32[2,2,16,128]{3,2,1,0:T(8,128)S(1)} %get-tuple-element.61), channel_id=1, source_target_pairs={{0,65},{1,64},{2,67},{3,66},{4,69},{5,68},{6,71},{7,70},{8,73},{9,... | collective-permute-start | bytes 98312 | tf_op jit(solution)/shard_map/ppermute | solution.py:828
  26.1 1.7 %factors.1 = (f32[2,48,2304]{2,1,0:T(8,128)S(1)}, f32[2,48,2304]{2,1,0:T(8,128)S(1)}, f32[2,48,2304]{2,1,0:T(8,128)S(1)}) custom-call(f32[2,48,2304]{2,1,0:T(8,128)} %c.7, f32[2,48,2304]{2,1,0:T(8,128)} %a.7), custom_call_target="tpu_custom_call" | custom-call | flops 3000000 | bytes 4000000 | tf_op jit(solution)/shard_map/factors/pallas_call | solution.py:447
  27.9 1.6 %ahead.2.raw = f32[2,48,2304]{2,1,0:T(8,128)S(1)} custom-call(f32[2,48,2304]{2,1,0:T(8,128)S(1)} %copy-done.2, f32[2,48,2304]{2,1,0:T(8,128)S(1)} %copy-done.3, f32[2,48,2304]{2,1,0:T(8,128)S(1)} %get-tuple-element.55.one, f32[2,48,2304]{2,1,0:T(8,128)S(1)} %get-tuple-element.56.two, f32[2,48,2304]{2,1,0:T(8,128)S(1)} %get-tuple-element.57.three, ...), custom_call_target="tpu_custom_call" | custom-call | flops 5000000 | bytes 5000000 | tf_op jit(solution)/shard_map/ahead/pallas_call | solution.py:514
  29.5 0.4 collective-permute-done.6.r3
  29.8 3.7 %fine.2 = (f32[2,48,2304]{2,1,0:T(8,128)S(1)}, f32[2,48,2304]{2,1,0:T(8,128)S(1)}, f32[2,16,256]{2,1,0:T(8,128)S(1)}) custom-call(s32[24]{0:T(128)S(1)} %pad_add_fusion.meta, f32[2,48,2304]{2,1,0:T(8,128)S(1)} %copy-done.2, f32[2,48,2304]{2,1,0:T(8,128)S(1)} %ahead.2.raw, f32[2,48,2304]{2,1,0:T(8,128)S(1)} %get-tuple-element.55.one, ...), custom_call_target="tpu_custom_call" | custom-call | tf_op jit(solution)/shard_map/fine/pallas_call | solution.py:638
  33.6 2.6 %collective-permute-start.9 = (f32[2,16,256]{2,1,0:T(8,128)S(1)}, f32[2,16,256]{2,1,0:T(8,128)S(1)}, u32[]{:S(2)}, u32[]{:S(2)}) collective-permute-start(f32[2,16,256]{2,1,0:T(8,128)S(1)} %get-tuple-element.62.r0), channel_id=1, source_target_pairs={{0,65},{1,64},{2,67},{3,66},{4,69},{5,68},{6,71},{7,70},{8,73},{9,... | collective-permute-start | bytes 98312 | tf_op jit(solution)/shard_map/ppermute | solution.py:828
  36.2 2.3 %collective-permute-start.8 = (f32[2,16,256]{2,1,0:T(8,128)S(1)}, f32[2,16,256]{2,1,0:T(8,128)S(1)}, u32[]{:S(2)}, u32[]{:S(2)}) collective-permute-start(f32[2,16,256]{2,1,0:T(8,128)S(1)} %get-tuple-element.62.r0), channel_id=1, source_target_pairs={{0,64},{1,65},{2,66},{3,67},{4,68},{5,69},{6,70},{7,71},{8,72},{9,... | collective-permute-start | bytes 98312 | tf_op jit(solution)/shard_map/ppermute | solution.py:828
  38.5 0.1 collective-permute-start.7
  38.6 1.6 %collective-permute-done.9.r3 = f32[2,16,256]{2,1,0:T(8,128)S(1)} collective-permute-done((f32[2,16,256]{2,1,0:T(8,128)S(1)}, f32[2,16,256]{2,1,0:T(8,128)S(1)}, u32[]{:S(2)}, u32[]{:S(2)}) %collective-permute-start.9) | collective-permute-done | bytes 32800 | tf_op jit(solution)/shard_map/ppermute | solution.py:828
  40.2 1.4 %collective-permute-done.8.r2 = f32[2,16,256]{2,1,0:T(8,128)S(1)} collective-permute-done((f32[2,16,256]{2,1,0:T(8,128)S(1)}, f32[2,16,256]{2,1,0:T(8,128)S(1)}, u32[]{:S(2)}, u32[]{:S(2)}) %collective-permute-start.8) | collective-permute-done | bytes 32800 | tf_op jit(solution)/shard_map/ppermute | solution.py:828
  41.6 0.8 collective-permute-done.7.r1
  42.4 1.1 %insert.1 = (f32[64,64,128]{2,1,0:T(8,128)S(1)}, f32[2,64,128]{2,1,0:T(8,128)S(1)}, f32[2,64,128]{2,1,0:T(8,128)S(1)}, f32[136,128]{1,0:T(8,128)S(1)}, f32[136,128]{1,0:T(8,128)S(1)}) custom-call(s32[24]{0:T(128)S(1)} %pad_add_fusion.meta, f32[64,64,128]{2,1,0:T(8,128)S(1)} %get-tuple-element.54.new, f32[2,16,256]{2,1,0:T(8,128)S(1)} %get-tuple-element.62.r0, ...), custom_call_target="tpu_custom_call" | custom-call | tf_op jit(solution)/shard_map/insert/pallas_call | solution.py:714
  43.5 2.9 %collective-permute-start.11 = (f32[2,64,128]{2,1,0:T(8,128)S(1)}, f32[2,64,128]{2,1,0:T(8,128)S(1)}, u32[]{:S(2)}, u32[]{:S(2)}) collective-permute-start(f32[2,64,128]{2,1,0:T(8,128)S(1)} %get-tuple-element.67), channel_id=1, source_target_pairs={{0,112},{16,0},{32,16},{48,32},{64,48},{80,64},{96,80},{112,96},{1... | collective-permute-start | bytes 196616 | tf_op jit(solution)/shard_map/ppermute | solution.py:818
  46.4 1.9 %collective-permute-done.10.xlo.pxlo = f32[2,64,128]{2,1,0:T(8,128)S(1)} collective-permute-done((f32[2,64,128]{2,1,0:T(8,128)S(1)}, f32[2,64,128]{2,1,0:T(8,128)S(1)}, u32[]{:S(2)}, u32[]{:S(2)}) %collective-permute-start.10) | collective-permute-done | bytes 65568 | tf_op jit(solution)/shard_map/ppermute | solution.py:817
  48.4 0.6 corners.3
  49.0 0.2 collective-permute-start.12
  49.1 5.3 %collective-permute-start.13 = (f32[136,128]{1,0:T(8,128)S(1)}, f32[136,128]{1,0:T(8,128)S(1)}, u32[]{:S(2)}, u32[]{:S(2)}) collective-permute-start(f32[136,128]{1,0:T(8,128)S(1)} %get-tuple-element.71), channel_id=1, source_target_pairs={{0,15},{1,0},{2,1},{3,2},{4,3},{5,4},{6,5},{7,6},{8,7},{9,8},{10,9... | collective-permute-start | bytes 208904 | tf_op jit(solution)/shard_map/ppermute | solution.py:821
  54.4 1.9 %second_inner.1 = (f32[64,64,128]{2,1,0:T(8,128)S(1)}, f32[64,64,128]{2,1,0:T(8,128)}) custom-call(f32[64,64,128]{2,1,0:T(8,128)S(1)} %get-tuple-element.63.p, f32[64,64,128]{2,1,0:T(8,128)S(1)} %get-tuple-element.45.p.q, f32[64,64,128]{2,1,0:T(8,128)S(1)} %get-tuple-element.64.two, f32[64,64,128]{2,1,0:T(8,128)S(1)} %get-tuple-element.47.weight.side), custom_call_target="tpu_custom_call" | custom-call | flops 12000000 | bytes 8000000 | tf_op jit(solution)/shard_map/second_inner/pallas_call | solution.py:274
  56.3 0.4 collective-permute-done.12.pylo
  56.7 1.3 %coarse.3 = (f32[64,64,128]{2,1,0:T(8,128)S(1)}, f32[2,2,16,128]{3,2,1,0:T(8,128)S(1)}, f32[2,2,16,128]{3,2,1,0:T(8,128)S(1)}, f32[2,2,16,128]{3,2,1,0:T(8,128)S(1)}, f32[2,2,16,128]{3,2,1,0:T(8,128)S(1)}) custom-call(s32[24]{0:T(128)S(1)} %pad_add_fusion.meta, f32[64,64,128]{2,1,0:T(8,128)S(1)} %get-tuple-element.63.p, ...), custom_call_target="tpu_custom_call" | custom-call | tf_op jit(solution)/shard_map/coarse/pallas_call | solution.py:407
  58.0 0.1 collective-permute-start.14
  58.1 2.2 %collective-permute-start.15 = (f32[2,2,16,128]{3,2,1,0:T(8,128)S(1)}, f32[2,2,16,128]{3,2,1,0:T(8,128)S(1)}, u32[]{:S(2)}, u32[]{:S(2)}) collective-permute-start(f32[2,2,16,128]{3,2,1,0:T(8,128)S(1)} %get-tuple-element.77), channel_id=1, source_target_pairs={{0,64},{1,65},{2,66},{3,67},{4,68},{5,69},{6,70},{7,71},{8,72},{9,... | collective-permute-start | bytes 98312 | tf_op jit(solution)/shard_map/ppermute | solution.py:828
  60.3 2.8 %collective-permute-start.16 = (f32[2,2,16,128]{3,2,1,0:T(8,128)S(1)}, f32[2,2,16,128]{3,2,1,0:T(8,128)S(1)}, u32[]{:S(2)}, u32[]{:S(2)}) collective-permute-start(f32[2,2,16,128]{3,2,1,0:T(8,128)S(1)} %get-tuple-element.78), channel_id=1, source_target_pairs={{0,65},{1,64},{2,67},{3,66},{4,69},{5,68},{6,71},{7,70},{8,73},{9,... | collective-permute-start | bytes 98312 | tf_op jit(solution)/shard_map/ppermute | solution.py:828
  63.1 1.6 %ahead.3.raw = f32[2,48,2304]{2,1,0:T(8,128)S(1)} custom-call(f32[2,48,2304]{2,1,0:T(8,128)S(1)} %get-tuple-element.73.f, f32[2,48,2304]{2,1,0:T(8,128)S(1)} %get-tuple-element.74.g, f32[2,48,2304]{2,1,0:T(8,128)S(1)} %get-tuple-element.55.one, f32[2,48,2304]{2,1,0:T(8,128)S(1)} %get-tuple-element.56.two, f32[2,48,2304]{2,1,0:T(8,128)S(1)} %get-tuple-element.57.three, ...), custom_call_target="tpu_custom_call" | custom-call | flops 5000000 | bytes 5000000 | tf_op jit(solution)/shard_map/ahead/pallas_call | solution.py:514
  64.7 1.9 %collective-permute-done.16.r3 = f32[2,2,16,128]{3,2,1,0:T(8,128)S(1)} collective-permute-done((f32[2,2,16,128]{3,2,1,0:T(8,128)S(1)}, f32[2,2,16,128]{3,2,1,0:T(8,128)S(1)}, u32[]{:S(2)}, u32[]{:S(2)}) %collective-permute-start.16) | collective-permute-done | bytes 32800 | tf_op jit(solution)/shard_map/ppermute | solution.py:828
  66.6 3.7 %fine.3 = (f32[2,48,2304]{2,1,0:T(8,128)S(1)}, f32[2,48,2304]{2,1,0:T(8,128)S(1)}, f32[2,16,256]{2,1,0:T(8,128)S(1)}) custom-call(s32[24]{0:T(128)S(1)} %pad_add_fusion.meta, f32[2,48,2304]{2,1,0:T(8,128)S(1)} %get-tuple-element.73.f, f32[2,48,2304]{2,1,0:T(8,128)S(1)} %ahead.3.raw, f32[2,48,2304]{2,1,0:T(8,128)S(1)} %get-tuple-element.55.one, ...), custom_call_target="tpu_custom_call" | custom-call | tf_op jit(solution)/shard_map/fine/pallas_call | solution.py:638
  70.3 2.8 %collective-permute-start.19 = (f32[2,16,256]{2,1,0:T(8,128)S(1)}, f32[2,16,256]{2,1,0:T(8,128)S(1)}, u32[]{:S(2)}, u32[]{:S(2)}) collective-permute-start(f32[2,16,256]{2,1,0:T(8,128)S(1)} %get-tuple-element.82.r0), channel_id=1, source_target_pairs={{0,65},{1,64},{2,67},{3,66},{4,69},{5,68},{6,71},{7,70},{8,73},{9,... | collective-permute-start | bytes 98312 | tf_op jit(solution)/shard_map/ppermute | solution.py:828
  73.1 2.1 %collective-permute-start.18 = (f32[2,16,256]{2,1,0:T(8,128)S(1)}, f32[2,16,256]{2,1,0:T(8,128)S(1)}, u32[]{:S(2)}, u32[]{:S(2)}) collective-permute-start(f32[2,16,256]{2,1,0:T(8,128)S(1)} %get-tuple-element.82.r0), channel_id=1, source_target_pairs={{0,64},{1,65},{2,66},{3,67},{4,68},{5,69},{6,70},{7,71},{8,72},{9,... | collective-permute-start | bytes 98312 | tf_op jit(solution)/shard_map/ppermute | solution.py:828
  75.2 0.1 collective-permute-start.17
  75.3 1.9 %emit.1 = (f32[64,64,128]{2,1,0:T(8,128)}, f32[2,48,2304]{2,1,0:T(8,128)}, f32[2,48,2304]{2,1,0:T(8,128)}) custom-call(f32[64,64,128]{2,1,0:T(8,128)S(1)} %get-tuple-element.72.new, f32[2,48,2304]{2,1,0:T(8,128)S(1)} %get-tuple-element.79.f, f32[2,48,2304]{2,1,0:T(8,128)S(1)} %get-tuple-element.80.g), custom_call_target="tpu_custom_call" | custom-call | bytes 9000000 | tf_op jit(solution)/shard_map/emit/pallas_call | solution.py:736
  77.2 1.3 %collective-permute-done.18.r2 = f32[2,16,256]{2,1,0:T(8,128)S(1)} collective-permute-done((f32[2,16,256]{2,1,0:T(8,128)S(1)}, f32[2,16,256]{2,1,0:T(8,128)S(1)}, u32[]{:S(2)}, u32[]{:S(2)}) %collective-permute-start.18) | collective-permute-done | bytes 32800 | tf_op jit(solution)/shard_map/ppermute | solution.py:828
  78.5 0.6 collective-permute-done.17.r1
  79.1 1.5 %finish.1 = f32[64,64,128]{2,1,0:T(8,128)} custom-call(s32[24]{0:T(128)S(1)} %pad_add_fusion.meta, f32[64,64,128]{2,1,0:T(8,128)S(1)} %get-tuple-element.72.new, f32[64,64,128]{2,1,0:T(8,128)} %get-tuple-element.81.written, f32[2,16,256]{2,1,0:T(8,128)S(1)} %get-tuple-element.82.r0, ...), custom_call_target="tpu_custom_call", output_to_operand_aliasing={{}: (2, {})} | custom-call | tf_op jit(solution)/shard_map/finish/pallas_call | solution.py:796
  (27 shorter events, 0.1 us)
Async XLA Ops:
  1.6 6.0 %collective-permute-start = (f32[5,64,128]{2,1,0:T(8,128)S(1)}, f32[5,64,128]{2,1,0:T(8,128)S(1)}, u32[]{:S(2)}, u32[]{:S(2)}) collective-permute-start(f32[5,64,128]{2,1,0:T(8,128)S(1)} %get-tuple-element.48), channel_id=1, source_target_pairs={{0,16},{16,32},{32,48},{48,64},{64,80},{80,96},{96,112},{112,0},{1... | collective-permute-start | bytes 491528 | tf_op jit(solution)/shard_map/ppermute | solution.py:817
  1.6 5.9 %collective-permute-start.1 = (f32[5,64,128]{2,1,0:T(8,128)S(1)}, f32[5,64,128]{2,1,0:T(8,128)S(1)}, u32[]{:S(2)}, u32[]{:S(2)}) collective-permute-start(f32[5,64,128]{2,1,0:T(8,128)S(1)} %get-tuple-element.49), channel_id=1, source_target_pairs={{0,112},{16,0},{32,16},{48,32},{64,48},{80,64},{96,80},{112,96},{1... | collective-permute-start | bytes 491528 | tf_op jit(solution)/shard_map/ppermute | solution.py:818
  4.6 1.7 %copy-start.7 = (s32[2,3]{1,0:T(2,128)S(1)}, s32[2,3]{1,0:T(2,128)}, u32[]{:S(2)}) copy-start(s32[2,3]{1,0:T(2,128)} %param.22) | copy-start | bytes 76
  4.6 1.8 %copy-start.6 = (s32[1,4,4]{2,1,0:T(4,128)S(1)}, s32[1,4,4]{2,1,0:T(4,128)}, u32[]{:S(2)}) copy-start(s32[1,4,4]{2,1,0:T(4,128)} %param.23) | copy-start | bytes 196
  8.2 11.5 %collective-permute-start.2 = (f32[328,128]{1,0:T(8,128)S(1)}, f32[328,128]{1,0:T(8,128)S(1)}, u32[]{:S(2)}, u32[]{:S(2)}) collective-permute-start(f32[328,128]{1,0:T(8,128)S(1)} %get-tuple-element.52), channel_id=1, source_target_pairs={{0,1},{1,2},{2,3},{3,4},{4,5},{5,6},{6,7},{7,8},{8,9},{9,10},{10,1... | collective-permute-start | bytes 503816 | tf_op jit(solution)/shard_map/ppermute | solution.py:820
  10.3 9.4 %collective-permute-start.3 = (f32[328,128]{1,0:T(8,128)S(1)}, f32[328,128]{1,0:T(8,128)S(1)}, u32[]{:S(2)}, u32[]{:S(2)}) collective-permute-start(f32[328,128]{1,0:T(8,128)S(1)} %get-tuple-element.53), channel_id=1, source_target_pairs={{0,15},{1,0},{2,1},{3,2},{4,3},{5,4},{6,5},{7,6},{8,7},{9,8},{10,9... | collective-permute-start | bytes 503816 | tf_op jit(solution)/shard_map/ppermute | solution.py:821
  19.7 8.2 %copy-start.5 = (f32[2,8,384]{2,1,0:T(8,128)S(1)}, f32[2,8,384]{2,1,0:T(8,128)}, u32[]{:S(2)}) copy-start(f32[2,8,384]{2,1,0:T(8,128)} %constant.17.clone.masks) | copy-start | bytes 73732
  21.0 6.8 %copy-start.2 = (f32[2,48,2304]{2,1,0:T(8,128)S(1)}, f32[2,48,2304]{2,1,0:T(8,128)}, u32[]{:S(2)}) copy-start(f32[2,48,2304]{2,1,0:T(8,128)} %f.3) | copy-start | bytes 2654212
  21.0 6.8 %copy-start.3 = (f32[2,48,2304]{2,1,0:T(8,128)S(1)}, f32[2,48,2304]{2,1,0:T(8,128)}, u32[]{:S(2)}) copy-start(f32[2,48,2304]{2,1,0:T(8,128)} %g.1) | copy-start | bytes 2654212
  21.0 8.4 %collective-permute-start.4 = (f32[2,2,16,128]{3,2,1,0:T(8,128)S(1)}, f32[2,2,16,128]{3,2,1,0:T(8,128)S(1)}, u32[]{:S(2)}, u32[]{:S(2)}) collective-permute-start(f32[2,2,16,128]{3,2,1,0:T(8,128)S(1)} %get-tuple-element.59), channel_id=1, source_target_pairs={{0,1},{1,0},{2,3},{3,2},{4,5},{5,4},{6,7},{7,6},{8,9},{9,8},{10,11... | collective-permute-start | bytes 98312 | tf_op jit(solution)/shard_map/ppermute | solution.py:828
  21.1 8.3 %collective-permute-start.5 = (f32[2,2,16,128]{3,2,1,0:T(8,128)S(1)}, f32[2,2,16,128]{3,2,1,0:T(8,128)S(1)}, u32[]{:S(2)}, u32[]{:S(2)}) collective-permute-start(f32[2,2,16,128]{3,2,1,0:T(8,128)S(1)} %get-tuple-element.60), channel_id=1, source_target_pairs={{0,64},{1,65},{2,66},{3,67},{4,68},{5,69},{6,70},{7,71},{8,72},{9,... | collective-permute-start | bytes 98312 | tf_op jit(solution)/shard_map/ppermute | solution.py:828
  23.5 6.3 %collective-permute-start.6 = (f32[2,2,16,128]{3,2,1,0:T(8,128)S(1)}, f32[2,2,16,128]{3,2,1,0:T(8,128)S(1)}, u32[]{:S(2)}, u32[]{:S(2)}) collective-permute-start(f32[2,2,16,128]{3,2,1,0:T(8,128)S(1)} %get-tuple-element.61), channel_id=1, source_target_pairs={{0,65},{1,64},{2,67},{3,66},{4,69},{5,68},{6,71},{7,70},{8,73},{9,... | collective-permute-start | bytes 98312 | tf_op jit(solution)/shard_map/ppermute | solution.py:828
  27.9 2.0 %copy-start = (bf16[2304,256]{1,0:T(8,128)(2,1)S(1)}, bf16[2304,256]{1,0:T(8,128)(2,1)}, u32[]{:S(2)}) copy-start(bf16[2304,256]{1,0:T(8,128)(2,1)} %constant.20.clone.pool) | copy-start | bytes 3538948
  27.9 2.0 %copy-start.1 = (bf16[256,2304]{1,0:T(8,128)(2,1)S(1)}, bf16[256,2304]{1,0:T(8,128)(2,1)}, u32[]{:S(2)}) copy-start(bf16[256,2304]{1,0:T(8,128)(2,1)} %constant.18.clone.spread) | copy-start | bytes 3538948
  27.9 2.0 %copy-start.4 = (f32[16,2304]{1,0:T(8,128)S(1)}, f32[16,2304]{1,0:T(8,128)}, u32[]{:S(2)}) copy-start(f32[16,2304]{1,0:T(8,128)} %constant.19.clone.pick) | copy-start | bytes 442372
  33.6 6.6 %collective-permute-start.9 = (f32[2,16,256]{2,1,0:T(8,128)S(1)}, f32[2,16,256]{2,1,0:T(8,128)S(1)}, u32[]{:S(2)}, u32[]{:S(2)}) collective-permute-start(f32[2,16,256]{2,1,0:T(8,128)S(1)} %get-tuple-element.62.r0), channel_id=1, source_target_pairs={{0,65},{1,64},{2,67},{3,66},{4,69},{5,68},{6,71},{7,70},{8,73},{9,... | collective-permute-start | bytes 98312 | tf_op jit(solution)/shard_map/ppermute | solution.py:828
  36.2 5.4 %collective-permute-start.8 = (f32[2,16,256]{2,1,0:T(8,128)S(1)}, f32[2,16,256]{2,1,0:T(8,128)S(1)}, u32[]{:S(2)}, u32[]{:S(2)}) collective-permute-start(f32[2,16,256]{2,1,0:T(8,128)S(1)} %get-tuple-element.62.r0), channel_id=1, source_target_pairs={{0,64},{1,65},{2,66},{3,67},{4,68},{5,69},{6,70},{7,71},{8,72},{9,... | collective-permute-start | bytes 98312 | tf_op jit(solution)/shard_map/ppermute | solution.py:828
  38.5 3.9 %collective-permute-start.7 = (f32[2,16,256]{2,1,0:T(8,128)S(1)}, f32[2,16,256]{2,1,0:T(8,128)S(1)}, u32[]{:S(2)}, u32[]{:S(2)}) collective-permute-start(f32[2,16,256]{2,1,0:T(8,128)S(1)} %get-tuple-element.62.r0), channel_id=1, source_target_pairs={{0,1},{1,0},{2,3},{3,2},{4,5},{5,4},{6,7},{7,6},{8,9},{9,8},{10,11... | collective-permute-start | bytes 98312 | tf_op jit(solution)/shard_map/ppermute | solution.py:828
  43.5 4.9 %collective-permute-start.10 = (f32[2,64,128]{2,1,0:T(8,128)S(1)}, f32[2,64,128]{2,1,0:T(8,128)S(1)}, u32[]{:S(2)}, u32[]{:S(2)}) collective-permute-start(f32[2,64,128]{2,1,0:T(8,128)S(1)} %get-tuple-element.66), channel_id=1, source_target_pairs={{0,16},{16,32},{32,48},{48,64},{64,80},{80,96},{96,112},{112,0},{1... | collective-permute-start | bytes 196616 | tf_op jit(solution)/shard_map/ppermute | solution.py:817
  43.5 4.9 %collective-permute-start.11 = (f32[2,64,128]{2,1,0:T(8,128)S(1)}, f32[2,64,128]{2,1,0:T(8,128)S(1)}, u32[]{:S(2)}, u32[]{:S(2)}) collective-permute-start(f32[2,64,128]{2,1,0:T(8,128)S(1)} %get-tuple-element.67), channel_id=1, source_target_pairs={{0,112},{16,0},{32,16},{48,32},{64,48},{80,64},{96,80},{112,96},{1... | collective-permute-start | bytes 196616 | tf_op jit(solution)/shard_map/ppermute | solution.py:818
  49.0 7.7 %collective-permute-start.12 = (f32[136,128]{1,0:T(8,128)S(1)}, f32[136,128]{1,0:T(8,128)S(1)}, u32[]{:S(2)}, u32[]{:S(2)}) collective-permute-start(f32[136,128]{1,0:T(8,128)S(1)} %get-tuple-element.70), channel_id=1, source_target_pairs={{0,1},{1,2},{2,3},{3,4},{4,5},{5,6},{6,7},{7,8},{8,9},{9,10},{10,1... | collective-permute-start | bytes 208904 | tf_op jit(solution)/shard_map/ppermute | solution.py:820
  49.1 7.5 %collective-permute-start.13 = (f32[136,128]{1,0:T(8,128)S(1)}, f32[136,128]{1,0:T(8,128)S(1)}, u32[]{:S(2)}, u32[]{:S(2)}) collective-permute-start(f32[136,128]{1,0:T(8,128)S(1)} %get-tuple-element.71), channel_id=1, source_target_pairs={{0,15},{1,0},{2,1},{3,2},{4,3},{5,4},{6,5},{7,6},{8,7},{9,8},{10,9... | collective-permute-start | bytes 208904 | tf_op jit(solution)/shard_map/ppermute | solution.py:821
  58.0 6.7 %collective-permute-start.14 = (f32[2,2,16,128]{3,2,1,0:T(8,128)S(1)}, f32[2,2,16,128]{3,2,1,0:T(8,128)S(1)}, u32[]{:S(2)}, u32[]{:S(2)}) collective-permute-start(f32[2,2,16,128]{3,2,1,0:T(8,128)S(1)} %get-tuple-element.76), channel_id=1, source_target_pairs={{0,1},{1,0},{2,3},{3,2},{4,5},{5,4},{6,7},{7,6},{8,9},{9,8},{10,11... | collective-permute-start | bytes 98312 | tf_op jit(solution)/shard_map/ppermute | solution.py:828
  58.1 6.6 %collective-permute-start.15 = (f32[2,2,16,128]{3,2,1,0:T(8,128)S(1)}, f32[2,2,16,128]{3,2,1,0:T(8,128)S(1)}, u32[]{:S(2)}, u32[]{:S(2)}) collective-permute-start(f32[2,2,16,128]{3,2,1,0:T(8,128)S(1)} %get-tuple-element.77), channel_id=1, source_target_pairs={{0,64},{1,65},{2,66},{3,67},{4,68},{5,69},{6,70},{7,71},{8,72},{9,... | collective-permute-start | bytes 98312 | tf_op jit(solution)/shard_map/ppermute | solution.py:828
  60.3 6.3 %collective-permute-start.16 = (f32[2,2,16,128]{3,2,1,0:T(8,128)S(1)}, f32[2,2,16,128]{3,2,1,0:T(8,128)S(1)}, u32[]{:S(2)}, u32[]{:S(2)}) collective-permute-start(f32[2,2,16,128]{3,2,1,0:T(8,128)S(1)} %get-tuple-element.78), channel_id=1, source_target_pairs={{0,65},{1,64},{2,67},{3,66},{4,69},{5,68},{6,71},{7,70},{8,73},{9,... | collective-permute-start | bytes 98312 | tf_op jit(solution)/shard_map/ppermute | solution.py:828
  70.3 6.9 %collective-permute-start.19 = (f32[2,16,256]{2,1,0:T(8,128)S(1)}, f32[2,16,256]{2,1,0:T(8,128)S(1)}, u32[]{:S(2)}, u32[]{:S(2)}) collective-permute-start(f32[2,16,256]{2,1,0:T(8,128)S(1)} %get-tuple-element.82.r0), channel_id=1, source_target_pairs={{0,65},{1,64},{2,67},{3,66},{4,69},{5,68},{6,71},{7,70},{8,73},{9,... | collective-permute-start | bytes 98312 | tf_op jit(solution)/shard_map/ppermute | solution.py:828
  73.1 5.4 %collective-permute-start.18 = (f32[2,16,256]{2,1,0:T(8,128)S(1)}, f32[2,16,256]{2,1,0:T(8,128)S(1)}, u32[]{:S(2)}, u32[]{:S(2)}) collective-permute-start(f32[2,16,256]{2,1,0:T(8,128)S(1)} %get-tuple-element.82.r0), channel_id=1, source_target_pairs={{0,64},{1,65},{2,66},{3,67},{4,68},{5,69},{6,70},{7,71},{8,72},{9,... | collective-permute-start | bytes 98312 | tf_op jit(solution)/shard_map/ppermute | solution.py:828
  75.2 3.9 %collective-permute-start.17 = (f32[2,16,256]{2,1,0:T(8,128)S(1)}, f32[2,16,256]{2,1,0:T(8,128)S(1)}, u32[]{:S(2)}, u32[]{:S(2)}) collective-permute-start(f32[2,16,256]{2,1,0:T(8,128)S(1)} %get-tuple-element.82.r0), channel_id=1, source_target_pairs={{0,1},{1,0},{2,3},{3,2},{4,5},{5,4},{6,7},{7,6},{8,9},{9,8},{10,11... | collective-permute-start | bytes 98312 | tf_op jit(solution)/shard_map/ppermute | solution.py:828
